TPU v7x, 512 devices: a whole 4x8x8 slice. The times are simulated.
512 devices in a mesh: dp: 8 (over y), row: 8 (over x, z_lo), col: 8 (over z_hi, core).
Axes of the slice: x: 4, y: 8, z: 8 (z_hi: 4, z_lo: 2; z = z_hi * 2 + z_lo), core: 2. Of those that a mesh axis runs over, the one named last changes fastest.
Arguments:
- timesteps: int32 [8], P('dp'), may hold values from 0 to 999
- features_win: bfloat16 [8, 64, 128, 320], P('dp', 'row', 'col'), may hold values from -25 to 25
- features_lose: bfloat16 [8, 64, 128, 320], P('dp', 'row', 'col'), may hold values from -25 to 25
- noise_win: bfloat16 [8, 64, 128, 320], P('dp', 'row', 'col'), may hold values from -6 to 6
- noise_lose: bfloat16 [8, 64, 128, 320], P('dp', 'row', 'col'), may hold values from -6 to 6
- conv_weight: bfloat16 [9, 320, 320], replicated, may hold values from -0.109375 to 0.109375
- ref_weight: bfloat16 [9, 320, 320], replicated, may hold values from -0.109375 to 0.109375
- norm_gain: float32 [320], replicated, may hold values from 0.5 to 1.5
- norm_shift: float32 [320], replicated, may hold values from -3 to 3
- ref_gain: float32 [320], replicated, may hold values from 0.5 to 1.5
- ref_shift: float32 [320], replicated, may hold values from -3 to 3
- time_weight: float32 [320, 320], replicated, may hold values from -0.3125 to 0.3125
Outputs:
- pair_loss: float32 [8], P('dp')
- grad_weight: float32 [320, 2880], P('dp', ('row', 'col'))
- grad_gain: float32 [320], replicated
- grad_shift: float32 [320], replicated
All inputs are finite; a program needn't handle non-finite values.
Results may differ from a plain program's by a relative error of at most 0.00086.
Values may be sent and summed in bfloat16 or wider, within the bound.
No kernel may reach another device: no remote copies, remote signals or barrier semaphores. Data moves between devices by JAX's collectives and lax.ppermute only.
A program may use at most 64 MiB of HBM per device.

v0:
```python
import math

import jax
import jax.numpy as jnp
from jax import lax
from jax.sharding import PartitionSpec as P

GROUPS = 32


beta_scale = 40.0


def padded_2(block, sides, width):
    for axis, dim in sides:
        count = lax.axis_size(axis)
        forward = [(i, i + 1) for i in range(count - 1)]
        backward = [(target, source) for source, target in forward]
        low = lax.ppermute(
            lax.slice_in_dim(block, block.shape[dim] - width, None, axis=dim), axis, forward
        )
        high = lax.ppermute(lax.slice_in_dim(block, 0, width, axis=dim), axis, backward)
        block = jnp.concatenate([low, block, high], axis=dim)
    return block


def time_embed(timesteps, time_weight):
    half_dim = time_weight.shape[0] // 2
    frequency = jnp.exp(-math.log(10000.0) * jnp.arange(half_dim, dtype=jnp.float32) / half_dim)
    angles = timesteps.astype(jnp.float32)[:, None] * frequency[None, :]
    sinusoid = jnp.concatenate([jnp.cos(angles), jnp.sin(angles)], axis=1)
    return jnp.dot(jax.nn.silu(sinusoid), time_weight, precision=lax.Precision.HIGHEST)


def group_totals(feature):
    channels = feature.shape[-1]
    values = feature.astype(jnp.float32).reshape(-1, GROUPS, channels // GROUPS)
    return (jnp.sum(values, axis=(0, 2)), jnp.sum(values * values, axis=(0, 2)))


def normalize(feature, first, second, entries):
    channels = feature.shape[-1]
    values = feature.astype(jnp.float32).reshape(-1, GROUPS, channels // GROUPS)
    group_mean = first / entries
    group_var = second / entries - group_mean * group_mean
    normed = (values - group_mean[None, :, None]) * lax.rsqrt(group_var + 1e-05)[None, :, None]
    return normed.reshape(feature.shape)


def forward_columns(padded, height, width_cells):
    pieces = [
        padded[row_off : row_off + height, col_off : col_off + width_cells, :]
        for row_off in range(3)
        for col_off in range(3)
    ]
    joined = jnp.concatenate(pieces, axis=-1)
    return joined.reshape(height * width_cells, joined.shape[-1])


def backward_columns(padded, height, width_cells):
    pieces = [
        padded[2 - row_off : 2 - row_off + height, 2 - col_off : 2 - col_off + width_cells, :]
        for row_off in range(3)
        for col_off in range(3)
    ]
    joined = jnp.concatenate(pieces, axis=-1)
    return joined.reshape(height * width_cells, joined.shape[-1])


def silu_slope(pre):
    gate_sig = jax.nn.sigmoid(pre)
    return gate_sig * (1.0 + pre * (1.0 - gate_sig))


def pad_acts(field):
    return padded_2(field, (("row", 0), ("col", 1)), 1)


def pad_cotangent(field):
    return padded_2(field, (("row", 0), ("col", 1)), 1)


def local(
    timesteps,
    features_win,
    features_lose,
    noise_win,
    noise_lose,
    conv_weight,
    ref_weight,
    norm_gain,
    norm_shift,
    ref_gain,
    ref_shift,
    time_weight,
):
    feature_w = features_win[0]
    feature_l = features_lose[0]
    tile_h, tile_w, channels = feature_w.shape
    pixels = tile_h * tile_w
    spread = lax.axis_size("row") * lax.axis_size("col")
    time_bias = time_embed(timesteps, time_weight)[0]
    first_w, second_w = group_totals(feature_w)
    first_l, second_l = group_totals(feature_l)
    first_w, second_w, first_l, second_l = lax.psum(
        (first_w, second_w, first_l, second_l), ("row", "col")
    )
    entries = pixels * spread * (channels // GROUPS)
    normed_w = normalize(feature_w, first_w, second_w, entries)
    normed_l = normalize(feature_l, first_l, second_l, entries)
    streams = ((feature_w, noise_win[0], normed_w), (feature_l, noise_lose[0], normed_l))
    models = ((conv_weight, norm_gain, norm_shift), (ref_weight, ref_gain, ref_shift))
    pre_acts = []
    activated = []
    for feature, target, normed in streams:
        for kernel, gain, shift in models:
            pre = normed * gain + shift + time_bias
            pre_acts.append(pre)
            activated.append(jax.nn.silu(pre).astype(jnp.bfloat16))
    padded = [pad_acts(field) for field in activated]
    column_sets = []
    residuals = []
    partial_err = []
    for index in range(4):
        feature, target, normed = streams[index // 2]
        kernel = models[index % 2][0]
        columns = forward_columns(padded[index], tile_h, tile_w)
        conv_out = jnp.dot(
            columns, kernel.reshape(9 * channels, channels), preferred_element_type=jnp.float32
        )
        resid = (
            feature.astype(jnp.float32).reshape(pixels, channels)
            + conv_out
            - target.astype(jnp.float32).reshape(pixels, channels)
        )
        column_sets.append(columns)
        residuals.append(resid)
        partial_err.append(jnp.sum(resid * resid))
    errors = lax.psum(
        (partial_err[0], partial_err[1], partial_err[2], partial_err[3]), ("row", "col")
    )
    total_cells = pixels * spread * channels
    scaled_err = [item / total_cells for item in errors]
    margin = scaled_err[0] - scaled_err[1] - (scaled_err[2] - scaled_err[3])
    pair_loss = jnp.reshape(jax.nn.softplus(beta_scale * margin), (1,))
    pair_count = lax.axis_size("dp")
    scale_value = beta_scale * jax.nn.sigmoid(beta_scale * margin) * 2.0 / (pair_count * channels)
    cotangents = [
        residuals[0].astype(jnp.bfloat16).reshape(tile_h, tile_w, channels),
        residuals[2].astype(jnp.bfloat16).reshape(tile_h, tile_w, channels),
    ]
    padded_cot = [pad_cotangent(field) for field in cotangents]
    flipped = jnp.transpose(conv_weight, (0, 2, 1)).reshape(9 * channels, channels)
    kernel_terms = []
    gain_terms = []
    shift_terms = []
    for stream_index, act_index in ((0, 0), (1, 2)):
        cot_flat = cotangents[stream_index].reshape(pixels, channels)
        kernel_terms.append(
            lax.dot_general(
                cot_flat,
                column_sets[act_index],
                (((0,), (0,)), ((), ())),
                preferred_element_type=jnp.float32,
            )
        )
        back = backward_columns(padded_cot[stream_index], tile_h, tile_w)
        grad_act = jnp.dot(back, flipped, preferred_element_type=jnp.float32)
        grad_pre = grad_act * silu_slope(pre_acts[act_index].reshape(pixels, channels))
        normed_flat = streams[stream_index][2].reshape(pixels, channels)
        gain_terms.append(jnp.sum(grad_pre * normed_flat, axis=0))
        shift_terms.append(jnp.sum(grad_pre, axis=0))
    kernel_delta = kernel_terms[0] - kernel_terms[1]
    grad_gain, grad_shift = lax.psum(
        (
            scale_value * (gain_terms[0] - gain_terms[1]),
            scale_value * (shift_terms[0] - shift_terms[1]),
        ),
        ("dp", "row", "col"),
    )
    by_tile = lax.psum_scatter(
        scale_value * kernel_delta, ("row", "col"), scatter_dimension=1, tiled=True
    )
    grad_weight = lax.psum_scatter(by_tile, "dp", scatter_dimension=0, tiled=True)
    return (pair_loss, grad_weight, grad_gain, grad_shift)


def solution(mesh):
    return jax.shard_map(
        local,
        mesh=mesh,
        in_specs=(
            P("dp"),
            P("dp", "row", "col", None),
            P("dp", "row", "col", None),
            P("dp", "row", "col", None),
            P("dp", "row", "col", None),
            P(),
            P(),
            P(),
            P(),
            P(),
            P(),
            P(),
        ),
        out_specs=(P("dp"), P("dp", ("row", "col")), P(), P()),
        check_vma=False,
    )
```

profile of v0, /device:TPU:2, one launch (start us, length us, event | category | flops | bytes accessed | tf_op | source)
XLA Modules:
  0.0 717.8 jit_solution(7388607360300289253)
XLA Ops:
  4.4 113.9 %all-reduce.5 = (f32[32]{0:T(128)S(1)}, f32[32]{0:T(128)S(1)}, f32[32]{0:T(128)S(1)}, f32[32]{0:T(128)S(1)}) all-reduce(f32[32]{0:T(128)S(1)} %reduce_sum.141, f32[32]{0:T(128)S(1)} %reduce_sum.138, f32[32]{0:T(128)S(1)} %reduce_sum.149, f32[32]{0:T(128)S(1)} %reduce_sum.146), channel_id=1, replica_groups=mesh['dp'=8,'row'=8,'col'=8] {'row','col'}, use_global_device_ids=true, to_apply=%region_5.6 | all-reduce | flops 128 | bytes 1024 | tf_op jit(solution)/shard_map/psum | solution.py:105
  119.1 1.4 convolution_reduce_fusion
  120.5 1.3 multiply_convert_fusion.2
  121.8 17.1 %collective-permute-start.4 = (bf16[1,16,320]{2,1,0:T(8,128)(2,1)S(1)}, bf16[1,16,320]{2,1,0:T(8,128)(2,1)S(1)}, u32[]{:S(2)}, u32[]{:S(2)}) collective-permute-start(bf16[1,16,320]{2,1,0:T(8,128)(2,1)S(1)} %get-tuple-element.116), channel_id=1, source_target_pairs={{0,8},{8,16},{16,24},{24,32},{32,40},{40,48},{48,56},{1,9},{9,17},... | collective-permute-start | bytes 30728 | tf_op jit(solution)/shard_map/ppermute | solution.py:19
  138.9 1.9 collective-permute-start.5
  140.9 3.9 collective-permute-start
  144.8 2.8 collective-permute-start.12
  147.7 6.0 collective-permute-start.13
  155.6 1.3 dynamic-slice.6
  160.0 4.2 copy.88
  166.8 1.9 collective-permute-start.8
  168.7 4.8 collective-permute-start.9
  174.3 3.0 collective-permute-start.1
  177.3 1.3 collective-permute-start.15
  180.0 3.6 collective-permute-start.14
  183.6 1.3 collective-permute-start.11
  185.6 1.3 collective-permute-start.7
  186.9 3.7 collective-permute-start.6
  191.3 1.3 collective-permute-start.3
  192.6 5.2 collective-permute-start.2
  199.4 5.1 collective-permute-start.10
  206.1 1.4 concatenate.187
  207.5 3.3 fusion.28
  211.5 2.8 collective-permute-start.16
  214.3 3.9 collective-permute-start.17
  222.9 2.1 concatenate.193
  225.0 2.8 fusion.9
  227.8 2.1 concatenate.199
  229.8 3.4 fusion.29
  233.2 2.1 concatenate.205
  235.3 2.7 fusion.8
  238.0 105.4 %all-reduce.4 = (f32[]{:T(128)}, f32[]{:T(128)}, f32[]{:T(128)}, f32[]{:T(128)}) all-reduce(f32[]{:T(128)} %get-tuple-element.71, f32[]{:T(128)} %fusion.9, f32[]{:T(128)} %get-tuple-element.73, f32[]{:T(128)} %fusion.8), channel_id=1, replica_groups=mesh['dp'=8,'row'=8,'col'=8] {'row','col'}, use_global_device_ids=true, to_apply=%region_7.8 | all-reduce | flops 4 | bytes 32 | tf_op jit(solution)/shard_map/psum | solution.py:139
  346.1 3.9 fusion.34
  350.0 5.1 fusion.1
  355.1 151.0 %fusion = f32[320,48]{0,1:T(8,128)S(1)} fusion(f32[320,2880]{0,1:T(8,128)} %fusion.1), kind=kCustom, calls=%all-reduce-scatter | all-reduce-scatter fusion | flops 983041 | bytes 3749888
  507.1 10.8 %collective-permute-start.26 = (f32[320,48]{0,1:T(8,128)S(1)}, f32[320,48]{0,1:T(8,128)}, u32[]{:S(2)}, u32[]{:S(2)}) collective-permute-start(f32[320,48]{0,1:T(8,128)S(1)} %fusion), channel_id=1, source_target_pairs={{0,3},{1,4},{2,5},{3,6},{4,7},{5,8},{6,9},{7,10},{8,11},{9,12},{10... | collective-permute-start | bytes 184328
  517.9 7.3 %collective-permute-start.25 = (f32[320,48]{0,1:T(8,128)S(1)}, f32[320,48]{0,1:T(8,128)}, u32[]{:S(2)}, u32[]{:S(2)}) collective-permute-start(f32[320,48]{0,1:T(8,128)S(1)} %fusion), channel_id=1, source_target_pairs={{0,2},{1,3},{2,4},{3,5},{4,6},{5,7},{6,8},{7,9},{8,10},{9,11},{10,... | collective-permute-start | bytes 184328
  525.2 6.0 collective-permute-start.24
  531.3 4.7 collective-permute-start.20
  537.0 2.0 collective-permute-start.21
  540.1 3.4 collective-permute-start.19
  543.6 1.5 collective-permute-start.18
  547.6 9.4 %collective-permute-start.23 = (bf16[10,1,320]{2,1,0:T(2,128)(2,1)S(1)}, bf16[10,1,320]{2,1,0:T(2,128)(2,1)}, u32[]{:S(2)}, u32[]{:S(2)}) collective-permute-start(bf16[10,1,320]{2,1,0:T(2,128)(2,1)S(1)} %get-tuple-element.76), channel_id=1, source_target_pairs={{0,1},{1,2},{2,3},{3,4},{4,5},{5,6},{6,7},{8,9},{9,10},{10,11},{11... | collective-permute-start | bytes 19208 | tf_op jit(solution)/shard_map/ppermute | solution.py:19
  557.0 1.3 collective-permute-start.22
  562.9 9.3 %collective-permute-start.27 = (f32[320,45]{0,1:T(8,128)}, f32[320,45]{0,1:T(8,128)}, u32[]{:S(2)}, u32[]{:S(2)}) collective-permute-start(f32[320,45]{0,1:T(8,128)} %slice.400), channel_id=1, source_target_pairs={{0,4},{1,5},{2,6},{3,7},{4,8},{5,9},{6,10},{7,11},{8,12},{9,13},{1... | collective-permute-start | bytes 172808
  587.0 95.6 %all-reduce.3 = (f32[320]{0:T(512)}, f32[320]{0:T(512)}) all-reduce(f32[320]{0:T(512)S(1)} %subtract_multiply_fusion.3, f32[320]{0:T(512)S(1)} %subtract_multiply_fusion.2), channel_id=1, replica_groups=mesh['dp'=8,'row'=8,'col'=8] {'dp','row','col'}, use_global_device_ids=true, to_apply=%region_24.25 | all-reduce | flops 640 | bytes 5120 | tf_op jit(solution)/shard_map/psum | solution.py:174
  682.7 3.7 concatenate.234
  686.5 29.5 %all-reduce.1 = f32[320,45]{0,1:T(8,128)S(1)} all-reduce(f32[320,45]{0,1:T(8,128)S(1)} %constant_dynamic-slice_fusion), channel_id=3, replica_groups=mesh['dp'=8,'row'=8,'col'=8] {'dp'}, use_global_device_ids=true, to_apply=%region_21.22.clone | all-reduce | flops 14400 | bytes 115200
  (193 shorter events, 47.5 us)
Async XLA Ops:
  0.6 224.3 %copy-start = (bf16[9,320,320]{2,1,0:T(8,128)(2,1)S(1)}, bf16[9,320,320]{2,1,0:T(8,128)(2,1)}, u32[]{:S(2)}) copy-start(bf16[9,320,320]{2,1,0:T(8,128)(2,1)} %param.18) | copy-start | bytes 5529604
  0.6 157.0 %copy-start.6 = (bf16[1,8,16,320]{3,2,1,0:T(8,128)(2,1)S(1)}, bf16[1,8,16,320]{3,2,1,0:T(8,128)(2,1)}, u32[]{:S(2)}) copy-start(bf16[1,8,16,320]{3,2,1,0:T(8,128)(2,1)} %param.13) | copy-start | bytes 245764
  0.7 156.2 %copy-start.5 = (bf16[1,8,16,320]{3,2,1,0:T(8,128)(2,1)S(1)}, bf16[1,8,16,320]{3,2,1,0:T(8,128)(2,1)}, u32[]{:S(2)}) copy-start(bf16[1,8,16,320]{3,2,1,0:T(8,128)(2,1)} %param.14) | copy-start | bytes 245764
  118.5 26.3 %copy-start.16 = (f32[320]{0:T(512)}, f32[320]{0:T(512)S(1)}, u32[]{:S(2)}) copy-start(f32[320]{0:T(512)S(1)} %sub.89) | copy-start | bytes 3844
  118.7 29.0 %copy-start.20 = (f32[320]{0:T(512)}, f32[320]{0:T(512)S(1)}, u32[]{:S(2)}) copy-start(f32[320]{0:T(512)S(1)} %mul.212) | copy-start | bytes 3844
  118.9 25.9 %copy-start.18 = (f32[320]{0:T(512)}, f32[320]{0:T(512)S(1)}, u32[]{:S(2)}) copy-start(f32[320]{0:T(512)S(1)} %mul.194) | copy-start | bytes 3844
  119.1 28.6 %copy-start.22 = (f32[320]{0:T(512)}, f32[320]{0:T(512)S(1)}, u32[]{:S(2)}) copy-start(f32[320]{0:T(512)S(1)} %sub.81) | copy-start | bytes 3844
  120.5 24.3 %copy-start.14 = (f32[320]{0:T(512)}, f32[320]{0:T(512)S(1)}, u32[]{:S(2)}) copy-start(f32[320]{0:T(512)S(1)} %convolution_reduce_fusion) | copy-start | bytes 3844
  121.8 58.1 %collective-permute-start.4 = (bf16[1,16,320]{2,1,0:T(8,128)(2,1)S(1)}, bf16[1,16,320]{2,1,0:T(8,128)(2,1)S(1)}, u32[]{:S(2)}, u32[]{:S(2)}) collective-permute-start(bf16[1,16,320]{2,1,0:T(8,128)(2,1)S(1)} %get-tuple-element.116), channel_id=1, source_target_pairs={{0,8},{8,16},{16,24},{24,32},{32,40},{40,48},{48,56},{1,9},{9,17},... | collective-permute-start | bytes 30728 | tf_op jit(solution)/shard_map/ppermute | solution.py:19
  138.9 44.7 %collective-permute-start.5 = (bf16[1,16,320]{2,1,0:T(8,128)(2,1)S(1)}, bf16[1,16,320]{2,1,0:T(8,128)(2,1)S(1)}, u32[]{:S(2)}, u32[]{:S(2)}) collective-permute-start(bf16[1,16,320]{2,1,0:T(8,128)(2,1)S(1)} %get-tuple-element.117), channel_id=1, source_target_pairs={{8,0},{16,8},{24,16},{32,24},{40,32},{48,40},{56,48},{9,1},{17,9},... | collective-permute-start | bytes 30728 | tf_op jit(solution)/shard_map/ppermute | solution.py:22
  140.9 44.7 %collective-permute-start = (bf16[1,16,320]{2,1,0:T(8,128)(2,1)S(1)}, bf16[1,16,320]{2,1,0:T(8,128)(2,1)S(1)}, u32[]{:S(2)}, u32[]{:S(2)}) collective-permute-start(bf16[1,16,320]{2,1,0:T(8,128)(2,1)S(1)} %get-tuple-element.120), channel_id=1, source_target_pairs={{0,8},{8,16},{16,24},{24,32},{32,40},{40,48},{48,56},{1,9},{9,17},... | collective-permute-start | bytes 30728 | tf_op jit(solution)/shard_map/ppermute | solution.py:19
  144.8 21.9 %collective-permute-start.12 = (bf16[1,16,320]{2,1,0:T(8,128)(2,1)S(1)}, bf16[1,16,320]{2,1,0:T(8,128)(2,1)S(1)}, u32[]{:S(2)}, u32[]{:S(2)}) collective-permute-start(bf16[1,16,320]{2,1,0:T(8,128)(2,1)S(1)} %get-tuple-element.108), channel_id=1, source_target_pairs={{0,8},{8,16},{16,24},{24,32},{32,40},{40,48},{48,56},{1,9},{9,17},... | collective-permute-start | bytes 30728 | tf_op jit(solution)/shard_map/ppermute | solution.py:19
  147.7 21.0 %collective-permute-start.13 = (bf16[1,16,320]{2,1,0:T(8,128)(2,1)S(1)}, bf16[1,16,320]{2,1,0:T(8,128)(2,1)S(1)}, u32[]{:S(2)}, u32[]{:S(2)}) collective-permute-start(bf16[1,16,320]{2,1,0:T(8,128)(2,1)S(1)} %get-tuple-element.109), channel_id=1, source_target_pairs={{8,0},{16,8},{24,16},{32,24},{40,32},{48,40},{56,48},{9,1},{17,9},... | collective-permute-start | bytes 30728 | tf_op jit(solution)/shard_map/ppermute | solution.py:22
  166.8 7.5 %collective-permute-start.8 = (bf16[1,16,320]{2,1,0:T(8,128)(2,1)S(1)}, bf16[1,16,320]{2,1,0:T(8,128)(2,1)S(1)}, u32[]{:S(2)}, u32[]{:S(2)}) collective-permute-start(bf16[1,16,320]{2,1,0:T(8,128)(2,1)S(1)} %get-tuple-element.112), channel_id=1, source_target_pairs={{0,8},{8,16},{16,24},{24,32},{32,40},{40,48},{48,56},{1,9},{9,17},... | collective-permute-start | bytes 30728 | tf_op jit(solution)/shard_map/ppermute | solution.py:19
  168.7 8.6 %collective-permute-start.9 = (bf16[1,16,320]{2,1,0:T(8,128)(2,1)S(1)}, bf16[1,16,320]{2,1,0:T(8,128)(2,1)S(1)}, u32[]{:S(2)}, u32[]{:S(2)}) collective-permute-start(bf16[1,16,320]{2,1,0:T(8,128)(2,1)S(1)} %get-tuple-element.113), channel_id=1, source_target_pairs={{8,0},{16,8},{24,16},{32,24},{40,32},{48,40},{56,48},{9,1},{17,9},... | collective-permute-start | bytes 30728 | tf_op jit(solution)/shard_map/ppermute | solution.py:22
  174.3 12.6 %collective-permute-start.1 = (bf16[1,16,320]{2,1,0:T(8,128)(2,1)S(1)}, bf16[1,16,320]{2,1,0:T(8,128)(2,1)S(1)}, u32[]{:S(2)}, u32[]{:S(2)}) collective-permute-start(bf16[1,16,320]{2,1,0:T(8,128)(2,1)S(1)} %get-tuple-element.121), channel_id=1, source_target_pairs={{8,0},{16,8},{24,16},{32,24},{40,32},{48,40},{56,48},{9,1},{17,9},... | collective-permute-start | bytes 30728 | tf_op jit(solution)/shard_map/ppermute | solution.py:22
  177.3 43.3 %collective-permute-start.15 = (bf16[10,1,320]{2,1,0:T(2,128)(2,1)S(1)}, bf16[10,1,320]{2,1,0:T(2,128)(2,1)}, u32[]{:S(2)}, u32[]{:S(2)}) collective-permute-start(bf16[10,1,320]{2,1,0:T(2,128)(2,1)S(1)} %get-tuple-element.84), channel_id=1, source_target_pairs={{1,0},{2,1},{3,2},{4,3},{5,4},{6,5},{7,6},{9,8},{10,9},{11,10},{12... | collective-permute-start | bytes 19208 | tf_op jit(solution)/shard_map/ppermute | solution.py:22
  180.0 40.6 %collective-permute-start.14 = (bf16[10,1,320]{2,1,0:T(2,128)(2,1)S(1)}, bf16[10,1,320]{2,1,0:T(2,128)(2,1)}, u32[]{:S(2)}, u32[]{:S(2)}) collective-permute-start(bf16[10,1,320]{2,1,0:T(2,128)(2,1)S(1)} %get-tuple-element.85), channel_id=1, source_target_pairs={{0,1},{1,2},{2,3},{3,4},{4,5},{5,6},{6,7},{8,9},{9,10},{10,11},{11... | collective-permute-start | bytes 19208 | tf_op jit(solution)/shard_map/ppermute | solution.py:19
  183.6 30.7 %collective-permute-start.11 = (bf16[10,1,320]{2,1,0:T(2,128)(2,1)}, bf16[10,1,320]{2,1,0:T(2,128)(2,1)}, u32[]{:S(2)}, u32[]{:S(2)}) collective-permute-start(bf16[10,1,320]{2,1,0:T(2,128)(2,1)} %get-tuple-element.88), channel_id=1, source_target_pairs={{1,0},{2,1},{3,2},{4,3},{5,4},{6,5},{7,6},{9,8},{10,9},{11,10},{12... | collective-permute-start | bytes 19208 | tf_op jit(solution)/shard_map/ppermute | solution.py:22
  185.6 5.7 collective-permute-start.7
  186.9 5.7 collective-permute-start.6
  191.3 8.0 %collective-permute-start.3 = (bf16[10,1,320]{2,1,0:T(2,128)(2,1)S(1)}, bf16[10,1,320]{2,1,0:T(2,128)(2,1)S(1)}, u32[]{:S(2)}, u32[]{:S(2)}) collective-permute-start(bf16[10,1,320]{2,1,0:T(2,128)(2,1)S(1)} %get-tuple-element.96), channel_id=1, source_target_pairs={{1,0},{2,1},{3,2},{4,3},{5,4},{6,5},{7,6},{9,8},{10,9},{11,10},{12... | collective-permute-start | bytes 19208 | tf_op jit(solution)/shard_map/ppermute | solution.py:22
  192.6 11.9 %collective-permute-start.2 = (bf16[10,1,320]{2,1,0:T(2,128)(2,1)S(1)}, bf16[10,1,320]{2,1,0:T(2,128)(2,1)S(1)}, u32[]{:S(2)}, u32[]{:S(2)}) collective-permute-start(bf16[10,1,320]{2,1,0:T(2,128)(2,1)S(1)} %get-tuple-element.97), channel_id=1, source_target_pairs={{0,1},{1,2},{2,3},{3,4},{4,5},{5,6},{6,7},{8,9},{9,10},{10,11},{11... | collective-permute-start | bytes 19208 | tf_op jit(solution)/shard_map/ppermute | solution.py:19
  199.4 18.9 %collective-permute-start.10 = (bf16[10,1,320]{2,1,0:T(2,128)(2,1)}, bf16[10,1,320]{2,1,0:T(2,128)(2,1)}, u32[]{:S(2)}, u32[]{:S(2)}) collective-permute-start(bf16[10,1,320]{2,1,0:T(2,128)(2,1)} %get-tuple-element.89), channel_id=1, source_target_pairs={{0,1},{1,2},{2,3},{3,4},{4,5},{5,6},{6,7},{8,9},{9,10},{10,11},{11... | collective-permute-start | bytes 19208 | tf_op jit(solution)/shard_map/ppermute | solution.py:19
  211.5 319.9 %collective-permute-start.16 = (bf16[1,16,320]{1,2,0:T(8,128)(2,1)}, bf16[1,16,320]{1,2,0:T(8,128)(2,1)}, u32[]{:S(2)}, u32[]{:S(2)}) collective-permute-start(bf16[1,16,320]{1,2,0:T(8,128)(2,1)} %get-tuple-element.124), channel_id=1, source_target_pairs={{0,8},{8,16},{16,24},{24,32},{32,40},{40,48},{48,56},{1,9},{9,17},... | collective-permute-start | bytes 30728 | tf_op jit(solution)/shard_map/ppermute | solution.py:19
  214.3 322.7 %collective-permute-start.17 = (bf16[1,16,320]{1,2,0:T(8,128)(2,1)}, bf16[1,16,320]{1,2,0:T(8,128)(2,1)}, u32[]{:S(2)}, u32[]{:S(2)}) collective-permute-start(bf16[1,16,320]{1,2,0:T(8,128)(2,1)} %get-tuple-element.125), channel_id=1, source_target_pairs={{8,0},{16,8},{24,16},{32,24},{40,32},{48,40},{56,48},{9,1},{17,9},... | collective-permute-start | bytes 30728 | tf_op jit(solution)/shard_map/ppermute | solution.py:22
  507.1 175.6 %collective-permute-start.26 = (f32[320,48]{0,1:T(8,128)S(1)}, f32[320,48]{0,1:T(8,128)}, u32[]{:S(2)}, u32[]{:S(2)}) collective-permute-start(f32[320,48]{0,1:T(8,128)S(1)} %fusion), channel_id=1, source_target_pairs={{0,3},{1,4},{2,5},{3,6},{4,7},{5,8},{6,9},{7,10},{8,11},{9,12},{10... | collective-permute-start | bytes 184328
  517.9 164.8 %collective-permute-start.25 = (f32[320,48]{0,1:T(8,128)S(1)}, f32[320,48]{0,1:T(8,128)}, u32[]{:S(2)}, u32[]{:S(2)}) collective-permute-start(f32[320,48]{0,1:T(8,128)S(1)} %fusion), channel_id=1, source_target_pairs={{0,2},{1,3},{2,4},{3,5},{4,6},{5,7},{6,8},{7,9},{8,10},{9,11},{10,... | collective-permute-start | bytes 184328
  525.2 157.5 %collective-permute-start.24 = (f32[320,48]{0,1:T(8,128)S(1)}, f32[320,48]{0,1:T(8,128)}, u32[]{:S(2)}, u32[]{:S(2)}) collective-permute-start(f32[320,48]{0,1:T(8,128)S(1)} %fusion), channel_id=1, source_target_pairs={{0,1},{1,2},{2,3},{3,4},{4,5},{5,6},{6,7},{7,8},{8,9},{9,10},{10,1... | collective-permute-start | bytes 184328
  531.3 8.8 %collective-permute-start.20 = (bf16[1,16,320]{1,2,0:T(8,128)(2,1)S(1)}, bf16[1,16,320]{1,2,0:T(8,128)(2,1)S(1)}, u32[]{:S(2)}, u32[]{:S(2)}) collective-permute-start(bf16[1,16,320]{1,2,0:T(8,128)(2,1)S(1)} %get-tuple-element.122), channel_id=1, source_target_pairs={{0,8},{8,16},{16,24},{24,32},{32,40},{40,48},{48,56},{1,9},{9,17},... | collective-permute-start | bytes 30728 | tf_op jit(solution)/shard_map/ppermute | solution.py:19
  537.0 6.6 collective-permute-start.21
  540.1 7.5 %collective-permute-start.19 = (bf16[10,1,320]{2,1,0:T(2,128)(2,1)S(1)}, bf16[10,1,320]{2,1,0:T(2,128)(2,1)S(1)}, u32[]{:S(2)}, u32[]{:S(2)}) collective-permute-start(bf16[10,1,320]{2,1,0:T(2,128)(2,1)S(1)} %get-tuple-element.80), channel_id=1, source_target_pairs={{0,1},{1,2},{2,3},{3,4},{4,5},{5,6},{6,7},{8,9},{9,10},{10,11},{11... | collective-permute-start | bytes 19208 | tf_op jit(solution)/shard_map/ppermute | solution.py:19
  543.6 13.4 %collective-permute-start.18 = (bf16[10,1,320]{2,1,0:T(2,128)(2,1)S(1)}, bf16[10,1,320]{2,1,0:T(2,128)(2,1)S(1)}, u32[]{:S(2)}, u32[]{:S(2)}) collective-permute-start(bf16[10,1,320]{2,1,0:T(2,128)(2,1)S(1)} %get-tuple-element.81), channel_id=1, source_target_pairs={{1,0},{2,1},{3,2},{4,3},{5,4},{6,5},{7,6},{9,8},{10,9},{11,10},{12... | collective-permute-start | bytes 19208 | tf_op jit(solution)/shard_map/ppermute | solution.py:22
  547.6 15.3 %collective-permute-start.23 = (bf16[10,1,320]{2,1,0:T(2,128)(2,1)S(1)}, bf16[10,1,320]{2,1,0:T(2,128)(2,1)}, u32[]{:S(2)}, u32[]{:S(2)}) collective-permute-start(bf16[10,1,320]{2,1,0:T(2,128)(2,1)S(1)} %get-tuple-element.76), channel_id=1, source_target_pairs={{0,1},{1,2},{2,3},{3,4},{4,5},{5,6},{6,7},{8,9},{9,10},{10,11},{11... | collective-permute-start | bytes 19208 | tf_op jit(solution)/shard_map/ppermute | solution.py:19
  557.0 15.2 %collective-permute-start.22 = (bf16[10,1,320]{2,1,0:T(2,128)(2,1)S(1)}, bf16[10,1,320]{2,1,0:T(2,128)(2,1)}, u32[]{:S(2)}, u32[]{:S(2)}) collective-permute-start(bf16[10,1,320]{2,1,0:T(2,128)(2,1)S(1)} %get-tuple-element.77), channel_id=1, source_target_pairs={{1,0},{2,1},{3,2},{4,3},{5,4},{6,5},{7,6},{9,8},{10,9},{11,10},{12... | collective-permute-start | bytes 19208 | tf_op jit(solution)/shard_map/ppermute | solution.py:22
  560.7 20.1 %copy-start.9 = (bf16[128,320]{0,1:T(8,128)(2,1)S(1)}, bf16[128,320]{0,1:T(8,128)(2,1)}, u32[]{:S(2)}) copy-start(bf16[128,320]{0,1:T(8,128)(2,1)} %copy.81) | copy-start | bytes 245764
  562.9 119.8 %collective-permute-start.27 = (f32[320,45]{0,1:T(8,128)}, f32[320,45]{0,1:T(8,128)}, u32[]{:S(2)}, u32[]{:S(2)}) collective-permute-start(f32[320,45]{0,1:T(8,128)} %slice.400), channel_id=1, source_target_pairs={{0,4},{1,5},{2,6},{3,7},{4,8},{5,9},{6,10},{7,11},{8,12},{9,13},{1... | collective-permute-start | bytes 172808
  573.0 8.8 %copy-start.8 = (bf16[128,320]{0,1:T(8,128)(2,1)S(1)}, bf16[128,320]{0,1:T(8,128)(2,1)}, u32[]{:S(2)}) copy-start(bf16[128,320]{0,1:T(8,128)(2,1)} %copy.101) | copy-start | bytes 245764
  573.8 10.9 %copy-start.4 = (f32[128,320]{0,1:T(8,128)S(1)}, f32[128,320]{0,1:T(8,128)}, u32[]{:S(2)}) copy-start(f32[128,320]{0,1:T(8,128)} %copy.71) | copy-start | bytes 491524
  573.8 10.9 %copy-start.15 = (f32[320]{0:T(512)S(1)}, f32[320]{0:T(512)}, u32[]{:S(2)}) copy-start(f32[320]{0:T(512)} %copy-done.14) | copy-start | bytes 3844
  573.8 10.9 %copy-start.17 = (f32[320]{0:T(512)S(1)}, f32[320]{0:T(512)}, u32[]{:S(2)}) copy-start(f32[320]{0:T(512)} %copy-done.16) | copy-start | bytes 3844
  573.8 10.9 %copy-start.21 = (f32[320]{0:T(512)S(1)}, f32[320]{0:T(512)}, u32[]{:S(2)}) copy-start(f32[320]{0:T(512)} %copy-done.20) | copy-start | bytes 3844
  573.8 10.9 %copy-start.24 = (f32[320]{0:T(512)S(1)}, f32[320]{0:T(512)}, u32[]{:S(2)}) copy-start(f32[320]{0:T(512)} %param.20) | copy-start | bytes 3844
  573.8 10.9 %copy-start.25 = (f32[320]{0:T(512)S(1)}, f32[320]{0:T(512)}, u32[]{:S(2)}) copy-start(f32[320]{0:T(512)} %param.19) | copy-start | bytes 3844
  574.6 7.1 copy-start.10
  575.4 6.4 copy-start.12
  575.4 6.5 copy-start.11
  577.0 7.8 %copy-start.1 = (bf16[9,320,320]{2,1,0:T(8,128)(2,1)S(1)}, bf16[9,320,320]{2,1,0:T(8,128)(2,1)}, u32[]{:S(2)}) copy-start(bf16[9,320,320]{2,1,0:T(8,128)(2,1)} %copy.88) | copy-start | bytes 5529604
  (6 other events, 25.9 us)
where the time goes:
time: 720 us; the launch traced here: 718 us
  blocking collectives  495 us (69%)
  starting transfers between devices  127 us (18%)
  local copies, waits for them, and re-layouts  51.3 us (7%)
  matrix products  24.8 us (3%)
  other arithmetic  12 us (2%)
  between operations  7.68 us (1%)
    unnamed x2, blocking collectives  180 us
    psum x1, blocking collectives, local(): lax.psum((first_w, second_w, first_l, second_l), ('row', 'col'))  114 us
    psum x1, blocking collectives, local(): lax.psum((partial_err[0], partial_err[1], partial_err[2], partial_err[3])...  105 us
    psum x1, blocking collectives, local(): lax.psum((scale_value * (gain_terms[0] - gain_terms[1]), scale_value * (s...  95.6 us
    ppermute x12, starting transfers between devices, padded_2(): lax.ppermute(lax.slice_in_dim(block, block.shape[dim] - width, None, axis...  63.6 us
    unnamed x4, starting transfers between devices  33.4 us
    ppermute x12, starting transfers between devices, padded_2(): lax.ppermute(lax.slice_in_dim(block, 0, width, axis=dim), axis, backward)  29.6 us
    unnamed x75, local copies, waits for them, and re-layouts  14.5 us
  transfers between devices with their start and end apart: 28, of which 0 were waited for; matrix products, arithmetic and copies ran while one was open for 32% of the time, Pallas kernels for 0%

commit v1 on v0

v1 whole, which is shorter than its diff:
```python
import functools
import math

import jax
import jax.numpy as jnp
from jax import lax
from jax.experimental import pallas as pl
from jax.experimental.pallas import tpu as pltpu
from jax.sharding import Mesh
from jax.sharding import PartitionSpec as P

C = 320
GROUPS = 32
TAPS = 9
TH, TW = 8, 16
PIX = TH * TW
BLK = 45
PIXELS = 64 * 128
BETA = 40.0
F32 = jnp.float32
BF16 = jnp.bfloat16
I16 = jnp.int16
HIGHEST = lax.Precision.HIGHEST
VMEM_LIMIT = 50 * 1024 * 1024


def call(kernel, outs, scratch=(), flops=0, nbytes=0, smem=()):
    def run(*args):
        specs = [
            pl.BlockSpec(memory_space=pltpu.SMEM if i in smem else pltpu.VMEM)
            for i in range(len(args))
        ]
        return pl.pallas_call(
            kernel,
            out_shape=[jax.ShapeDtypeStruct(s, d) for s, d in outs],
            in_specs=specs,
            out_specs=[pl.BlockSpec(memory_space=pltpu.VMEM) for _ in outs],
            scratch_shapes=list(scratch),
            compiler_params=pltpu.CompilerParams(vmem_limit_bytes=VMEM_LIMIT),
            cost_estimate=pl.CostEstimate(flops=flops, bytes_accessed=nbytes, transcendentals=0),
        )(*args)

    return run


def pow2(n):
    size = jnp.abs(n)
    out = jnp.ones(n.shape, F32)
    for bit in range(7):
        step = jnp.where(n < 0, 0.5 ** (2**bit) if bit < 7 else 0.0, 2.0 ** (2**bit))
        out = out * jnp.where((size & (1 << bit)) != 0, step, 1.0)
    return out


def exponent(peak):
    level = jnp.log(jnp.maximum(peak, 1e-30)) * (1.0 / math.log(2.0))
    return jnp.clip(jnp.ceil(level + 0.01), -100.0, 100.0).astype(jnp.int32)


def rounded(values, exps):
    return jnp.clip(jnp.round(values * pow2(15 - exps)), -32767.0, 32767.0)


def split_small(small):
    exps = exponent(jnp.abs(small))
    scaled = small * pow2(15 - exps)
    high = jnp.round(scaled)
    low = jnp.round((scaled - high) * 32768.0)
    return jnp.clip(high, -32767.0, 32767.0), low, exps.astype(F32)


def write_extras(extra, small):
    high, low, exps = split_small(small)
    extra[...] = jnp.zeros_like(extra)
    for k in range(3):
        extra[k, 0:1, :] = high[k : k + 1]
        extra[k, 1:2, :] = low[k : k + 1]
    extra[3, 0:1, :] = exps[0:1]
    extra[3, 1:2, :] = exps[1:2]
    extra[4, 0:1, :] = exps[2:3]


def read_extras(blocks, base):
    tails = [blocks[base + k].astype(jnp.int32)[40:48] for k in range(5)]
    exps = [tails[3][6:7], tails[3][7:8], tails[4][6:7]]
    rows = []
    for k in range(3):
        high = tails[k][6:7].astype(F32)
        low = tails[k][7:8].astype(F32)
        rows.append((high + low * (1.0 / 32768.0)) * pow2(exps[k] - 15))
    return jnp.concatenate(rows + [jnp.zeros((5, C), F32)], axis=0)


def packed_block(block, extra):
    row = lax.broadcasted_iota(jnp.int32, block.shape, 0)
    exps = exponent(jnp.max(jnp.abs(block), axis=0, keepdims=True))
    q = rounded(block, exps)
    q = jnp.where(row == 45, exps.astype(F32), q)
    q = jnp.where(row == 46, extra[0:1], q)
    q = jnp.where(row == 47, extra[1:2], q)
    return q.astype(jnp.int32).astype(I16)


def unpacked_block(block):
    q = block.astype(jnp.int32)
    row = lax.broadcasted_iota(jnp.int32, q.shape, 0)
    return jnp.where(row < BLK, q.astype(F32) * pow2(q[45:46] - 15), 0.0)


def edge_rows(fw, fl, first, last):
    first[0] = fw[0]
    first[1] = fl[0]
    last[0] = fw[TH - 1]
    last[1] = fl[TH - 1]


def stats_and_time(step, fw, fl, time_weight, stats, bias):
    total = jnp.zeros((8, 128), F32)
    rows = lax.broadcasted_iota(jnp.int32, (C, 128), 0)
    lanes = lax.broadcasted_iota(jnp.int32, (C, 128), 1)
    size = C // GROUPS
    for k, ref in enumerate((fw, fl)):
        x = ref[...].astype(F32).reshape(PIX, C)
        sums = jnp.sum(x, axis=0, keepdims=True)
        squares = jnp.sum(x * x, axis=0, keepdims=True)
        for j, part in enumerate((sums, squares)):
            group = lanes - GROUPS * (2 * k + j)
            member = (group >= 0) & (group < GROUPS)
            member = member & (rows >= group * size) & (rows < group * size + size)
            total = total + jnp.dot(
                jnp.broadcast_to(part, (8, C)),
                member.astype(F32),
                precision=HIGHEST,
                preferred_element_type=F32,
            )
    stats[...] = jnp.broadcast_to(total[0:1], stats.shape)
    half = C // 2
    lane = lax.broadcasted_iota(jnp.int32, (8, C), 1)
    place = jnp.where(lane < half, lane, lane - half).astype(F32)
    frequency = jnp.exp(-math.log(10000.0) * place / half)
    angles = step[0].astype(F32) * frequency
    sinusoid = jnp.where(lane < half, jnp.cos(angles), jnp.sin(angles))
    gate = sinusoid * jax.nn.sigmoid(sinusoid)
    bias[...] = jnp.dot(gate, time_weight[...], precision=HIGHEST, preferred_element_type=F32)


def edge_columns(top, bottom, fw, fl, first, last):
    for s, ref in enumerate((fw, fl)):
        x = ref[...].astype(F32)
        above = top[s].astype(F32)
        below = bottom[s].astype(F32)
        for out, col in ((first, 0), (last, TW - 1)):
            side = jnp.concatenate(
                [above[col : col + 1]]
                + [x[r, col : col + 1] for r in range(TH)]
                + [below[col : col + 1], jnp.zeros((6, C), F32)],
                axis=0,
            )
            out[s] = side.astype(BF16)


def step_kernel(
    stats, bias, gain, shift, ref_gain, ref_shift, fw, fl, nw, nl, top, bottom, left, right,
    weight, ref_weight, own, send, small, field, act, cols, grad, parts, back, extra,
):
    x_at, zl_at = lax.axis_index("x"), lax.axis_index("zl")
    zh_at, core = lax.axis_index("zh"), lax.axis_index("core")
    row_at, col_at = 2 * x_at + zl_at, 2 * zh_at + core

    total = jnp.broadcast_to(jnp.sum(stats[...], axis=0, keepdims=True), (8, 128))
    groups = lax.broadcasted_iota(jnp.int32, (128, C), 0)
    chans = lax.broadcasted_iota(jnp.int32, (128, C), 1)
    size = C // GROUPS
    entries = float(PIXELS * size)

    def by_channel(k):
        group = groups - GROUPS * k
        member = (group >= 0) & (group < GROUPS)
        member = member & (chans >= group * size) & (chans < group * size + size)
        spread = jnp.dot(total, member.astype(F32), precision=HIGHEST, preferred_element_type=F32)
        return spread[0:1] / entries

    means, scales = [], []
    for s in range(2):
        mean, square = by_channel(2 * s), by_channel(2 * s + 1)
        means.append(mean)
        scales.append(lax.rsqrt(square - mean * mean + 1e-05))

    for s, ref in enumerate((fw, fl)):
        field[s] = jnp.zeros((TH + 2, 24, C), F32)
        field[s, 1 : TH + 1, 1 : TW + 1, :] = ref[...].astype(F32)
        field[s, 0, 1 : TW + 1, :] = top[s].astype(F32)
        field[s, TH + 1, 1 : TW + 1, :] = bottom[s].astype(F32)
        lhs = left[s].astype(F32)
        rhs = right[s].astype(F32)
        for r in range(TH + 2):
            field[s, r, 0:1, :] = lhs[r : r + 1]
            field[s, r, TW + 1 : TW + 2, :] = rhs[r : r + 1]

    column = lax.broadcasted_iota(jnp.int32, (24, C), 0)
    inside = (column < TW + 2) & ((column > 0) | (col_at > 0))
    inside = inside & ((column < TW + 1) | (col_at < 7))

    def valid(r):
        if r == 0:
            return inside & (row_at > 0)
        if r == TH + 1:
            return inside & (row_at < 7)
        return inside

    def pre_act(s, r, g, b):
        normed = (field[s, r] - means[s]) * scales[s]
        return normed, normed * g + b

    def columns_of(g, b):
        for s in range(2):
            for r in range(TH + 2):
                _, pre = pre_act(s, r, g, b)
                act[r] = jnp.where(valid(r), pre * jax.nn.sigmoid(pre), 0.0)
            for t in range(TAPS):
                a, c = t // 3, t % 3
                piece = act[a : a + TH, c : c + TW, :].reshape(PIX, C).astype(BF16)
                cols[s * PIX : (s + 1) * PIX, C * t : C * (t + 1)] = piece

    base = jnp.concatenate(
        [
            fw[...].astype(F32).reshape(PIX, C) - nw[...].astype(F32).reshape(PIX, C),
            fl[...].astype(F32).reshape(PIX, C) - nl[...].astype(F32).reshape(PIX, C),
        ],
        axis=0,
    )
    streams = lax.broadcasted_iota(jnp.int32, (2 * PIX, C), 0)
    sign = jnp.where(streams < PIX, 1.0, -1.0)

    def residual(kernel):
        conv = jnp.dot(cols[...], kernel[...].reshape(TAPS * C, C), preferred_element_type=F32)
        return base + conv

    time_row = bias[0:1]
    columns_of(ref_gain[...], ref_shift[...] + time_row)
    resid = residual(ref_weight)
    margin = -jnp.sum(resid * resid * sign, axis=0, keepdims=True)
    g, b = gain[...], shift[...] + time_row
    columns_of(g, b)
    resid = residual(weight)
    margin = margin + jnp.sum(resid * resid * sign, axis=0, keepdims=True)
    cot = (resid * sign).astype(BF16)

    grad[0 : TAPS * C, :] = lax.dot_general(
        cols[...], cot, (((0,), (0,)), ((), ())), preferred_element_type=F32
    )

    back[...] = jnp.zeros_like(back)
    for t in range(TAPS):
        a, c = t // 3, t % 3
        term = lax.dot_general(
            cot, weight[t], (((1,), (1,)), ((), ())), preferred_element_type=F32
        )
        for s in range(2):
            back[s, a : a + TH, c : c + TW, :] += term[s * PIX : (s + 1) * PIX].reshape(TH, TW, C)
    gains = jnp.zeros((24, C), F32)
    shifts = jnp.zeros((24, C), F32)
    for s in range(2):
        for r in range(TH + 2):
            normed, pre = pre_act(s, r, g, b)
            gate = jax.nn.sigmoid(pre)
            slope = gate * (1.0 + pre * (1.0 - gate))
            dpre = jnp.where(valid(r), back[s, r] * slope, 0.0)
            gains = gains + dpre * normed
            shifts = shifts + dpre
    totals = jnp.concatenate(
        [
            jnp.sum(gains, axis=0, keepdims=True),
            jnp.sum(shifts, axis=0, keepdims=True),
            jnp.broadcast_to(jnp.sum(margin, axis=1, keepdims=True), (1, C)),
            jnp.zeros((5, C), F32),
        ],
        axis=0,
    )
    small[...] = totals
    write_extras(extra, totals)

    row = lax.broadcasted_iota(jnp.int32, (48, C), 0)

    for k in range(64):
        parts[k] = jnp.where(row < BLK, grad[BLK * k : BLK * k + 48, :], 0.0)

    def split(q, carry):
        own[q] = parts[2 * q + core]
        send[q] = packed_block(parts[2 * q + 1 - core], extra[lax.rem(q, 8)])
        return carry

    lax.fori_loop(0, 32, split, 0)


def core_sum(own, small, other, out, extra):
    write_extras(extra, small[...] + read_extras(other, 0))

    def body(q, carry):
        out[q] = packed_block(own[q] + unpacked_block(other[q]), extra[lax.rem(q, 8)])
        return carry

    lax.fori_loop(0, 32, body, 0)


def chip_sum(blocks, out):
    small = read_extras(blocks, 0)
    for source in range(1, 4):
        small = small + read_extras(blocks, 8 * source)
    high, low, exps = split_small(small)
    lane = lax.broadcasted_iota(jnp.int32, (1, 128), 1)
    tail = jnp.zeros((1, 128), F32)
    vectors = []
    for k in range(2):
        e = exponent(jnp.max(jnp.abs(small[k : k + 1]), axis=1, keepdims=True))
        q = rounded(small[k : k + 1], e)
        q = jnp.concatenate([q, jnp.zeros((1, 64), F32)], axis=1)
        vectors += [q[:, 0:128], q[:, 128:256], q[:, 256:384]]
        tail = jnp.where(lane == k, e.astype(F32), tail)
    for k, part in enumerate((high, low, exps)):
        tail = jnp.where(lane == 2 + k, part[2:3, 0:128], tail)

    def body(z, carry):
        block = unpacked_block(blocks[z])
        for source in range(1, 4):
            block = block + unpacked_block(blocks[8 * source + z])
        e = exponent(jnp.max(jnp.abs(block), axis=0, keepdims=True))
        q = rounded(block, e)
        e = e.astype(F32)
        for y in range(8):
            part = q[:, 40 * y : 40 * y + 40]
            tile = jnp.concatenate(
                [part[0:16], part[16:32], part[32:48], jnp.zeros((16, 8), F32)], axis=1
            )
            ey = e[:, 40 * y : 40 * y + 40]
            ey = jnp.concatenate([ey, ey, ey, jnp.zeros((1, 8), F32)], axis=1)
            full = jnp.concatenate([tile] + vectors + [ey, tail], axis=0)
            out[y, z] = full.astype(jnp.int32).astype(I16)
        return carry

    lax.fori_loop(0, 8, body, 0)


def final_sum(blocks, loss, grad, gain, shift):
    y_at = lax.axis_index("y")
    weights = jnp.zeros((16, 128), F32)
    vectors = jnp.zeros((8, 128), F32)
    mine = jnp.zeros((1, 1), F32)
    row = lax.broadcasted_iota(jnp.int32, (8, 128), 0)
    for pair in range(8):
        part = jnp.zeros((16, 128), F32)
        vector = jnp.zeros((8, 128), F32)
        margin = jnp.zeros((1, 1), F32)
        for z in range(8):
            q = blocks[pair, z].astype(jnp.int32)
            v = q.astype(F32)
            tail = q[16:24]
            part = part + v[0:16] * pow2(tail[6:7] - 15)
            factor = pow2(tail[7:8] - 15)
            vector = vector + v[16:24] * jnp.where(row < 3, factor[:, 0:1], factor[:, 1:2])
            margin = margin + (v[23:24, 2:3] + v[23:24, 3:4] * (1.0 / 32768.0)) * factor[:, 4:5]
        margin = BETA * (margin / float(PIXELS * C))
        scale = BETA * jax.nn.sigmoid(margin) * (2.0 / (8 * C))
        weights = weights + scale * part
        vectors = vectors + scale * vector
        mine = jnp.where(y_at == pair, margin, mine)
    near = jnp.exp(-jnp.abs(mine))
    one = 1.0 + near
    log1p = jnp.where(one == 1.0, near, jnp.log(one) * near / jnp.where(one == 1.0, 1.0, one - 1.0))
    loss[...] = jnp.maximum(mine, 0.0) + log1p
    tall = jnp.concatenate([weights, jnp.roll(weights, -40, 1), jnp.roll(weights, -80, 1)], axis=0)
    tall = jnp.concatenate([tall, jnp.zeros((80, 128), F32)], axis=0)
    grad[...] = tall.T[0:40, 0:BLK]
    gain[...] = jnp.concatenate([vectors[0:1], vectors[1:2], vectors[2:3, 0:64]], axis=1)
    shift[...] = jnp.concatenate([vectors[3:4], vectors[4:5], vectors[5:6, 0:64]], axis=1)


def local(
    timesteps, features_win, features_lose, noise_win, noise_lose, conv_weight, ref_weight,
    norm_gain, norm_shift, ref_gain, ref_shift, time_weight,
):
    fw, fl = features_win[0], features_lose[0]
    strip = (2, TW, C)
    rows, columns = ("x", "zl"), ("zh", "core")
    up = [((i + 1) % 8, i) for i in range(8)]
    down = [(i, (i + 1) % 8) for i in range(8)]

    first, last = call(edge_rows, [(strip, BF16), (strip, BF16)])(fw, fl)
    top = lax.ppermute(last, rows, down)
    bottom = lax.ppermute(first, rows, up)
    stats, bias = call(
        stats_and_time, [((64, 128), F32), ((8, C), F32)], flops=10**7, nbytes=10**6, smem=(0,)
    )(timesteps, fw, fl, time_weight)
    first, last = call(edge_columns, [(strip, BF16), (strip, BF16)])(top, bottom, fw, fl)
    stats, first, last = lax.optimization_barrier((stats, first, last))
    left = lax.ppermute(last, columns, down)
    right = lax.ppermute(first, columns, up)
    stats = lax.all_to_all(stats, ("x", "zl", "zh", "core"), 0, 0, tiled=True)

    block = (32, 48, C)
    vectors = [v.reshape(1, C) for v in (norm_gain, norm_shift, ref_gain, ref_shift)]
    own, send, small = call(
        step_kernel,
        [(block, F32), (block, I16), ((8, C), F32)],
        [
            pltpu.VMEM((2, TH + 2, 24, C), F32),
            pltpu.VMEM((TH + 2, 24, C), F32),
            pltpu.VMEM((2 * PIX, TAPS * C), BF16),
            pltpu.VMEM((TAPS * C + 8, C), F32),
            pltpu.VMEM((64, 48, C), F32),
            pltpu.VMEM((2, TH + 2, 24, C), F32),
            pltpu.VMEM((8, 8, C), F32),
        ],
        flops=2 * 10**9,
        nbytes=10**7,
    )(
        stats, bias, *vectors, fw, fl, noise_win[0], noise_lose[0], top, bottom, left, right,
        conv_weight, ref_weight,
    )
    other = lax.ppermute(send, "core", [(0, 1), (1, 0)])
    (sums,) = call(core_sum, [(block, I16)], [pltpu.VMEM((8, 8, C), F32)])(own, small, other)
    sums = lax.all_to_all(sums, "x", 0, 0, tiled=True)
    (sums,) = call(chip_sum, [((8, 8, 24, 128), I16)])(sums)
    sums = lax.all_to_all(sums.reshape(64, 24, 128), ("y", "zl", "zh"), 0, 0, tiled=True)
    loss, grad, gain, shift = call(
        final_sum, [((1, 1), F32), ((40, BLK), F32), ((1, C), F32), ((1, C), F32)]
    )(sums.reshape(8, 8, 24, 128))
    return loss.reshape(1), grad, gain.reshape(C), shift.reshape(C)


def solution(mesh):
    fine = Mesh(mesh.devices.reshape(8, 4, 2, 4, 2), ("y", "x", "zl", "zh", "core"))
    image = P("y", ("x", "zl"), ("zh", "core"), None)
    return jax.shard_map(
        local,
        mesh=fine,
        in_specs=(P("y"), image, image, image, image) + (P(),) * 7,
        out_specs=(P("y"), P("y", ("x", "zl", "zh", "core")), P(), P()),
        check_vma=False,
    )
```

time: 720 us -> 116 us (0.16)
  the two profiles are of different devices: /device:TPU:2 before, /device:TPU:8 now
where the time goes in v1:
time: 116 us
  blocking collectives  50.2 us (43%)
  starting transfers between devices  31.4 us (27%)
  Pallas kernels  20.7 us (18%)
  local copies, waits for them, and re-layouts  6.93 us (6%)
  waiting for transfers between devices  3.6 us (3%)
  between operations  1.44 us (1%)
  other arithmetic  1.19 us (1%)
    all_to_all x1, blocking collectives, local(): lax.all_to_all(sums.reshape(64, 24, 128), ('y', 'zl', 'zh'), 0, 0, tiled=...  29.1 us
    all_to_all x1, blocking collectives, local(): sums = lax.all_to_all(sums, 'x', 0, 0, tiled=True)  21.2 us
    pallas_call x7, Pallas kernels, run(): pl.pallas_call(kernel, out_shape=[jax.ShapeDtypeStruct(s, d) for s, d in...  20.7 us
    all_to_all x1, starting transfers between devices, local(): stats = lax.all_to_all(stats, ('x', 'zl', 'zh', 'core'), 0, 0, tiled=True)  12.3 us
    unnamed x22, local copies, waits for them, and re-layouts  6.24 us
    ppermute x1, starting transfers between devices, local(): right = lax.ppermute(first, columns, up)  5.71 us
    ppermute x1, starting transfers between devices, local(): top = lax.ppermute(last, rows, down)  4.41 us
    ppermute x1, starting transfers between devices, local(): bottom = lax.ppermute(first, rows, up)  4.12 us
  transfers between devices with their start and end apart: 6, of which 3 were waited for; matrix products, arithmetic and copies ran while one was open for 1% of the time, Pallas kernels for 1%

profile of v1, /device:TPU:8, one launch (start us, length us, event | category | flops | bytes accessed | tf_op | source)
XLA Modules:
  0.0 115.5 jit_solution(16578873157442168645)
XLA Ops:
  0.6 0.0 copy-start.8
  0.6 0.0 copy-start
  0.7 0.9 copy-done
  1.5 0.0 copy-start.2
  1.5 0.9 copy-done.2
  2.4 0.0 copy-start.9
  2.4 0.0 copy-start.10
  2.4 0.0 copy-start.1
  2.4 0.0 copy-start.3
  2.5 4.4 %collective-permute-start = (bf16[2,16,320]{2,1,0:T(8,128)(2,1)S(1)}, bf16[2,16,320]{2,1,0:T(8,128)(2,1)S(1)}, u32[]{:S(2)}, u32[]{:S(2)}) collective-permute-start(bf16[2,16,320]{2,1,0:T(8,128)(2,1)S(1)} %get-tuple-element.21), channel_id=1, source_target_pairs={{0,8},{8,16},{16,24},{24,32},{32,40},{40,48},{48,56},{56,0},{1,9},... | collective-permute-start | bytes 61448 | tf_op jit(solution)/shard_map/ppermute | solution.py:389
  6.9 4.1 %collective-permute-start.1 = (bf16[2,16,320]{2,1,0:T(8,128)(2,1)S(1)}, bf16[2,16,320]{2,1,0:T(8,128)(2,1)S(1)}, u32[]{:S(2)}, u32[]{:S(2)}) collective-permute-start(bf16[2,16,320]{2,1,0:T(8,128)(2,1)S(1)} %get-tuple-element.22), channel_id=1, source_target_pairs={{8,0},{16,8},{24,16},{32,24},{40,32},{48,40},{56,48},{0,56},{9,1},... | collective-permute-start | bytes 61448 | tf_op jit(solution)/shard_map/ppermute | solution.py:390
  11.7 0.0 copy-start.4
  11.7 1.0 copy-done.4
  12.7 1.3 %shard_map.147 = (f32[64,128]{1,0:T(8,128)}, f32[8,320]{1,0:T(8,128)S(1)}) custom-call(s32[1]{0:T(128)S(6)} %copy.17.step, bf16[8,16,320]{2,1,0:T(8,128)(2,1)S(1)} %bitcast.14, bf16[8,16,320]{2,1,0:T(8,128)(2,1)S(1)} %bitcast.18, f32[320,320]{1,0:T(8,128)S(1)} %copy-done.4), custom_call_target="tpu_custom_call" | custom-call | flops 10000000 | bytes 1000000 | tf_op jit(solution)/shard_map/pallas_call | solution.py:33
  14.0 0.0 collective-permute-done.top
  14.0 0.0 collective-permute-done.1.bottom
  14.0 12.3 %all-to-all-start = ((f32[64,1,128]{2,1,0:T(1,128)}), f32[64,1,128]{2,1,0:T(1,128)S(1)}, u32[]{:S(2)}, u32[]{:S(2)}) async-start(f32[64,1,128]{2,1,0:T(1,128)} %bitcast.3), calls=%async_computation | async-start | bytes 65536 | tf_op jit(solution)/shard_map/all_to_all | solution.py:398
  26.4 2.0 %collective-permute-start.2 = (bf16[2,16,320]{2,1,0:T(8,128)(2,1)S(1)}, bf16[2,16,320]{2,1,0:T(8,128)(2,1)S(1)}, u32[]{:S(2)}, u32[]{:S(2)}) collective-permute-start(bf16[2,16,320]{2,1,0:T(8,128)(2,1)S(1)} %get-tuple-element.27), channel_id=1, source_target_pairs={{0,1},{1,2},{2,3},{3,4},{4,5},{5,6},{6,7},{7,0},{8,9},{9,10},{10,1... | collective-permute-start | bytes 61448 | tf_op jit(solution)/shard_map/ppermute | solution.py:396
  28.4 5.7 %collective-permute-start.3 = (bf16[2,16,320]{2,1,0:T(8,128)(2,1)S(1)}, bf16[2,16,320]{2,1,0:T(8,128)(2,1)S(1)}, u32[]{:S(2)}, u32[]{:S(2)}) collective-permute-start(bf16[2,16,320]{2,1,0:T(8,128)(2,1)S(1)} %get-tuple-element.28), channel_id=1, source_target_pairs={{1,0},{2,1},{3,2},{4,3},{5,4},{6,5},{7,6},{0,7},{9,8},{10,9},{11,1... | collective-permute-start | bytes 61448 | tf_op jit(solution)/shard_map/ppermute | solution.py:397
  34.1 0.0 copy-done.8
  34.1 0.0 copy-done.9
  34.1 0.0 copy-done.10
  34.2 0.7 reshape.40.ref_shift
  34.8 0.0 collective-permute-done.2.left
  34.8 0.7 collective-permute-done.3.right
  35.6 0.4 all-to-all-done
  36.0 0.0 copy-done.1
  36.0 0.0 copy-done.3
  36.0 0.0 copy-start.5
  36.0 1.6 %copy-done.5 = bf16[9,320,320]{2,1,0:T(8,128)(2,1)S(1)} copy-done((bf16[9,320,320]{2,1,0:T(8,128)(2,1)S(1)}, bf16[9,320,320]{2,1,0:T(8,128)(2,1)}, u32[]{:S(2)}) %copy-start.5) | copy-done | bytes 1843224
  37.6 0.0 copy-start.6
  37.6 0.9 copy-done.6
  38.5 0.0 copy-start.7
  38.5 0.9 copy-done.7
  39.4 11.1 %shard_map.150 = (f32[32,48,320]{2,1,0:T(8,128)}, s16[32,48,320]{2,1,0:T(8,128)(2,1)S(1)}, f32[8,320]{1,0:T(8,128)S(1)}) custom-call(f32[64,128]{1,0:T(8,128)S(1)} %bitcast.21, f32[8,320]{1,0:T(8,128)S(1)} %get-tuple-element.26.bias, f32[1,320]{1,0:T(1,128)S(1)} %reshape.37.gain, f32[1,320]{1,0:T(1,128)S(1)} %reshape.38.shift, ...), custom_call_target="tpu_custom_call" | custom-call | flops 2000000000 | bytes 10000000 | tf_op jit(solution)/shard_map/pallas_call | solution.py:33
  50.5 2.9 %collective-permute-start.4 = (s16[32,48,320]{2,1,0:T(8,128)(2,1)S(1)}, s16[32,48,320]{2,1,0:T(8,128)(2,1)S(1)}, u32[]{:S(2)}, u32[]{:S(2)}) collective-permute-start(s16[32,48,320]{2,1,0:T(8,128)(2,1)S(1)} %get-tuple-element.31), channel_id=1, source_target_pairs={{0,1},{1,0},{2,3},{3,2},{4,5},{5,4},{6,7},{7,6},{8,9},{9,8},{10,11... | collective-permute-start | bytes 2949128 | tf_op jit(solution)/shard_map/ppermute | solution.py:420
  53.3 2.5 %collective-permute-done.4.other = s16[32,48,320]{2,1,0:T(8,128)(2,1)S(1)} collective-permute-done((s16[32,48,320]{2,1,0:T(8,128)(2,1)S(1)}, s16[32,48,320]{2,1,0:T(8,128)(2,1)S(1)}, u32[]{:S(2)}, u32[]{:S(2)}) %collective-permute-start.4) | collective-permute-done | bytes 983072 | tf_op jit(solution)/shard_map/ppermute | solution.py:420
  55.8 4.3 %shard_map.151 = s16[32,48,320]{2,1,0:T(8,128)(2,1)S(1)} custom-call(f32[32,48,320]{2,1,0:T(8,128)} %get-tuple-element.29.own, f32[8,320]{1,0:T(8,128)S(1)} %get-tuple-element.30.small, s16[32,48,320]{2,1,0:T(8,128)(2,1)S(1)} %collective-permute-done.4.other), custom_call_target="tpu_custom_call" | custom-call | tf_op jit(solution)/shard_map/pallas_call | solution.py:33
  60.1 21.2 %all_to_all.21.blocks = s16[32,48,320]{2,1,0:T(8,128)(2,1)S(1)} all-to-all(s16[32,48,320]{2,1,0:T(8,128)(2,1)S(1)} %shard_map.151), channel_id=1, replica_groups=mesh['y'=8,'x'=4,'zl'=2,'zh'=4,'core'=2] {'x'}, dimensions={0} | all-to-all | bytes 1966080 | tf_op jit(solution)/shard_map/all_to_all | solution.py:422
  81.3 2.6 %shard_map.152 = s16[8,8,24,128]{3,2,1,0:T(8,128)(2,1)S(1)} custom-call(s16[32,48,320]{2,1,0:T(8,128)(2,1)S(1)} %all_to_all.21.blocks), custom_call_target="tpu_custom_call" | custom-call | tf_op jit(solution)/shard_map/pallas_call | solution.py:33
  83.9 29.1 %all_to_all.22 = s16[64,24,128]{2,1,0:T(8,128)(2,1)S(1)} all-to-all(s16[64,24,128]{2,1,0:T(8,128)(2,1)S(1)} %bitcast.12), channel_id=1, replica_groups=mesh['y'=8,'x'=4,'zl'=2,'zh'=4,'core'=2] {'y','zl','zh'}, dimensions={0} | all-to-all | bytes 786432 | tf_op jit(solution)/shard_map/all_to_all | solution.py:424
  113.0 1.4 %shard_map.153 = (f32[1,1]{1,0:T(1,128)}, f32[40,45]{1,0:T(8,128)}, f32[1,320]{1,0:T(1,128)S(1)}, f32[1,320]{1,0:T(1,128)S(1)}) custom-call(s16[8,8,24,128]{3,2,1,0:T(8,128)(2,1)S(1)} %bitcast.11), custom_call_target="tpu_custom_call" | custom-call | tf_op jit(solution)/shard_map/pallas_call | solution.py:33
  114.3 0.6 reduce
  114.9 0.6 reduce.1
  (5 shorter events, 0.1 us)
Async XLA Ops:
  0.6 33.5 %copy-start.8 = (f32[320]{0:T(512)S(1)}, f32[320]{0:T(512)}, u32[]{:S(2)}) copy-start(f32[320]{0:T(512)} %param.19) | copy-start | bytes 3844
  0.6 0.9 copy-start
  1.5 0.9 copy-start.2
  2.4 31.7 %copy-start.9 = (f32[320]{0:T(512)S(1)}, f32[320]{0:T(512)}, u32[]{:S(2)}) copy-start(f32[320]{0:T(512)} %param.20) | copy-start | bytes 3844
  2.4 31.7 %copy-start.10 = (f32[320]{0:T(512)S(1)}, f32[320]{0:T(512)}, u32[]{:S(2)}) copy-start(f32[320]{0:T(512)} %param.21) | copy-start | bytes 3844
  2.4 33.5 %copy-start.1 = (bf16[1,8,16,320]{3,2,1,0:T(8,128)(2,1)S(1)}, bf16[1,8,16,320]{3,2,1,0:T(8,128)(2,1)}, u32[]{:S(2)}) copy-start(bf16[1,8,16,320]{3,2,1,0:T(8,128)(2,1)} %param.13) | copy-start | bytes 245764
  2.4 33.5 %copy-start.3 = (bf16[1,8,16,320]{3,2,1,0:T(8,128)(2,1)S(1)}, bf16[1,8,16,320]{3,2,1,0:T(8,128)(2,1)}, u32[]{:S(2)}) copy-start(bf16[1,8,16,320]{3,2,1,0:T(8,128)(2,1)} %param.14) | copy-start | bytes 245764
  2.5 11.5 %collective-permute-start = (bf16[2,16,320]{2,1,0:T(8,128)(2,1)S(1)}, bf16[2,16,320]{2,1,0:T(8,128)(2,1)S(1)}, u32[]{:S(2)}, u32[]{:S(2)}) collective-permute-start(bf16[2,16,320]{2,1,0:T(8,128)(2,1)S(1)} %get-tuple-element.21), channel_id=1, source_target_pairs={{0,8},{8,16},{16,24},{24,32},{32,40},{40,48},{48,56},{56,0},{1,9},... | collective-permute-start | bytes 61448 | tf_op jit(solution)/shard_map/ppermute | solution.py:389
  6.9 7.1 %collective-permute-start.1 = (bf16[2,16,320]{2,1,0:T(8,128)(2,1)S(1)}, bf16[2,16,320]{2,1,0:T(8,128)(2,1)S(1)}, u32[]{:S(2)}, u32[]{:S(2)}) collective-permute-start(bf16[2,16,320]{2,1,0:T(8,128)(2,1)S(1)} %get-tuple-element.22), channel_id=1, source_target_pairs={{8,0},{16,8},{24,16},{32,24},{40,32},{48,40},{56,48},{0,56},{9,1},... | collective-permute-start | bytes 61448 | tf_op jit(solution)/shard_map/ppermute | solution.py:390
  11.7 1.0 copy-start.4
  14.0 21.9 %all-to-all-start = ((f32[64,1,128]{2,1,0:T(1,128)}), f32[64,1,128]{2,1,0:T(1,128)S(1)}, u32[]{:S(2)}, u32[]{:S(2)}) async-start(f32[64,1,128]{2,1,0:T(1,128)} %bitcast.3), calls=%async_computation | async-start | bytes 65536 | tf_op jit(solution)/shard_map/all_to_all | solution.py:398
  26.4 8.4 %collective-permute-start.2 = (bf16[2,16,320]{2,1,0:T(8,128)(2,1)S(1)}, bf16[2,16,320]{2,1,0:T(8,128)(2,1)S(1)}, u32[]{:S(2)}, u32[]{:S(2)}) collective-permute-start(bf16[2,16,320]{2,1,0:T(8,128)(2,1)S(1)} %get-tuple-element.27), channel_id=1, source_target_pairs={{0,1},{1,2},{2,3},{3,4},{4,5},{5,6},{6,7},{7,0},{8,9},{9,10},{10,1... | collective-permute-start | bytes 61448 | tf_op jit(solution)/shard_map/ppermute | solution.py:396
  28.4 7.2 %collective-permute-start.3 = (bf16[2,16,320]{2,1,0:T(8,128)(2,1)S(1)}, bf16[2,16,320]{2,1,0:T(8,128)(2,1)S(1)}, u32[]{:S(2)}, u32[]{:S(2)}) collective-permute-start(bf16[2,16,320]{2,1,0:T(8,128)(2,1)S(1)} %get-tuple-element.28), channel_id=1, source_target_pairs={{1,0},{2,1},{3,2},{4,3},{5,4},{6,5},{7,6},{0,7},{9,8},{10,9},{11,1... | collective-permute-start | bytes 61448 | tf_op jit(solution)/shard_map/ppermute | solution.py:397
  36.0 1.6 %copy-start.5 = (bf16[9,320,320]{2,1,0:T(8,128)(2,1)S(1)}, bf16[9,320,320]{2,1,0:T(8,128)(2,1)}, u32[]{:S(2)}) copy-start(bf16[9,320,320]{2,1,0:T(8,128)(2,1)} %weight.1) | copy-start | bytes 5529604
  37.6 0.9 copy-start.6
  38.5 0.9 copy-start.7
  50.5 5.3 %collective-permute-start.4 = (s16[32,48,320]{2,1,0:T(8,128)(2,1)S(1)}, s16[32,48,320]{2,1,0:T(8,128)(2,1)S(1)}, u32[]{:S(2)}, u32[]{:S(2)}) collective-permute-start(s16[32,48,320]{2,1,0:T(8,128)(2,1)S(1)} %get-tuple-element.31), channel_id=1, source_target_pairs={{0,1},{1,0},{2,3},{3,2},{4,5},{5,4},{6,7},{7,6},{8,9},{9,8},{10,11... | collective-permute-start | bytes 2949128 | tf_op jit(solution)/shard_map/ppermute | solution.py:420

commit v2 on v1

v2 whole, which is shorter than its diff:
```python
import functools
import math

import jax
import jax.numpy as jnp
from jax import lax
from jax.experimental import pallas as pl
from jax.experimental.pallas import tpu as pltpu
from jax.sharding import Mesh
from jax.sharding import PartitionSpec as P

C = 320
GROUPS = 32
TAPS = 9
TH, TW = 8, 16
PIX = TH * TW
BLK = 45
PIXELS = 64 * 128
BETA = 40.0
F32 = jnp.float32
BF16 = jnp.bfloat16
I16 = jnp.int16
HIGHEST = lax.Precision.HIGHEST
VMEM_LIMIT = 28 * 1024 * 1024


def call(kernel, outs, scratch=(), flops=0, nbytes=0, far=()):
    def run(*args):
        specs = [
            pl.BlockSpec(memory_space=pl.ANY if i in far else pltpu.VMEM) for i in range(len(args))
        ]
        return pl.pallas_call(
            kernel,
            out_shape=[jax.ShapeDtypeStruct(s, d) for s, d in outs],
            in_specs=specs,
            out_specs=[pl.BlockSpec(memory_space=pltpu.VMEM) for _ in outs],
            scratch_shapes=list(scratch),
            compiler_params=pltpu.CompilerParams(vmem_limit_bytes=VMEM_LIMIT),
            cost_estimate=pl.CostEstimate(flops=flops, bytes_accessed=nbytes, transcendentals=0),
        )(*args)

    return run


def pow2(n):
    size = jnp.abs(n)
    out = jnp.ones(n.shape, F32)
    for bit in range(7):
        step = jnp.where(n < 0, 0.5 ** (2**bit) if bit < 7 else 0.0, 2.0 ** (2**bit))
        out = out * jnp.where((size & (1 << bit)) != 0, step, 1.0)
    return out


def exponent(peak):
    level = jnp.log(jnp.maximum(peak, 1e-30)) * (1.0 / math.log(2.0))
    return jnp.clip(jnp.ceil(level + 0.01), -100.0, 100.0).astype(jnp.int32)


def rounded(values, exps):
    return jnp.round(values * pow2(15 - exps))


def split_small(small):
    exps = exponent(jnp.abs(small))
    scaled = small * pow2(15 - exps)
    high = jnp.round(scaled)
    low = jnp.round((scaled - high) * 32768.0)
    return high, low, exps.astype(F32)


def write_extras(extra, small):
    high, low, exps = split_small(small)
    extra[...] = jnp.zeros_like(extra)
    for k in range(3):
        extra[k, 0:1, :] = high[k : k + 1]
        extra[k, 1:2, :] = low[k : k + 1]
    extra[3, 0:1, :] = exps[0:1]
    extra[3, 1:2, :] = exps[1:2]
    extra[4, 0:1, :] = exps[2:3]


def read_extras(blocks, base):
    tails = [blocks[base + k].astype(jnp.int32)[40:48] for k in range(5)]
    exps = [tails[3][6:7], tails[3][7:8], tails[4][6:7]]
    rows = []
    for k in range(3):
        high = tails[k][6:7].astype(F32)
        low = tails[k][7:8].astype(F32)
        rows.append((high + low * (1.0 / 32768.0)) * pow2(exps[k] - 15))
    return jnp.concatenate(rows + [jnp.zeros((5, C), F32)], axis=0)


def packed_block(block, extra):
    exps = exponent(jnp.max(jnp.abs(block), axis=0, keepdims=True))
    q = rounded(block, exps)
    row = lax.broadcasted_iota(jnp.int32, (8, C), 0)
    tail = jnp.where(row == 5, exps.astype(F32), q[40:48])
    tail = jnp.where(row == 6, extra[0:1], tail)
    tail = jnp.where(row == 7, extra[1:2], tail)
    q = jnp.concatenate([q[0:40], tail], axis=0)
    return q.astype(jnp.int32).astype(I16)


def unpacked_block(block):
    q = block.astype(jnp.int32)
    v = q.astype(F32) * pow2(q[45:46] - 15)
    row = lax.broadcasted_iota(jnp.int32, (8, C), 0)
    return jnp.concatenate([v[0:40], jnp.where(row < BLK - 40, v[40:48], 0.0)], axis=0)


def stats_and_time(
    step, fw, fl, time_weight, stats, bias, first, last, here, table, number, sems
):
    copies = [
        pltpu.make_async_copy(fw, here.at[0], sems.at[0]),
        pltpu.make_async_copy(fl, here.at[1], sems.at[1]),
        pltpu.make_async_copy(step, number, sems.at[2]),
        pltpu.make_async_copy(time_weight, table, sems.at[3]),
    ]
    for copy in copies:
        copy.start()
    copies[0].wait()
    copies[1].wait()
    total = jnp.zeros((8, 128), F32)
    rows = lax.broadcasted_iota(jnp.int32, (C, 128), 0)
    lanes = lax.broadcasted_iota(jnp.int32, (C, 128), 1)
    size = C // GROUPS
    for k in range(2):
        first[k] = here[k, 0]
        last[k] = here[k, TH - 1]
        x = here[k].astype(F32).reshape(PIX, C)
        sums = jnp.sum(x, axis=0, keepdims=True)
        squares = jnp.sum(x * x, axis=0, keepdims=True)
        for j, part in enumerate((sums, squares)):
            group = lanes - GROUPS * (2 * k + j)
            member = (group >= 0) & (group < GROUPS)
            member = member & (rows >= group * size) & (rows < group * size + size)
            total = total + jnp.dot(
                jnp.broadcast_to(part, (8, C)),
                member.astype(F32),
                precision=HIGHEST,
                preferred_element_type=F32,
            )
    stats[...] = jnp.broadcast_to(total[0:1], stats.shape)
    half = C // 2
    lane = lax.broadcasted_iota(jnp.int32, (8, C), 1)
    place = jnp.where(lane < half, lane, lane - half).astype(F32)
    frequency = jnp.exp(-math.log(10000.0) * place / half)
    copies[2].wait()
    angles = number[0].astype(F32) * frequency
    sinusoid = jnp.where(lane < half, jnp.cos(angles), jnp.sin(angles))
    gate = sinusoid * jax.nn.sigmoid(sinusoid)
    copies[3].wait()
    bias[...] = jnp.dot(gate, table[...], precision=HIGHEST, preferred_element_type=F32)


def edge_column(top, bottom, fw, fl, side):
    core = lax.axis_index("core")
    for s, ref in enumerate((fw, fl)):
        x = ref[...].astype(F32)
        above = top[s].astype(F32)
        below = bottom[s].astype(F32)
        column = [
            jnp.concatenate(
                [above[col : col + 1]]
                + [x[r, col : col + 1] for r in range(TH)]
                + [below[col : col + 1], jnp.zeros((6, C), F32)],
                axis=0,
            )
            for col in (0, TW - 1)
        ]
        side[s] = jnp.where(core == 0, column[0], column[1]).astype(BF16)


def tile_payload(top, bottom, side, fw, fl, nw, nl, out, sems):
    copies = [
        pltpu.make_async_copy(nw, out.at[0, pl.ds(11, TH)], sems.at[0]),
        pltpu.make_async_copy(nl, out.at[1, pl.ds(11, TH)], sems.at[1]),
    ]
    for copy in copies:
        copy.start()
    for s, ref in enumerate((fw, fl)):
        out[s, 0] = top[s]
        out[s, 1 : TH + 1] = ref[...]
        out[s, TH + 1] = bottom[s]
        out[s, TH + 2] = side[s]
    for copy in copies:
        copy.wait()


def forward(
    stats, bias, gain, shift, ref_gain, ref_shift, mine, theirs, weight_far, ref_far,
    cols, cot_out, small, field, act, back, weight, ref_weight, sems,
):
    copies = [
        pltpu.make_async_copy(ref_far, ref_weight, sems.at[0]),
        pltpu.make_async_copy(weight_far, weight, sems.at[1]),
    ]
    for copy in copies:
        copy.start()
    core = lax.axis_index("core")
    row_at = 2 * lax.axis_index("x") + lax.axis_index("zl")
    chip_at = 2 * lax.axis_index("zh")
    col_at = (chip_at + core, chip_at + 1 - core)

    total = jnp.broadcast_to(jnp.sum(stats[...], axis=0, keepdims=True), (8, 128))
    groups = lax.broadcasted_iota(jnp.int32, (128, C), 0)
    chans = lax.broadcasted_iota(jnp.int32, (128, C), 1)
    size = C // GROUPS
    entries = float(PIXELS * size)

    def by_channel(k):
        group = groups - GROUPS * k
        member = (group >= 0) & (group < GROUPS)
        member = member & (chans >= group * size) & (chans < group * size + size)
        spread = jnp.dot(total, member.astype(F32), precision=HIGHEST, preferred_element_type=F32)
        return spread[0:1] / entries

    means, scales = [], []
    for s in range(2):
        mean, square = by_channel(2 * s), by_channel(2 * s + 1)
        means.append(mean)
        scales.append(lax.rsqrt(square - mean * mean + 1e-05))

    tiles = (mine, theirs)
    for w in range(2):
        for s in range(2):
            here, beside = tiles[w], tiles[1 - w]
            f = 2 * w + s
            field[f, :, TW + 2 :, :] = jnp.zeros((TH + 2, 22 - TW, C), F32)
            field[f, :, 1 : TW + 1, :] = here[s, 0 : TH + 2].astype(F32)
            outer = here[s, TH + 2].astype(F32)
            is_left = core == w
            for r in range(TH + 2):
                near = beside[s, r].astype(F32)
                out = outer[r : r + 1]
                field[f, r, 0:1, :] = jnp.where(is_left, out, near[TW - 1 : TW])
                field[f, r, TW + 1 : TW + 2, :] = jnp.where(is_left, near[0:1], out)

    column = lax.broadcasted_iota(jnp.int32, (24, C), 0)
    inside = []
    for w in range(2):
        ok = (column < TW + 2) & ((column > 0) | (col_at[w] > 0))
        inside.append(ok & ((column < TW + 1) | (col_at[w] < 7)))

    def valid(w, r):
        if r == 0:
            return inside[w] & (row_at > 0)
        if r == TH + 1:
            return inside[w] & (row_at < 7)
        return inside[w]

    def pre_act(f, r, g, b):
        normed = (field[f, r] - means[f % 2]) * scales[f % 2]
        return normed, normed * g + b

    def columns_of(fields, g, b):
        for f in fields:
            for r in range(TH + 2):
                _, pre = pre_act(f, r, g, b)
                act[r] = jnp.where(valid(f // 2, r), pre * jax.nn.sigmoid(pre), 0.0)
            for t in range(TAPS):
                a, c = t // 3, t % 3
                piece = act[a : a + TH, c : c + TW, :].reshape(PIX, C).astype(BF16)
                cols[f * PIX : (f + 1) * PIX, C * t : C * (t + 1)] = piece

    def base(f):
        tile, s = tiles[f // 2], f % 2
        noise = tile[s, TH + 3 : 2 * TH + 3].astype(F32)
        return (tile[s, 1 : TH + 1].astype(F32) - noise).reshape(PIX, C)

    def residual(fields, kernel):
        conv = jnp.dot(
            cols[0 : PIX * len(fields)],
            kernel[...].reshape(TAPS * C, C),
            preferred_element_type=F32,
        )
        return [base(f) + conv[PIX * f : PIX * (f + 1)] for f in fields]

    def signed_squares(resid):
        return jnp.sum(resid[0] * resid[0] - resid[1] * resid[1], axis=0, keepdims=True)

    time_row = bias[0:1]
    columns_of((0, 1), ref_gain[...].reshape(1, C), ref_shift[...].reshape(1, C) + time_row)
    copies[0].wait()
    resid = residual((0, 1), ref_weight)
    margin = -signed_squares(resid)
    g, b = gain[...].reshape(1, C), shift[...].reshape(1, C) + time_row
    columns_of((0, 1, 2, 3), g, b)
    copies[1].wait()
    resid = residual((0, 1, 2, 3), weight)
    margin = margin + signed_squares(resid)
    for f in range(4):
        cot_out[PIX * f : PIX * (f + 1)] = (resid[f] if f % 2 == 0 else -resid[f]).astype(BF16)

    cot = cot_out[0 : 2 * PIX]
    back[...] = jnp.zeros_like(back)
    for t in range(TAPS):
        a, c = t // 3, t % 3
        term = lax.dot_general(
            cot, weight[t], (((1,), (1,)), ((), ())), preferred_element_type=F32
        )
        for s in range(2):
            back[s, a : a + TH, c : c + TW, :] += term[s * PIX : (s + 1) * PIX].reshape(TH, TW, C)
    gains = jnp.zeros((24, C), F32)
    shifts = jnp.zeros((24, C), F32)
    for s in range(2):
        for r in range(TH + 2):
            normed, pre = pre_act(s, r, g, b)
            gate = jax.nn.sigmoid(pre)
            slope = gate * (1.0 + pre * (1.0 - gate))
            dpre = jnp.where(valid(0, r), back[s, r] * slope, 0.0)
            gains = gains + dpre * normed
            shifts = shifts + dpre
    small[...] = jnp.concatenate(
        [
            jnp.sum(gains, axis=0, keepdims=True),
            jnp.sum(shifts, axis=0, keepdims=True),
            jnp.broadcast_to(jnp.sum(margin, axis=1, keepdims=True), (1, C)),
            jnp.zeros((5, C), F32),
        ],
        axis=0,
    )


def kernel_gradient(cols, cot, out, grad):
    grad[0 : TAPS * C, :] = lax.dot_general(
        cols[...], cot[...], (((0,), (0,)), ((), ())), preferred_element_type=F32
    )
    row = lax.broadcasted_iota(jnp.int32, (48, C), 0)
    for core in range(2):

        @pl.when(lax.axis_index("core") == core)
        def _():
            for q in range(32):
                start = BLK * (2 * q + core)
                out[q] = jnp.where(row < BLK, grad[start : start + 48, :], 0.0)


def pack_blocks(blocks, small, other, out, extra):
    write_extras(extra, small[...] + other[...])

    def body(i, carry):
        for k in range(4):
            q = 4 * i + k
            out[q] = packed_block(blocks[q], extra[lax.rem(q, 8)])
        return carry

    lax.fori_loop(0, 8, body, 0)


def chip_sum(blocks, out):
    small = read_extras(blocks, 0)
    for source in range(1, 4):
        small = small + read_extras(blocks, 8 * source)
    high, low, exps = split_small(small)
    lane = lax.broadcasted_iota(jnp.int32, (1, 128), 1)
    tail = jnp.zeros((1, 128), F32)
    vectors = []
    for k in range(2):
        e = exponent(jnp.max(jnp.abs(small[k : k + 1]), axis=1, keepdims=True))
        q = rounded(small[k : k + 1], e)
        q = jnp.concatenate([q, jnp.zeros((1, 64), F32)], axis=1)
        vectors += [q[:, 0:128], q[:, 128:256], q[:, 256:384]]
        tail = jnp.where(lane == k, e.astype(F32), tail)
    for k, part in enumerate((high, low, exps)):
        tail = jnp.where(lane == 2 + k, part[2:3, 0:128], tail)

    def body(z, carry):
        block = unpacked_block(blocks[z])
        for source in range(1, 4):
            block = block + unpacked_block(blocks[8 * source + z])
        e = exponent(jnp.max(jnp.abs(block), axis=0, keepdims=True))
        q = rounded(block, e)
        e = e.astype(F32)
        for y in range(8):
            part = q[:, 40 * y : 40 * y + 40]
            tile = jnp.concatenate(
                [part[0:16], part[16:32], part[32:48], jnp.zeros((16, 8), F32)], axis=1
            )
            ey = e[:, 40 * y : 40 * y + 40]
            ey = jnp.concatenate([ey, ey, ey, jnp.zeros((1, 8), F32)], axis=1)
            full = jnp.concatenate([tile] + vectors + [ey, tail], axis=0)
            out[y, z] = full.astype(jnp.int32).astype(I16)
        return carry

    lax.fori_loop(0, 8, body, 0)


def final_sum(blocks, loss, grad, gain, shift):
    y_at = lax.axis_index("y")
    weights = jnp.zeros((16, 128), F32)
    vectors = jnp.zeros((8, 128), F32)
    mine = jnp.zeros((1, 1), F32)
    row = lax.broadcasted_iota(jnp.int32, (8, 128), 0)
    for pair in range(8):
        part = jnp.zeros((16, 128), F32)
        vector = jnp.zeros((8, 128), F32)
        margin = jnp.zeros((1, 1), F32)
        for z in range(8):
            q = blocks[pair, z].astype(jnp.int32)
            v = q.astype(F32)
            tail = q[16:24]
            part = part + v[0:16] * pow2(tail[6:7] - 15)
            factor = pow2(tail[7:8] - 15)
            vector = vector + v[16:24] * jnp.where(row < 3, factor[:, 0:1], factor[:, 1:2])
            margin = margin + (v[23:24, 2:3] + v[23:24, 3:4] * (1.0 / 32768.0)) * factor[:, 4:5]
        margin = BETA * (margin / float(PIXELS * C))
        scale = BETA * jax.nn.sigmoid(margin) * (2.0 / (8 * C))
        weights = weights + scale * part
        vectors = vectors + scale * vector
        mine = jnp.where(y_at == pair, margin, mine)
    near = jnp.exp(-jnp.abs(mine))
    one = 1.0 + near
    log1p = jnp.where(one == 1.0, near, jnp.log(one) * near / jnp.where(one == 1.0, 1.0, one - 1.0))
    loss[...] = jnp.maximum(mine, 0.0) + log1p
    tall = jnp.concatenate([weights, jnp.roll(weights, -40, 1), jnp.roll(weights, -80, 1)], axis=0)
    tall = jnp.concatenate([tall, jnp.zeros((80, 128), F32)], axis=0)
    grad[...] = tall.T[0:40, 0:BLK]
    for out, k in ((gain, 0), (shift, 3)):
        pieces = [vectors[k : k + 1], vectors[k + 1 : k + 2], vectors[k + 2 : k + 3, 0:64]]
        out[...] = jnp.concatenate(pieces, axis=1).reshape(C)


def local(
    timesteps, features_win, features_lose, noise_win, noise_lose, conv_weight, ref_weight,
    norm_gain, norm_shift, ref_gain, ref_shift, time_weight,
):
    fw, fl = features_win[0], features_lose[0]
    strip = (2, TW, C)
    rows, columns = ("x", "zl"), ("zh", "core")
    up = [((i + 1) % 8, i) for i in range(8)]
    down = [(i, (i + 1) % 8) for i in range(8)]
    outward = [(i, (i + 1) % 8 if i % 2 else (i + 7) % 8) for i in range(8)]
    swap = [(0, 1), (1, 0)]

    stats, bias, first, last = call(
        stats_and_time,
        [((64, 128), F32), ((8, C), F32), (strip, BF16), (strip, BF16)],
        [
            pltpu.VMEM((2, TH, TW, C), BF16),
            pltpu.VMEM((C, C), F32),
            pltpu.SMEM((1,), jnp.int32),
            pltpu.SemaphoreType.DMA((4,)),
        ],
        flops=10**7,
        nbytes=10**6,
        far=(0, 1, 2, 3),
    )(timesteps, fw, fl, time_weight)
    stats = lax.all_to_all(stats, ("x", "zl", "zh", "core"), 0, 0, tiled=True)
    top = lax.ppermute(last, rows, down)
    bottom = lax.ppermute(first, rows, up)
    (side,) = call(edge_column, [(strip, BF16)])(top, bottom, fw, fl)
    side = lax.ppermute(side, columns, outward)
    payload = (2, 2 * TH + 3, TW, C)
    (mine,) = call(
        tile_payload, [(payload, BF16)], [pltpu.SemaphoreType.DMA((2,))], far=(5, 6)
    )(top, bottom, side, fw, fl, noise_win[0], noise_lose[0])
    theirs = lax.ppermute(mine, "core", swap)

    cols, cot, small = call(
        forward,
        [((4 * PIX, TAPS * C), BF16), ((4 * PIX, C), BF16), ((8, C), F32)],
        [
            pltpu.VMEM((4, TH + 2, 24, C), F32),
            pltpu.VMEM((TH + 2, 24, C), F32),
            pltpu.VMEM((2, TH + 2, 24, C), F32),
            pltpu.VMEM((TAPS, C, C), BF16),
            pltpu.VMEM((TAPS, C, C), BF16),
            pltpu.SemaphoreType.DMA((2,)),
        ],
        flops=2 * 10**9,
        nbytes=10**7,
        far=(8, 9),
    )(
        stats, bias, norm_gain, norm_shift, ref_gain, ref_shift, mine, theirs, conv_weight,
        ref_weight,
    )
    other = lax.ppermute(small, "core", swap)
    block = (32, 48, C)
    (blocks,) = call(
        kernel_gradient,
        [(block, F32)],
        [pltpu.VMEM((TAPS * C + 8, C), F32)],
        flops=10**9,
        nbytes=10**7,
    )(cols, cot)
    (blocks,) = call(pack_blocks, [(block, I16)], [pltpu.VMEM((8, 8, C), F32)])(
        blocks, small, other
    )
    blocks = lax.all_to_all(blocks, "x", 0, 0, tiled=True)
    (sums,) = call(chip_sum, [((8, 8, 24, 128), I16)])(blocks)
    sums = lax.all_to_all(sums.reshape(64, 24, 128), ("y", "zl", "zh"), 0, 0, tiled=True)
    loss, grad, gain, shift = call(
        final_sum, [((1, 1), F32), ((40, BLK), F32), ((C,), F32), ((C,), F32)]
    )(sums.reshape(8, 8, 24, 128))
    return loss.reshape(1), grad, gain, shift


def solution(mesh):
    fine = Mesh(mesh.devices.reshape(8, 4, 2, 4, 2), ("y", "x", "zl", "zh", "core"))
    image = P("y", ("x", "zl"), ("zh", "core"), None)
    return jax.shard_map(
        local,
        mesh=fine,
        in_specs=(P("y"), image, image, image, image) + (P(),) * 7,
        out_specs=(P("y"), P("y", ("x", "zl", "zh", "core")), P(), P()),
        check_vma=False,
    )
```

time: 116 us -> 118 us (1.017)
  blocking collectives: 50.2 us -> 65.1 us
  starting transfers between devices: 31.4 us -> 20.9 us
  Pallas kernels: 20.7 us -> 16 us
  local copies, waits for them, and re-layouts: 6.93 us -> 10.6 us
  other arithmetic: 1.19 us -> 0 us
    all_to_all x1 -> x2, blocking collectives: 21.2 us -> 40.1 us  [the longest x1 20.2 us: local(): stats = lax.all_to_all(stats, ('x', 'zl', 'zh', 'core'), 0, 0, tiled=True)]
    all_to_all x1 -> x0, starting transfers between devices: 12.3 us -> none  [local(): stats = lax.all_to_all(stats, ('x', 'zl', 'zh', 'core'), 0, 0, tiled=True)]
    pallas_call x7 -> x8, Pallas kernels: 20.7 us -> 16 us  [run(): pl.pallas_call(kernel, out_shape=[jax.ShapeDtypeStruct(s, d) for s, d in...]
    unnamed x22, local copies, waits for them, and re-layouts: 6.24 us -> 10.6 us
    all_to_all x1, blocking collectives: 29.1 us -> 24.9 us  [local(): lax.all_to_all(sums.reshape(64, 24, 128), ('y', 'zl', 'zh'), 0, 0, tiled=...]
    ppermute x3, starting transfers between devices: 10.5 us -> 12.5 us  [the longest x1 8.7 us: local(): side = lax.ppermute(side, columns, outward)]
    ppermute x3, waiting for transfers between devices: 3.2 us -> 1.5 us  [the longest x1 1.5 us: local(): side = lax.ppermute(side, columns, outward)]
    ppermute x1, waiting for transfers between devices: 0.01 us -> 1.59 us  [local(): bottom = lax.ppermute(first, rows, up)]
  transfers between devices with their start and end apart: 6 -> 5, of which waited for: 3 -> 2; matrix products, arithmetic and copies ran while one was open for 1% -> 0% of each run, Pallas kernels for 1% -> 2%
where the time goes in v2:
time: 118 us; the launch traced here: 117 us
  blocking collectives  65.1 us (55%)
  starting transfers between devices  20.9 us (18%)
  Pallas kernels  16 us (14%)
  local copies, waits for them, and re-layouts  10.6 us (9%)
  waiting for transfers between devices  3.09 us (3%)
  between operations  1.4 us (1%)
    all_to_all x1, blocking collectives, local(): lax.all_to_all(sums.reshape(64, 24, 128), ('y', 'zl', 'zh'), 0, 0, tiled=...  24.9 us
    all_to_all x1, blocking collectives, local(): stats = lax.all_to_all(stats, ('x', 'zl', 'zh', 'core'), 0, 0, tiled=True)  20.2 us
    all_to_all x1, blocking collectives, local(): blocks = lax.all_to_all(blocks, 'x', 0, 0, tiled=True)  19.9 us
    pallas_call x8, Pallas kernels, run(): pl.pallas_call(kernel, out_shape=[jax.ShapeDtypeStruct(s, d) for s, d in...  16 us
    unnamed x22, local copies, waits for them, and re-layouts  10.6 us
    ppermute x1, starting transfers between devices, local(): side = lax.ppermute(side, columns, outward)  8.7 us
    ppermute x1, starting transfers between devices, local(): top = lax.ppermute(last, rows, down)  4.28 us
    ppermute x1, starting transfers between devices, local(): bottom = lax.ppermute(first, rows, up)  4.12 us
  transfers between devices with their start and end apart: 5, of which 2 were waited for; matrix products, arithmetic and copies ran while one was open for 0% of the time, Pallas kernels for 2%

profile of v2, /device:TPU:8, one launch (start us, length us, event | category | flops | bytes accessed | tf_op | source)
XLA Modules:
  0.0 117.0 jit_solution(16461596237379789075)
XLA Ops:
  1.3 0.0 copy-start
  1.3 0.9 copy-done
  2.2 0.0 copy-start.1
  2.2 0.9 copy-done.1
  3.1 0.0 copy-start.2
  3.1 1.0 copy-done.2
  4.1 1.7 %shard_map.147 = (f32[64,128]{1,0:T(8,128)S(1)}, f32[8,320]{1,0:T(8,128)S(1)}, bf16[2,16,320]{2,1,0:T(8,128)(2,1)S(1)}, bf16[2,16,320]{2,1,0:T(8,128)(2,1)S(1)}) custom-call(s32[1]{0:T(128)S(6)} %copy.17.step, bf16[8,16,320]{2,1,0:T(8,128)(2,1)S(1)} %bitcast.13, bf16[8,16,320]{2,1,0:T(8,128)(2,1)S(1)} %bitcast.16, f32[320,320]{1,0:T(8,128)S(1)} %copy-done.2), custom_call_target="tpu_custom_call" | custom-call | flops 10000000 | bytes 1000000 | tf_op jit(solution)/shard_map/pallas_call | solution.py:32
  5.8 4.3 %collective-permute-start = (bf16[2,16,320]{2,1,0:T(8,128)(2,1)S(1)}, bf16[2,16,320]{2,1,0:T(8,128)(2,1)S(1)}, u32[]{:S(2)}, u32[]{:S(2)}) collective-permute-start(bf16[2,16,320]{2,1,0:T(8,128)(2,1)S(1)} %get-tuple-element.17), channel_id=1, source_target_pairs={{0,8},{8,16},{16,24},{24,32},{32,40},{40,48},{48,56},{56,0},{1,9},... | collective-permute-start | bytes 61448 | tf_op jit(solution)/shard_map/ppermute | solution.py:451
  10.1 4.1 %collective-permute-start.1 = (bf16[2,16,320]{2,1,0:T(8,128)(2,1)S(1)}, bf16[2,16,320]{2,1,0:T(8,128)(2,1)S(1)}, u32[]{:S(2)}, u32[]{:S(2)}) collective-permute-start(bf16[2,16,320]{2,1,0:T(8,128)(2,1)S(1)} %get-tuple-element.18), channel_id=1, source_target_pairs={{8,0},{16,8},{24,16},{32,24},{40,32},{48,40},{56,48},{0,56},{9,1},... | collective-permute-start | bytes 61448 | tf_op jit(solution)/shard_map/ppermute | solution.py:452
  14.2 0.0 collective-permute-done.top
  14.2 1.6 %collective-permute-done.1.bottom = bf16[2,16,320]{2,1,0:T(8,128)(2,1)S(1)} collective-permute-done((bf16[2,16,320]{2,1,0:T(8,128)(2,1)S(1)}, bf16[2,16,320]{2,1,0:T(8,128)(2,1)S(1)}, u32[]{:S(2)}, u32[]{:S(2)}) %collective-permute-start.1) | collective-permute-done | bytes 20512 | tf_op jit(solution)/shard_map/ppermute | solution.py:452
  15.8 0.1 shard_map.148
  15.8 8.7 %collective-permute-start.2 = (bf16[2,16,320]{2,1,0:T(8,128)(2,1)S(1)}, bf16[2,16,320]{2,1,0:T(8,128)(2,1)S(1)}, u32[]{:S(2)}, u32[]{:S(2)}) collective-permute-start(bf16[2,16,320]{2,1,0:T(8,128)(2,1)S(1)} %shard_map.148), channel_id=1, source_target_pairs={{0,7},{1,2},{2,1},{3,4},{4,3},{5,6},{6,5},{7,0},{8,15},{9,10},{10,... | collective-permute-start | bytes 61448 | tf_op jit(solution)/shard_map/ppermute | solution.py:454
  24.5 1.5 %collective-permute-done.2.side = bf16[2,16,320]{2,1,0:T(8,128)(2,1)S(1)} collective-permute-done((bf16[2,16,320]{2,1,0:T(8,128)(2,1)S(1)}, bf16[2,16,320]{2,1,0:T(8,128)(2,1)S(1)}, u32[]{:S(2)}, u32[]{:S(2)}) %collective-permute-start.2) | collective-permute-done | bytes 20512 | tf_op jit(solution)/shard_map/ppermute | solution.py:454
  26.0 0.0 copy-start.3
  26.0 0.9 copy-done.3
  26.9 0.0 copy-start.4
  26.9 0.9 copy-done.4
  27.8 0.3 shard_map.149.mine
  28.1 1.9 %collective-permute-start.3 = (bf16[2,19,16,320]{3,2,1,0:T(8,128)(2,1)S(1)}, bf16[2,19,16,320]{3,2,1,0:T(8,128)(2,1)S(1)}, u32[]{:S(2)}, u32[]{:S(2)}) collective-permute-start(bf16[2,19,16,320]{3,2,1,0:T(8,128)(2,1)S(1)} %shard_map.149.mine), channel_id=1, source_target_pairs={{0,1},{1,0},{2,3},{3,2},{4,5},{5,4},{6,7},{7,6},{8,9},{9,8},{10,11... | collective-permute-start | bytes 1167368 | tf_op jit(solution)/shard_map/ppermute | solution.py:459
  30.0 20.2 %all_to_all.21 = f32[64,1,128]{2,1,0:T(1,128)S(1)} all-to-all(f32[64,1,128]{2,1,0:T(1,128)S(1)} %bitcast.21), channel_id=1, replica_groups=mesh['y'=8,'x'=4,'zl'=2,'zh'=4,'core'=2] {'x','zl','zh','core'}, dimensions={0} | all-to-all | bytes 65536 | tf_op jit(solution)/shard_map/all_to_all | solution.py:450
  50.3 0.0 collective-permute-done.3.theirs
  50.3 0.0 copy-start.5
  50.3 1.6 %copy-done.5 = bf16[9,320,320]{2,1,0:T(8,128)(2,1)S(1)} copy-done((bf16[9,320,320]{2,1,0:T(8,128)(2,1)S(1)}, bf16[9,320,320]{2,1,0:T(8,128)(2,1)}, u32[]{:S(2)}) %copy-start.5) | copy-done | bytes 1843224
  51.9 0.0 copy-start.6
  51.9 1.6 %copy-done.6 = bf16[9,320,320]{2,1,0:T(8,128)(2,1)S(1)} copy-done((bf16[9,320,320]{2,1,0:T(8,128)(2,1)S(1)}, bf16[9,320,320]{2,1,0:T(8,128)(2,1)}, u32[]{:S(2)}) %copy-start.6) | copy-done | bytes 1843224
  53.5 0.0 copy-start.7
  53.5 0.7 copy-done.7
  54.2 0.0 copy-start.8
  54.2 0.7 copy-done.8
  54.9 0.0 copy-start.9
  54.9 0.7 copy-done.9
  55.6 0.0 copy-start.10
  55.6 0.7 copy-done.10
  56.3 6.9 %shard_map.150 = (bf16[512,2880]{1,0:T(8,128)(2,1)S(1)}, bf16[512,320]{1,0:T(8,128)(2,1)S(1)}, f32[8,320]{1,0:T(8,128)S(1)}) custom-call(f32[64,128]{1,0:T(8,128)S(1)} %bitcast.22, f32[8,320]{1,0:T(8,128)S(1)} %get-tuple-element.16.bias, f32[320]{0:T(512)S(1)} %copy-done.7, f32[320]{0:T(512)S(1)} %copy-done.8, f32[320]{0:T(512)S(1)} %copy-done.9, ...), custom_call_target="tpu_custom_call" | custom-call | flops 2000000000 | bytes 10000000 | tf_op jit(solution)/shard_map/pallas_call | solution.py:32
  63.1 1.9 %collective-permute-start.4 = (f32[8,320]{1,0:T(8,128)S(1)}, f32[8,320]{1,0:T(8,128)S(1)}, u32[]{:S(2)}, u32[]{:S(2)}) collective-permute-start(f32[8,320]{1,0:T(8,128)S(1)} %get-tuple-element.21.small), channel_id=1, source_target_pairs={{0,1},{1,0},{2,3},{3,2},{4,5},{5,4},{6,7},{7,6},{8,9},{9,8},{10,11... | collective-permute-start | bytes 30728 | tf_op jit(solution)/shard_map/ppermute | solution.py:479
  65.1 1.9 %shard_map.151.blocks = f32[32,48,320]{2,1,0:T(8,128)S(1)} custom-call(bf16[512,2880]{1,0:T(8,128)(2,1)S(1)} %get-tuple-element.19.cols, bf16[512,320]{1,0:T(8,128)(2,1)S(1)} %get-tuple-element.20.cot), custom_call_target="tpu_custom_call" | custom-call | flops 1000000000 | bytes 10000000 | tf_op jit(solution)/shard_map/pallas_call | solution.py:32
  67.0 0.0 collective-permute-done.4.other
  67.0 1.3 %shard_map.152 = s16[32,48,320]{2,1,0:T(8,128)(2,1)S(1)} custom-call(f32[32,48,320]{2,1,0:T(8,128)S(1)} %shard_map.151.blocks, f32[8,320]{1,0:T(8,128)S(1)} %get-tuple-element.21.small, f32[8,320]{1,0:T(8,128)S(1)} %collective-permute-done.4.other), custom_call_target="tpu_custom_call" | custom-call | tf_op jit(solution)/shard_map/pallas_call | solution.py:32
  68.3 19.9 %all_to_all.22.blocks = s16[32,48,320]{2,1,0:T(8,128)(2,1)S(1)} all-to-all(s16[32,48,320]{2,1,0:T(8,128)(2,1)S(1)} %shard_map.152), channel_id=1, replica_groups=mesh['y'=8,'x'=4,'zl'=2,'zh'=4,'core'=2] {'x'}, dimensions={0} | all-to-all | bytes 1966080 | tf_op jit(solution)/shard_map/all_to_all | solution.py:491
  88.2 2.6 %shard_map.153 = s16[8,8,24,128]{3,2,1,0:T(8,128)(2,1)S(1)} custom-call(s16[32,48,320]{2,1,0:T(8,128)(2,1)S(1)} %all_to_all.22.blocks), custom_call_target="tpu_custom_call" | custom-call | tf_op jit(solution)/shard_map/pallas_call | solution.py:32
  90.7 24.9 %all_to_all.23 = s16[64,24,128]{2,1,0:T(8,128)(2,1)S(1)} all-to-all(s16[64,24,128]{2,1,0:T(8,128)(2,1)S(1)} %bitcast.12), channel_id=1, replica_groups=mesh['y'=8,'x'=4,'zl'=2,'zh'=4,'core'=2] {'y','zl','zh'}, dimensions={0} | all-to-all | bytes 786432 | tf_op jit(solution)/shard_map/all_to_all | solution.py:493
  115.7 1.4 %shard_map.154 = (f32[1,1]{1,0:T(1,128)}, f32[40,45]{1,0:T(8,128)}, f32[320]{0:T(512)}, f32[320]{0:T(512)}) custom-call(s16[8,8,24,128]{3,2,1,0:T(8,128)(2,1)S(1)} %bitcast.11), custom_call_target="tpu_custom_call" | custom-call | tf_op jit(solution)/shard_map/pallas_call | solution.py:32
Async XLA Ops:
  1.3 0.9 copy-start
  2.2 0.9 copy-start.1
  3.1 1.0 copy-start.2
  5.8 8.4 %collective-permute-start = (bf16[2,16,320]{2,1,0:T(8,128)(2,1)S(1)}, bf16[2,16,320]{2,1,0:T(8,128)(2,1)S(1)}, u32[]{:S(2)}, u32[]{:S(2)}) collective-permute-start(bf16[2,16,320]{2,1,0:T(8,128)(2,1)S(1)} %get-tuple-element.17), channel_id=1, source_target_pairs={{0,8},{8,16},{16,24},{24,32},{32,40},{40,48},{48,56},{56,0},{1,9},... | collective-permute-start | bytes 61448 | tf_op jit(solution)/shard_map/ppermute | solution.py:451
  10.1 5.7 %collective-permute-start.1 = (bf16[2,16,320]{2,1,0:T(8,128)(2,1)S(1)}, bf16[2,16,320]{2,1,0:T(8,128)(2,1)S(1)}, u32[]{:S(2)}, u32[]{:S(2)}) collective-permute-start(bf16[2,16,320]{2,1,0:T(8,128)(2,1)S(1)} %get-tuple-element.18), channel_id=1, source_target_pairs={{8,0},{16,8},{24,16},{32,24},{40,32},{48,40},{56,48},{0,56},{9,1},... | collective-permute-start | bytes 61448 | tf_op jit(solution)/shard_map/ppermute | solution.py:452
  15.8 10.2 %collective-permute-start.2 = (bf16[2,16,320]{2,1,0:T(8,128)(2,1)S(1)}, bf16[2,16,320]{2,1,0:T(8,128)(2,1)S(1)}, u32[]{:S(2)}, u32[]{:S(2)}) collective-permute-start(bf16[2,16,320]{2,1,0:T(8,128)(2,1)S(1)} %shard_map.148), channel_id=1, source_target_pairs={{0,7},{1,2},{2,1},{3,4},{4,3},{5,6},{6,5},{7,0},{8,15},{9,10},{10,... | collective-permute-start | bytes 61448 | tf_op jit(solution)/shard_map/ppermute | solution.py:454
  26.0 0.9 copy-start.3
  26.9 0.9 copy-start.4
  28.1 22.2 %collective-permute-start.3 = (bf16[2,19,16,320]{3,2,1,0:T(8,128)(2,1)S(1)}, bf16[2,19,16,320]{3,2,1,0:T(8,128)(2,1)S(1)}, u32[]{:S(2)}, u32[]{:S(2)}) collective-permute-start(bf16[2,19,16,320]{3,2,1,0:T(8,128)(2,1)S(1)} %shard_map.149.mine), channel_id=1, source_target_pairs={{0,1},{1,0},{2,3},{3,2},{4,5},{5,4},{6,7},{7,6},{8,9},{9,8},{10,11... | collective-permute-start | bytes 1167368 | tf_op jit(solution)/shard_map/ppermute | solution.py:459
  50.3 1.6 %copy-start.5 = (bf16[9,320,320]{2,1,0:T(8,128)(2,1)S(1)}, bf16[9,320,320]{2,1,0:T(8,128)(2,1)}, u32[]{:S(2)}) copy-start(bf16[9,320,320]{2,1,0:T(8,128)(2,1)} %weight_far.1) | copy-start | bytes 5529604
  51.9 1.6 %copy-start.6 = (bf16[9,320,320]{2,1,0:T(8,128)(2,1)S(1)}, bf16[9,320,320]{2,1,0:T(8,128)(2,1)}, u32[]{:S(2)}) copy-start(bf16[9,320,320]{2,1,0:T(8,128)(2,1)} %ref_far.1) | copy-start | bytes 5529604
  53.5 0.7 copy-start.7
  54.2 0.7 copy-start.8
  54.9 0.7 copy-start.9
  55.6 0.7 copy-start.10
  63.1 3.9 %collective-permute-start.4 = (f32[8,320]{1,0:T(8,128)S(1)}, f32[8,320]{1,0:T(8,128)S(1)}, u32[]{:S(2)}, u32[]{:S(2)}) collective-permute-start(f32[8,320]{1,0:T(8,128)S(1)} %get-tuple-element.21.small), channel_id=1, source_target_pairs={{0,1},{1,0},{2,3},{3,2},{4,5},{5,4},{6,7},{7,6},{8,9},{9,8},{10,11... | collective-permute-start | bytes 30728 | tf_op jit(solution)/shard_map/ppermute | solution.py:479

commit v3 on v2

--- a/solution.py
+++ b/solution.py
@@ -14,6 +14,7 @@
 TAPS = 9
 TH, TW = 8, 16
 PIX = TH * TW
+WIDE = 2 * C
 BLK = 45
 PIXELS = 64 * 128
 BETA = 40.0
@@ -21,13 +22,12 @@
 BF16 = jnp.bfloat16
 I16 = jnp.int16
 HIGHEST = lax.Precision.HIGHEST
-VMEM_LIMIT = 28 * 1024 * 1024
-
-
-def call(kernel, outs, scratch=(), flops=0, nbytes=0, far=()):
+
+
+def call(kernel, outs, scratch=(), flops=0, nbytes=0, far=(), grant=28):
     def run(*args):
         specs = [
-            pl.BlockSpec(memory_space=pl.ANY if i in far else pltpu.VMEM) for i in range(len(args))
+            pl.BlockSpec(memory_space=pltpu.HBM if i in far else pltpu.VMEM) for i in range(len(args))
         ]
         return pl.pallas_call(
             kernel,
@@ -35,7 +35,7 @@
             in_specs=specs,
             out_specs=[pl.BlockSpec(memory_space=pltpu.VMEM) for _ in outs],
             scratch_shapes=list(scratch),
-            compiler_params=pltpu.CompilerParams(vmem_limit_bytes=VMEM_LIMIT),
+            compiler_params=pltpu.CompilerParams(vmem_limit_bytes=grant * 2**20),
             cost_estimate=pl.CostEstimate(flops=flops, bytes_accessed=nbytes, transcendentals=0),
         )(*args)
 
@@ -68,32 +68,40 @@
     return high, low, exps.astype(F32)
 
 
+def side_by_side(one, two):
+    return jnp.concatenate([one[:, 0:256], two[:, 0:256], one[:, 256:C], two[:, 256:C]], axis=1)
+
+
+def apart(both):
+    one = jnp.concatenate([both[:, 0:256], both[:, 512:576]], axis=1)
+    two = jnp.concatenate([both[:, 256:512], both[:, 576:640]], axis=1)
+    return one, two
+
+
 def write_extras(extra, small):
     high, low, exps = split_small(small)
     extra[...] = jnp.zeros_like(extra)
-    for k in range(3):
-        extra[k, 0:1, :] = high[k : k + 1]
-        extra[k, 1:2, :] = low[k : k + 1]
-    extra[3, 0:1, :] = exps[0:1]
-    extra[3, 1:2, :] = exps[1:2]
-    extra[4, 0:1, :] = exps[2:3]
-
-
-def read_extras(blocks, base):
-    tails = [blocks[base + k].astype(jnp.int32)[40:48] for k in range(5)]
-    exps = [tails[3][6:7], tails[3][7:8], tails[4][6:7]]
-    rows = []
-    for k in range(3):
-        high = tails[k][6:7].astype(F32)
-        low = tails[k][7:8].astype(F32)
-        rows.append((high + low * (1.0 / 32768.0)) * pow2(exps[k] - 15))
-    return jnp.concatenate(rows + [jnp.zeros((5, C), F32)], axis=0)
-
-
-def packed_block(block, extra):
-    exps = exponent(jnp.max(jnp.abs(block), axis=0, keepdims=True))
-    q = rounded(block, exps)
-    row = lax.broadcasted_iota(jnp.int32, (8, C), 0)
+    extra[0, 0:1] = high[0:1]
+    extra[0, 1:2] = low[0:1]
+    extra[1, 0:1] = exps[0:1]
+    extra[1, 1:2] = high[1:2]
+    extra[2, 0:1] = low[1:2]
+    extra[2, 1:2] = exps[1:2]
+
+
+def read_extras(tails):
+    rows = [tails[0][6:7], tails[0][7:8], tails[1][6:7], tails[1][7:8], tails[2][6:7], tails[2][7:8]]
+    out = []
+    for high, low, exps in (rows[0:3], rows[3:6]):
+        value = high.astype(F32) + low.astype(F32) * (1.0 / 32768.0)
+        out.append(value * pow2(exps - 15))
+    return jnp.concatenate(out + [jnp.zeros((6, WIDE), F32)], axis=0)
+
+
+def packed_pair(pair, extra):
+    exps = exponent(jnp.max(jnp.abs(pair), axis=0, keepdims=True))
+    q = rounded(pair, exps)
+    row = lax.broadcasted_iota(jnp.int32, (8, WIDE), 0)
     tail = jnp.where(row == 5, exps.astype(F32), q[40:48])
     tail = jnp.where(row == 6, extra[0:1], tail)
     tail = jnp.where(row == 7, extra[1:2], tail)
@@ -101,21 +109,26 @@
     return q.astype(jnp.int32).astype(I16)
 
 
-def unpacked_block(block):
-    q = block.astype(jnp.int32)
+def unpacked_pair(q):
     v = q.astype(F32) * pow2(q[45:46] - 15)
-    row = lax.broadcasted_iota(jnp.int32, (8, C), 0)
+    row = lax.broadcasted_iota(jnp.int32, (8, WIDE), 0)
     return jnp.concatenate([v[0:40], jnp.where(row < BLK - 40, v[40:48], 0.0)], axis=0)
 
 
+def tiles_of(pair):
+    return [4 * pair, 4 * pair + 1, 4 * pair + 2, 4 * pair + 3, 16 + pair]
+
+
 def stats_and_time(
-    step, fw, fl, time_weight, stats, bias, first, last, here, table, number, sems
+    step, fw, fl, nw, nl, time_weight, stats, bias, first, last, here, table, number, sems
 ):
     copies = [
-        pltpu.make_async_copy(fw, here.at[0], sems.at[0]),
-        pltpu.make_async_copy(fl, here.at[1], sems.at[1]),
+        pltpu.make_async_copy(fw, here.at[0, pl.ds(0, TH)], sems.at[0]),
+        pltpu.make_async_copy(fl, here.at[1, pl.ds(0, TH)], sems.at[1]),
         pltpu.make_async_copy(step, number, sems.at[2]),
         pltpu.make_async_copy(time_weight, table, sems.at[3]),
+        pltpu.make_async_copy(nw, here.at[0, pl.ds(TH, TH)], sems.at[4]),
+        pltpu.make_async_copy(nl, here.at[1, pl.ds(TH, TH)], sems.at[5]),
     ]
     for copy in copies:
         copy.start()
@@ -128,7 +141,7 @@
     for k in range(2):
         first[k] = here[k, 0]
         last[k] = here[k, TH - 1]
-        x = here[k].astype(F32).reshape(PIX, C)
+        x = here[k, 0:TH].astype(F32).reshape(PIX, C)
         sums = jnp.sum(x, axis=0, keepdims=True)
         squares = jnp.sum(x * x, axis=0, keepdims=True)
         for j, part in enumerate((sums, squares)):
@@ -152,50 +165,35 @@
     gate = sinusoid * jax.nn.sigmoid(sinusoid)
     copies[3].wait()
     bias[...] = jnp.dot(gate, table[...], precision=HIGHEST, preferred_element_type=F32)
-
-
-def edge_column(top, bottom, fw, fl, side):
+    copies[4].wait()
+    copies[5].wait()
+
+
+def outer_column_and_tile(top, bottom, here, side, tile):
     core = lax.axis_index("core")
-    for s, ref in enumerate((fw, fl)):
-        x = ref[...].astype(F32)
-        above = top[s].astype(F32)
-        below = bottom[s].astype(F32)
+    for s in range(2):
+        tile[s, 0] = top[s]
+        tile[s, 1 : TH + 1] = here[s, 0:TH]
+        tile[s, TH + 1] = bottom[s]
+        tile[s, TH + 2 :] = here[s, TH:]
+        x = [tile[s, r].astype(F32) for r in range(TH + 2)]
         column = [
-            jnp.concatenate(
-                [above[col : col + 1]]
-                + [x[r, col : col + 1] for r in range(TH)]
-                + [below[col : col + 1], jnp.zeros((6, C), F32)],
-                axis=0,
-            )
+            jnp.concatenate([v[col : col + 1] for v in x] + [jnp.zeros((6, C), F32)], axis=0)
             for col in (0, TW - 1)
         ]
         side[s] = jnp.where(core == 0, column[0], column[1]).astype(BF16)
 
 
-def tile_payload(top, bottom, side, fw, fl, nw, nl, out, sems):
-    copies = [
-        pltpu.make_async_copy(nw, out.at[0, pl.ds(11, TH)], sems.at[0]),
-        pltpu.make_async_copy(nl, out.at[1, pl.ds(11, TH)], sems.at[1]),
+def forward(
+    stats, bias, mine, theirs, my_side, their_side, gain_far, shift_far, ref_gain_far, ref_shift_far,
+    weight_far, ref_far, cols, cot_out, small, field, act, back, weight, ref_weight, gain, shift,
+    ref_gain, ref_shift, sems,
+):
+    pairs = [
+        (ref_gain_far, ref_gain), (ref_shift_far, ref_shift), (gain_far, gain), (shift_far, shift),
+        (ref_far, ref_weight), (weight_far, weight),
     ]
-    for copy in copies:
-        copy.start()
-    for s, ref in enumerate((fw, fl)):
-        out[s, 0] = top[s]
-        out[s, 1 : TH + 1] = ref[...]
-        out[s, TH + 1] = bottom[s]
-        out[s, TH + 2] = side[s]
-    for copy in copies:
-        copy.wait()
-
-
-def forward(
-    stats, bias, gain, shift, ref_gain, ref_shift, mine, theirs, weight_far, ref_far,
-    cols, cot_out, small, field, act, back, weight, ref_weight, sems,
-):
-    copies = [
-        pltpu.make_async_copy(ref_far, ref_weight, sems.at[0]),
-        pltpu.make_async_copy(weight_far, weight, sems.at[1]),
-    ]
+    copies = [pltpu.make_async_copy(a, b, sems.at[i]) for i, (a, b) in enumerate(pairs)]
     for copy in copies:
         copy.start()
     core = lax.axis_index("core")
@@ -223,13 +221,14 @@
         scales.append(lax.rsqrt(square - mean * mean + 1e-05))
 
     tiles = (mine, theirs)
+    sides = (my_side, their_side)
     for w in range(2):
         for s in range(2):
             here, beside = tiles[w], tiles[1 - w]
             f = 2 * w + s
             field[f, :, TW + 2 :, :] = jnp.zeros((TH + 2, 22 - TW, C), F32)
             field[f, :, 1 : TW + 1, :] = here[s, 0 : TH + 2].astype(F32)
-            outer = here[s, TH + 2].astype(F32)
+            outer = sides[w][s].astype(F32)
             is_left = core == w
             for r in range(TH + 2):
                 near = beside[s, r].astype(F32)
@@ -266,7 +265,7 @@
 
     def base(f):
         tile, s = tiles[f // 2], f % 2
-        noise = tile[s, TH + 3 : 2 * TH + 3].astype(F32)
+        noise = tile[s, TH + 2 : 2 * TH + 2].astype(F32)
         return (tile[s, 1 : TH + 1].astype(F32) - noise).reshape(PIX, C)
 
     def residual(fields, kernel):
@@ -281,13 +280,15 @@
         return jnp.sum(resid[0] * resid[0] - resid[1] * resid[1], axis=0, keepdims=True)
 
     time_row = bias[0:1]
+    for copy in copies[0:4]:
+        copy.wait()
     columns_of((0, 1), ref_gain[...].reshape(1, C), ref_shift[...].reshape(1, C) + time_row)
-    copies[0].wait()
+    copies[4].wait()
     resid = residual((0, 1), ref_weight)
     margin = -signed_squares(resid)
     g, b = gain[...].reshape(1, C), shift[...].reshape(1, C) + time_row
     columns_of((0, 1, 2, 3), g, b)
-    copies[1].wait()
+    copies[5].wait()
     resid = residual((0, 1, 2, 3), weight)
     margin = margin + signed_squares(resid)
     for f in range(4):
@@ -312,14 +313,11 @@
             dpre = jnp.where(valid(0, r), back[s, r] * slope, 0.0)
             gains = gains + dpre * normed
             shifts = shifts + dpre
+    gains = jnp.sum(gains, axis=0, keepdims=True)
+    shifts = jnp.sum(shifts, axis=0, keepdims=True)
+    margin = jnp.broadcast_to(jnp.sum(margin, axis=1, keepdims=True), (1, WIDE))
     small[...] = jnp.concatenate(
-        [
-            jnp.sum(gains, axis=0, keepdims=True),
-            jnp.sum(shifts, axis=0, keepdims=True),
-            jnp.broadcast_to(jnp.sum(margin, axis=1, keepdims=True), (1, C)),
-            jnp.zeros((5, C), F32),
-        ],
-        axis=0,
+        [side_by_side(gains, shifts), margin, jnp.zeros((6, WIDE), F32)], axis=0
     )
 
 
@@ -340,51 +338,59 @@
 def pack_blocks(blocks, small, other, out, extra):
     write_extras(extra, small[...] + other[...])
 
-    def body(i, carry):
-        for k in range(4):
-            q = 4 * i + k
-            out[q] = packed_block(blocks[q], extra[lax.rem(q, 8)])
+    def body(dest, carry):
+        for pair in range(4):
+            q = 8 * dest + 2 * pair
+            packed = packed_pair(side_by_side(blocks[q], blocks[q + 1]), extra[pair])
+            for k, tile in enumerate(tiles_of(pair)):
+                out[dest, tile] = packed[:, 128 * k : 128 * k + 128]
         return carry
 
-    lax.fori_loop(0, 8, body, 0)
+    lax.fori_loop(0, 4, body, 0)
 
 
 def chip_sum(blocks, out):
-    small = read_extras(blocks, 0)
-    for source in range(1, 4):
-        small = small + read_extras(blocks, 8 * source)
-    high, low, exps = split_small(small)
+    def pair_of(source, pair, rows):
+        parts = [blocks[source, tile].astype(jnp.int32)[rows] for tile in tiles_of(pair)]
+        return jnp.concatenate(parts, axis=1)
+
+    tail_rows = slice(40, 48)
+    small = jnp.zeros((8, WIDE), F32)
+    for source in range(4):
+        small = small + read_extras([pair_of(source, k, tail_rows) for k in range(3)])
+    high, low, exps = split_small(small[:, 0:128])
     lane = lax.broadcasted_iota(jnp.int32, (1, 128), 1)
     tail = jnp.zeros((1, 128), F32)
     vectors = []
-    for k in range(2):
-        e = exponent(jnp.max(jnp.abs(small[k : k + 1]), axis=1, keepdims=True))
-        q = rounded(small[k : k + 1], e)
+    for k, vector in enumerate(apart(small[0:1])):
+        e = exponent(jnp.max(jnp.abs(vector), axis=1, keepdims=True))
+        q = rounded(vector, e)
         q = jnp.concatenate([q, jnp.zeros((1, 64), F32)], axis=1)
         vectors += [q[:, 0:128], q[:, 128:256], q[:, 256:384]]
         tail = jnp.where(lane == k, e.astype(F32), tail)
     for k, part in enumerate((high, low, exps)):
-        tail = jnp.where(lane == 2 + k, part[2:3, 0:128], tail)
-
-    def body(z, carry):
-        block = unpacked_block(blocks[z])
-        for source in range(1, 4):
-            block = block + unpacked_block(blocks[8 * source + z])
-        e = exponent(jnp.max(jnp.abs(block), axis=0, keepdims=True))
-        q = rounded(block, e)
-        e = e.astype(F32)
-        for y in range(8):
-            part = q[:, 40 * y : 40 * y + 40]
-            tile = jnp.concatenate(
-                [part[0:16], part[16:32], part[32:48], jnp.zeros((16, 8), F32)], axis=1
-            )
-            ey = e[:, 40 * y : 40 * y + 40]
-            ey = jnp.concatenate([ey, ey, ey, jnp.zeros((1, 8), F32)], axis=1)
-            full = jnp.concatenate([tile] + vectors + [ey, tail], axis=0)
-            out[y, z] = full.astype(jnp.int32).astype(I16)
+        tail = jnp.where(lane == 2 + k, part[1:2], tail)
+
+    def body(pair, carry):
+        both = jnp.zeros((48, WIDE), F32)
+        for source in range(4):
+            both = both + unpacked_pair(pair_of(source, pair, slice(0, 48)))
+        e = exponent(jnp.max(jnp.abs(both), axis=0, keepdims=True))
+        values = apart(rounded(both, e))
+        levels = apart(e.astype(F32))
+        for k in range(2):
+            for y in range(8):
+                part = values[k][:, 40 * y : 40 * y + 40]
+                tile = jnp.concatenate(
+                    [part[0:16], part[16:32], part[32:48], jnp.zeros((16, 8), F32)], axis=1
+                )
+                ey = levels[k][:, 40 * y : 40 * y + 40]
+                ey = jnp.concatenate([ey, ey, ey, jnp.zeros((1, 8), F32)], axis=1)
+                full = jnp.concatenate([tile] + vectors + [ey, tail], axis=0)
+                out[y, 2 * pair + k] = full.astype(jnp.int32).astype(I16)
         return carry
 
-    lax.fori_loop(0, 8, body, 0)
+    lax.fori_loop(0, 4, body, 0)
 
 
 def final_sum(blocks, loss, grad, gain, shift):
@@ -432,49 +438,55 @@
     up = [((i + 1) % 8, i) for i in range(8)]
     down = [(i, (i + 1) % 8) for i in range(8)]
     outward = [(i, (i + 1) % 8 if i % 2 else (i + 7) % 8) for i in range(8)]
+    beyond = [(i, (i + 2) % 8 if i % 2 else (i + 6) % 8) for i in range(8)]
     swap = [(0, 1), (1, 0)]
 
-    stats, bias, first, last = call(
+    stats, bias, first, last, here = call(
         stats_and_time,
-        [((64, 128), F32), ((8, C), F32), (strip, BF16), (strip, BF16)],
+        [((64, 128), F32), ((8, C), F32), (strip, BF16), (strip, BF16)]
+        + [((2, 2 * TH, TW, C), BF16)],
         [
-            pltpu.VMEM((2, TH, TW, C), BF16),
             pltpu.VMEM((C, C), F32),
             pltpu.SMEM((1,), jnp.int32),
-            pltpu.SemaphoreType.DMA((4,)),
+            pltpu.SemaphoreType.DMA((6,)),
         ],
         flops=10**7,
         nbytes=10**6,
-        far=(0, 1, 2, 3),
-    )(timesteps, fw, fl, time_weight)
-    stats = lax.all_to_all(stats, ("x", "zl", "zh", "core"), 0, 0, tiled=True)
+        far=range(6),
+        grant=57,
+    )(timesteps, fw, fl, noise_win[0], noise_lose[0], time_weight)
     top = lax.ppermute(last, rows, down)
     bottom = lax.ppermute(first, rows, up)
-    (side,) = call(edge_column, [(strip, BF16)])(top, bottom, fw, fl)
-    side = lax.ppermute(side, columns, outward)
-    payload = (2, 2 * TH + 3, TW, C)
-    (mine,) = call(
-        tile_payload, [(payload, BF16)], [pltpu.SemaphoreType.DMA((2,))], far=(5, 6)
-    )(top, bottom, side, fw, fl, noise_win[0], noise_lose[0])
+    side, mine = call(
+        outer_column_and_tile,
+        [(strip, BF16), ((2, 2 * TH + 2, TW, C), BF16)],
+        flops=10**10,
+        nbytes=10**6,
+    )(top, bottom, here)
+    stats, side, mine = lax.optimization_barrier((stats, side, mine))
+    stats = lax.all_to_all(stats, ("x", "zl", "zh", "core"), 0, 0, tiled=True)
+    my_side = lax.ppermute(side, columns, outward)
+    their_side = lax.ppermute(side, columns, beyond)
     theirs = lax.ppermute(mine, "core", swap)
 
     cols, cot, small = call(
         forward,
-        [((4 * PIX, TAPS * C), BF16), ((4 * PIX, C), BF16), ((8, C), F32)],
+        [((4 * PIX, TAPS * C), BF16), ((4 * PIX, C), BF16), ((8, WIDE), F32)],
         [
             pltpu.VMEM((4, TH + 2, 24, C), F32),
             pltpu.VMEM((TH + 2, 24, C), F32),
             pltpu.VMEM((2, TH + 2, 24, C), F32),
             pltpu.VMEM((TAPS, C, C), BF16),
             pltpu.VMEM((TAPS, C, C), BF16),
-            pltpu.SemaphoreType.DMA((2,)),
-        ],
+        ]
+        + [pltpu.VMEM((C,), F32)] * 4
+        + [pltpu.SemaphoreType.DMA((6,))],
         flops=2 * 10**9,
         nbytes=10**7,
-        far=(8, 9),
+        far=range(6, 12),
     )(
-        stats, bias, norm_gain, norm_shift, ref_gain, ref_shift, mine, theirs, conv_weight,
-        ref_weight,
+        stats, bias, mine, theirs, my_side, their_side, norm_gain, norm_shift, ref_gain, ref_shift,
+        conv_weight, ref_weight,
     )
     other = lax.ppermute(small, "core", swap)
     block = (32, 48, C)
@@ -485,9 +497,9 @@
         flops=10**9,
         nbytes=10**7,
     )(cols, cot)
-    (blocks,) = call(pack_blocks, [(block, I16)], [pltpu.VMEM((8, 8, C), F32)])(
-        blocks, small, other
-    )
+    (blocks,) = call(
+        pack_blocks, [((4, 20, 48, 128), I16)], [pltpu.VMEM((4, 8, WIDE), F32)]
+    )(blocks, small, other)
     blocks = lax.all_to_all(blocks, "x", 0, 0, tiled=True)
     (sums,) = call(chip_sum, [((8, 8, 24, 128), I16)])(blocks)
     sums = lax.all_to_all(sums.reshape(64, 24, 128), ("y", "zl", "zh"), 0, 0, tiled=True)

time: 118 us -> 108 us (0.915)
  blocking collectives: 65.1 us -> 46 us
  starting transfers between devices: 20.9 us -> 33.7 us
  local copies, waits for them, and re-layouts: 10.6 us -> 2.64 us
  waiting for transfers between devices: 3.09 us -> 7.13 us
    all_to_all x1 -> x0, blocking collectives: 20.2 us -> none  [local(): stats = lax.all_to_all(stats, ('x', 'zl', 'zh', 'core'), 0, 0, tiled=True)]
    all_to_all x0 -> x1, starting transfers between devices: none -> 13.8 us  [local(): stats = lax.all_to_all(stats, ('x', 'zl', 'zh', 'core'), 0, 0, tiled=True)]
    unnamed x22 -> x16, local copies, waits for them, and re-layouts: 10.6 us -> 2.64 us
    ppermute x1 -> x2, waiting for transfers between devices: 1.5 us -> 5.32 us  [the longest x1 5.32 us: local(): my_side = lax.ppermute(side, columns, outward)]
    all_to_all x1, blocking collectives: 24.9 us -> 26.8 us  [local(): lax.all_to_all(sums.reshape(64, 24, 128), ('y', 'zl', 'zh'), 0, 0, tiled=...]
    ppermute x1 -> x2, starting transfers between devices: 8.7 us -> 7.51 us  [the longest x1 5.59 us: local(): their_side = lax.ppermute(side, columns, beyond)]
    pallas_call x8 -> x7, Pallas kernels: 16 us -> 16.1 us  [run(): pl.pallas_call(kernel, out_shape=[jax.ShapeDtypeStruct(s, d) for s, d in...]
  transfers between devices with their start and end apart: 5 -> 7, of which waited for: 2 -> 3; matrix products, arithmetic and copies ran while one was open for 0% -> 0% of each run, Pallas kernels for 2% -> 2%
where the time goes in v3:
time: 108 us; the launch traced here: 107 us
  blocking collectives  46 us (43%)
  starting transfers between devices  33.7 us (31%)
  Pallas kernels  16.1 us (15%)
  waiting for transfers between devices  7.13 us (7%)
  local copies, waits for them, and re-layouts  2.64 us (2%)
  between operations  1.47 us (1%)
    all_to_all x1, blocking collectives, local(): lax.all_to_all(sums.reshape(64, 24, 128), ('y', 'zl', 'zh'), 0, 0, tiled=...  26.8 us
    all_to_all x1, blocking collectives, local(): blocks = lax.all_to_all(blocks, 'x', 0, 0, tiled=True)  19.3 us
    pallas_call x7, Pallas kernels, run(): pl.pallas_call(kernel, out_shape=[jax.ShapeDtypeStruct(s, d) for s, d in...  16.1 us
    all_to_all x1, starting transfers between devices, local(): stats = lax.all_to_all(stats, ('x', 'zl', 'zh', 'core'), 0, 0, tiled=True)  13.8 us
    ppermute x1, starting transfers between devices, local(): their_side = lax.ppermute(side, columns, beyond)  5.59 us
    ppermute x1, waiting for transfers between devices, local(): my_side = lax.ppermute(side, columns, outward)  5.32 us
    ppermute x1, starting transfers between devices, local(): top = lax.ppermute(last, rows, down)  4.28 us
    ppermute x1, starting transfers between devices, local(): bottom = lax.ppermute(first, rows, up)  4.11 us
  transfers between devices with their start and end apart: 7, of which 3 were waited for; matrix products, arithmetic and copies ran while one was open for 0% of the time, Pallas kernels for 2%

profile of v3, /device:TPU:8, one launch (start us, length us, event | category | flops | bytes accessed | tf_op | source)
XLA Modules:
  0.0 107.1 jit_solution(9833613019824797244)
XLA Ops:
  1.3 2.9 %shard_map.147 = (f32[64,128]{1,0:T(8,128)}, f32[8,320]{1,0:T(8,128)}, bf16[2,16,320]{2,1,0:T(8,128)(2,1)}, bf16[2,16,320]{2,1,0:T(8,128)(2,1)}, bf16[2,16,16,320]{3,2,1,0:T(8,128)(2,1)}) custom-call(s32[1]{0:T(128)S(6)} %copy.17.step, bf16[8,16,320]{2,1,0:T(8,128)(2,1)} %bitcast.14, bf16[8,16,320]{2,1,0:T(8,128)(2,1)} %bitcast.15, ...), custom_call_target="tpu_custom_call" | custom-call | flops 10000000 | bytes 1000000 | tf_op jit(solution)/shard_map/pallas_call | solution.py:32
  4.2 4.3 %collective-permute-start = (bf16[2,16,320]{2,1,0:T(8,128)(2,1)}, bf16[2,16,320]{2,1,0:T(8,128)(2,1)S(1)}, u32[]{:S(2)}, u32[]{:S(2)}) collective-permute-start(bf16[2,16,320]{2,1,0:T(8,128)(2,1)} %get-tuple-element.22), channel_id=1, source_target_pairs={{0,8},{8,16},{16,24},{24,32},{32,40},{40,48},{48,56},{56,0},{1,9},... | collective-permute-start | bytes 61448 | tf_op jit(solution)/shard_map/ppermute | solution.py:458
  8.4 4.1 %collective-permute-start.1 = (bf16[2,16,320]{2,1,0:T(8,128)(2,1)}, bf16[2,16,320]{2,1,0:T(8,128)(2,1)S(1)}, u32[]{:S(2)}, u32[]{:S(2)}) collective-permute-start(bf16[2,16,320]{2,1,0:T(8,128)(2,1)} %get-tuple-element.23), channel_id=1, source_target_pairs={{8,0},{16,8},{24,16},{32,24},{40,32},{48,40},{56,48},{0,56},{9,1},... | collective-permute-start | bytes 61448 | tf_op jit(solution)/shard_map/ppermute | solution.py:459
  12.6 0.1 collective-permute-done.top
  12.6 1.7 %collective-permute-done.1.bottom = bf16[2,16,320]{2,1,0:T(8,128)(2,1)S(1)} collective-permute-done((bf16[2,16,320]{2,1,0:T(8,128)(2,1)}, bf16[2,16,320]{2,1,0:T(8,128)(2,1)S(1)}, u32[]{:S(2)}, u32[]{:S(2)}) %collective-permute-start.1) | collective-permute-done | bytes 20512 | tf_op jit(solution)/shard_map/ppermute | solution.py:459
  14.4 0.0 copy-start.2
  14.4 1.0 copy-done.2
  15.4 0.0 copy-start
  15.4 0.0 copy-start.3
  15.4 0.0 copy-start.4
  15.4 0.0 copy-start.5
  15.4 0.0 copy-start.6
  15.4 0.0 copy-start.7
  15.4 0.1 shard_map.148
  15.5 2.1 %collective-permute-start.2 = (bf16[2,18,16,320]{3,2,1,0:T(8,128)(2,1)S(1)}, bf16[2,18,16,320]{3,2,1,0:T(8,128)(2,1)S(1)}, u32[]{:S(2)}, u32[]{:S(2)}) collective-permute-start(bf16[2,18,16,320]{3,2,1,0:T(8,128)(2,1)S(1)} %get-tuple-element.29.mine), channel_id=1, source_target_pairs={{0,1},{1,0},{2,3},{3,2},{4,5},{5,4},{6,7},{7,6},{8,9},{9,8},{10,11... | collective-permute-start | bytes 1105928 | tf_op jit(solution)/shard_map/ppermute | solution.py:470
  17.5 13.8 %all-to-all-start = ((f32[64,1,128]{2,1,0:T(1,128)}), f32[64,1,128]{2,1,0:T(1,128)S(1)}, u32[]{:S(2)}, u32[]{:S(2)}) async-start(f32[64,1,128]{2,1,0:T(1,128)} %bitcast.5), calls=%async_computation | async-start | bytes 65536 | tf_op jit(solution)/shard_map/all_to_all | solution.py:467
  31.4 5.6 %collective-permute-start.4 = (bf16[2,16,320]{2,1,0:T(8,128)(2,1)S(1)}, bf16[2,16,320]{2,1,0:T(8,128)(2,1)S(1)}, u32[]{:S(2)}, u32[]{:S(2)}) collective-permute-start(bf16[2,16,320]{2,1,0:T(8,128)(2,1)S(1)} %get-tuple-element.30), channel_id=1, source_target_pairs={{0,6},{1,3},{2,0},{3,5},{4,2},{5,7},{6,4},{7,1},{8,14},{9,11},{10,... | collective-permute-start | bytes 61448 | tf_op jit(solution)/shard_map/ppermute | solution.py:469
  37.0 1.9 %collective-permute-start.3 = (bf16[2,16,320]{2,1,0:T(8,128)(2,1)S(1)}, bf16[2,16,320]{2,1,0:T(8,128)(2,1)S(1)}, u32[]{:S(2)}, u32[]{:S(2)}) collective-permute-start(bf16[2,16,320]{2,1,0:T(8,128)(2,1)S(1)} %get-tuple-element.30), channel_id=1, source_target_pairs={{0,7},{1,2},{2,1},{3,4},{4,3},{5,6},{6,5},{7,0},{8,15},{9,10},{10,... | collective-permute-start | bytes 61448 | tf_op jit(solution)/shard_map/ppermute | solution.py:468
  38.9 0.0 collective-permute-done.4.their_side
  38.9 5.3 %collective-permute-done.3.my_side = bf16[2,16,320]{2,1,0:T(8,128)(2,1)S(1)} collective-permute-done((bf16[2,16,320]{2,1,0:T(8,128)(2,1)S(1)}, bf16[2,16,320]{2,1,0:T(8,128)(2,1)S(1)}, u32[]{:S(2)}, u32[]{:S(2)}) %collective-permute-start.3) | collective-permute-done | bytes 20512 | tf_op jit(solution)/shard_map/ppermute | solution.py:468
  44.2 0.0 all-to-all-done
  44.3 0.0 collective-permute-done.2.theirs
  44.3 0.0 copy-done
  44.3 0.0 copy-done.3
  44.3 0.0 copy-done.4
  44.3 0.0 copy-done.5
  44.3 0.0 copy-done.6
  44.3 0.0 copy-done.7
  44.3 0.0 copy-start.1
  44.3 1.6 %copy-done.1 = bf16[9,320,320]{2,1,0:T(8,128)(2,1)S(1)} copy-done((bf16[9,320,320]{2,1,0:T(8,128)(2,1)S(1)}, bf16[9,320,320]{2,1,0:T(8,128)(2,1)}, u32[]{:S(2)}) %copy-start.1) | copy-done | bytes 1843224
  45.9 6.9 %shard_map.149 = (bf16[512,2880]{1,0:T(8,128)(2,1)S(1)}, bf16[512,320]{1,0:T(8,128)(2,1)S(1)}, f32[8,640]{1,0:T(8,128)S(1)}) custom-call(f32[64,128]{1,0:T(8,128)S(1)} %bitcast.13, f32[8,320]{1,0:T(8,128)S(1)} %copy-done.3, bf16[2,18,16,320]{3,2,1,0:T(8,128)(2,1)S(1)} %get-tuple-element.29.mine, bf16[2,18,16,320]{3,2,1,0:T(8,128)(2,1)S(1)} %collective-permute-done.2.theirs, ...), custom_call_target="tpu_custom_call" | custom-call | flops 2000000000 | bytes 10000000 | tf_op jit(solution)/shard_map/pallas_call | solution.py:32
  52.9 1.9 %collective-permute-start.5 = (f32[8,640]{1,0:T(8,128)S(1)}, f32[8,640]{1,0:T(8,128)S(1)}, u32[]{:S(2)}, u32[]{:S(2)}) collective-permute-start(f32[8,640]{1,0:T(8,128)S(1)} %get-tuple-element.33.small), channel_id=1, source_target_pairs={{0,1},{1,0},{2,3},{3,2},{4,5},{5,4},{6,7},{7,6},{8,9},{9,8},{10,11... | collective-permute-start | bytes 61448 | tf_op jit(solution)/shard_map/ppermute | solution.py:491
  54.8 1.9 %shard_map.150.blocks = f32[32,48,320]{2,1,0:T(8,128)S(1)} custom-call(bf16[512,2880]{1,0:T(8,128)(2,1)S(1)} %get-tuple-element.31.cols, bf16[512,320]{1,0:T(8,128)(2,1)S(1)} %get-tuple-element.32.cot), custom_call_target="tpu_custom_call" | custom-call | flops 1000000000 | bytes 10000000 | tf_op jit(solution)/shard_map/pallas_call | solution.py:32
  56.7 0.0 collective-permute-done.5.other
  56.7 1.1 %shard_map.151 = s16[4,20,48,128]{3,2,1,0:T(8,128)(2,1)S(1)} custom-call(f32[32,48,320]{2,1,0:T(8,128)S(1)} %shard_map.150.blocks, f32[8,640]{1,0:T(8,128)S(1)} %get-tuple-element.33.small, f32[8,640]{1,0:T(8,128)S(1)} %collective-permute-done.5.other), custom_call_target="tpu_custom_call" | custom-call | tf_op jit(solution)/shard_map/pallas_call | solution.py:32
  57.8 19.3 %all_to_all.21.blocks = s16[4,20,48,128]{3,2,1,0:T(8,128)(2,1)S(1)} all-to-all(s16[4,20,48,128]{3,2,1,0:T(8,128)(2,1)S(1)} %shard_map.151), channel_id=1, replica_groups=mesh['y'=8,'x'=4,'zl'=2,'zh'=4,'core'=2] {'x'}, dimensions={0} | all-to-all | bytes 1966080 | tf_op jit(solution)/shard_map/all_to_all | solution.py:503
  77.1 1.8 %shard_map.152 = s16[8,8,24,128]{3,2,1,0:T(8,128)(2,1)S(1)} custom-call(s16[4,20,48,128]{3,2,1,0:T(8,128)(2,1)S(1)} %all_to_all.21.blocks), custom_call_target="tpu_custom_call" | custom-call | tf_op jit(solution)/shard_map/pallas_call | solution.py:32
  78.9 26.8 %all_to_all.22 = s16[64,24,128]{2,1,0:T(8,128)(2,1)S(1)} all-to-all(s16[64,24,128]{2,1,0:T(8,128)(2,1)S(1)} %bitcast.12), channel_id=1, replica_groups=mesh['y'=8,'x'=4,'zl'=2,'zh'=4,'core'=2] {'y','zl','zh'}, dimensions={0} | all-to-all | bytes 786432 | tf_op jit(solution)/shard_map/all_to_all | solution.py:505
  105.7 1.4 %shard_map.153 = (f32[1,1]{1,0:T(1,128)}, f32[40,45]{1,0:T(8,128)}, f32[320]{0:T(512)}, f32[320]{0:T(512)}) custom-call(s16[8,8,24,128]{3,2,1,0:T(8,128)(2,1)S(1)} %bitcast.11), custom_call_target="tpu_custom_call" | custom-call | tf_op jit(solution)/shard_map/pallas_call | solution.py:32
Async XLA Ops:
  4.2 8.5 %collective-permute-start = (bf16[2,16,320]{2,1,0:T(8,128)(2,1)}, bf16[2,16,320]{2,1,0:T(8,128)(2,1)S(1)}, u32[]{:S(2)}, u32[]{:S(2)}) collective-permute-start(bf16[2,16,320]{2,1,0:T(8,128)(2,1)} %get-tuple-element.22), channel_id=1, source_target_pairs={{0,8},{8,16},{16,24},{24,32},{32,40},{40,48},{48,56},{56,0},{1,9},... | collective-permute-start | bytes 61448 | tf_op jit(solution)/shard_map/ppermute | solution.py:458
  8.4 5.9 %collective-permute-start.1 = (bf16[2,16,320]{2,1,0:T(8,128)(2,1)}, bf16[2,16,320]{2,1,0:T(8,128)(2,1)S(1)}, u32[]{:S(2)}, u32[]{:S(2)}) collective-permute-start(bf16[2,16,320]{2,1,0:T(8,128)(2,1)} %get-tuple-element.23), channel_id=1, source_target_pairs={{8,0},{16,8},{24,16},{32,24},{40,32},{48,40},{56,48},{0,56},{9,1},... | collective-permute-start | bytes 61448 | tf_op jit(solution)/shard_map/ppermute | solution.py:459
  14.4 1.0 copy-start.2
  15.4 28.9 %copy-start = (bf16[9,320,320]{2,1,0:T(8,128)(2,1)S(1)}, bf16[9,320,320]{2,1,0:T(8,128)(2,1)}, u32[]{:S(2)}) copy-start(bf16[9,320,320]{2,1,0:T(8,128)(2,1)} %weight_far.1) | copy-start | bytes 5529604
  15.4 28.9 %copy-start.3 = (f32[8,320]{1,0:T(8,128)S(1)}, f32[8,320]{1,0:T(8,128)}, u32[]{:S(2)}) copy-start(f32[8,320]{1,0:T(8,128)} %get-tuple-element.28.bias) | copy-start | bytes 30724
  15.4 28.9 %copy-start.4 = (f32[320]{0:T(512)S(1)}, f32[320]{0:T(512)}, u32[]{:S(2)}) copy-start(f32[320]{0:T(512)} %gain_far.1) | copy-start | bytes 3844
  15.4 28.9 %copy-start.5 = (f32[320]{0:T(512)S(1)}, f32[320]{0:T(512)}, u32[]{:S(2)}) copy-start(f32[320]{0:T(512)} %shift_far.1) | copy-start | bytes 3844
  15.4 28.9 %copy-start.6 = (f32[320]{0:T(512)S(1)}, f32[320]{0:T(512)}, u32[]{:S(2)}) copy-start(f32[320]{0:T(512)} %ref_gain_far.1) | copy-start | bytes 3844
  15.4 28.9 %copy-start.7 = (f32[320]{0:T(512)S(1)}, f32[320]{0:T(512)}, u32[]{:S(2)}) copy-start(f32[320]{0:T(512)} %ref_shift_far.1) | copy-start | bytes 3844
  15.5 28.8 %collective-permute-start.2 = (bf16[2,18,16,320]{3,2,1,0:T(8,128)(2,1)S(1)}, bf16[2,18,16,320]{3,2,1,0:T(8,128)(2,1)S(1)}, u32[]{:S(2)}, u32[]{:S(2)}) collective-permute-start(bf16[2,18,16,320]{3,2,1,0:T(8,128)(2,1)S(1)} %get-tuple-element.29.mine), channel_id=1, source_target_pairs={{0,1},{1,0},{2,3},{3,2},{4,5},{5,4},{6,7},{7,6},{8,9},{9,8},{10,11... | collective-permute-start | bytes 1105928 | tf_op jit(solution)/shard_map/ppermute | solution.py:470
  17.5 26.7 %all-to-all-start = ((f32[64,1,128]{2,1,0:T(1,128)}), f32[64,1,128]{2,1,0:T(1,128)S(1)}, u32[]{:S(2)}, u32[]{:S(2)}) async-start(f32[64,1,128]{2,1,0:T(1,128)} %bitcast.5), calls=%async_computation | async-start | bytes 65536 | tf_op jit(solution)/shard_map/all_to_all | solution.py:467
  31.4 7.5 %collective-permute-start.4 = (bf16[2,16,320]{2,1,0:T(8,128)(2,1)S(1)}, bf16[2,16,320]{2,1,0:T(8,128)(2,1)S(1)}, u32[]{:S(2)}, u32[]{:S(2)}) collective-permute-start(bf16[2,16,320]{2,1,0:T(8,128)(2,1)S(1)} %get-tuple-element.30), channel_id=1, source_target_pairs={{0,6},{1,3},{2,0},{3,5},{4,2},{5,7},{6,4},{7,1},{8,14},{9,11},{10,... | collective-permute-start | bytes 61448 | tf_op jit(solution)/shard_map/ppermute | solution.py:469
  37.0 7.3 %collective-permute-start.3 = (bf16[2,16,320]{2,1,0:T(8,128)(2,1)S(1)}, bf16[2,16,320]{2,1,0:T(8,128)(2,1)S(1)}, u32[]{:S(2)}, u32[]{:S(2)}) collective-permute-start(bf16[2,16,320]{2,1,0:T(8,128)(2,1)S(1)} %get-tuple-element.30), channel_id=1, source_target_pairs={{0,7},{1,2},{2,1},{3,4},{4,3},{5,6},{6,5},{7,0},{8,15},{9,10},{10,... | collective-permute-start | bytes 61448 | tf_op jit(solution)/shard_map/ppermute | solution.py:468
  44.3 1.6 %copy-start.1 = (bf16[9,320,320]{2,1,0:T(8,128)(2,1)S(1)}, bf16[9,320,320]{2,1,0:T(8,128)(2,1)}, u32[]{:S(2)}) copy-start(bf16[9,320,320]{2,1,0:T(8,128)(2,1)} %ref_far.1) | copy-start | bytes 5529604
  52.9 3.8 %collective-permute-start.5 = (f32[8,640]{1,0:T(8,128)S(1)}, f32[8,640]{1,0:T(8,128)S(1)}, u32[]{:S(2)}, u32[]{:S(2)}) collective-permute-start(f32[8,640]{1,0:T(8,128)S(1)} %get-tuple-element.33.small), channel_id=1, source_target_pairs={{0,1},{1,0},{2,3},{3,2},{4,5},{5,4},{6,7},{7,6},{8,9},{9,8},{10,11... | collective-permute-start | bytes 61448 | tf_op jit(solution)/shard_map/ppermute | solution.py:491

commit v4 on v3

--- a/solution.py
+++ b/solution.py
@@ -24,7 +24,7 @@
 HIGHEST = lax.Precision.HIGHEST
 
 
-def call(kernel, outs, scratch=(), flops=0, nbytes=0, far=(), grant=28):
+def call(kernel, outs, scratch=(), flops=0, nbytes=0, far=(), far_outs=(), grant=28):
     def run(*args):
         specs = [
             pl.BlockSpec(memory_space=pltpu.HBM if i in far else pltpu.VMEM) for i in range(len(args))
@@ -33,7 +33,10 @@
             kernel,
             out_shape=[jax.ShapeDtypeStruct(s, d) for s, d in outs],
             in_specs=specs,
-            out_specs=[pl.BlockSpec(memory_space=pltpu.VMEM) for _ in outs],
+            out_specs=[
+                pl.BlockSpec(memory_space=pltpu.HBM if i in far_outs else pltpu.VMEM)
+                for i in range(len(outs))
+            ],
             scratch_shapes=list(scratch),
             compiler_params=pltpu.CompilerParams(vmem_limit_bytes=grant * 2**20),
             cost_estimate=pl.CostEstimate(flops=flops, bytes_accessed=nbytes, transcendentals=0),
@@ -78,33 +81,11 @@
     return one, two
 
 
-def write_extras(extra, small):
-    high, low, exps = split_small(small)
-    extra[...] = jnp.zeros_like(extra)
-    extra[0, 0:1] = high[0:1]
-    extra[0, 1:2] = low[0:1]
-    extra[1, 0:1] = exps[0:1]
-    extra[1, 1:2] = high[1:2]
-    extra[2, 0:1] = low[1:2]
-    extra[2, 1:2] = exps[1:2]
-
-
-def read_extras(tails):
-    rows = [tails[0][6:7], tails[0][7:8], tails[1][6:7], tails[1][7:8], tails[2][6:7], tails[2][7:8]]
-    out = []
-    for high, low, exps in (rows[0:3], rows[3:6]):
-        value = high.astype(F32) + low.astype(F32) * (1.0 / 32768.0)
-        out.append(value * pow2(exps - 15))
-    return jnp.concatenate(out + [jnp.zeros((6, WIDE), F32)], axis=0)
-
-
-def packed_pair(pair, extra):
+def packed_pair(pair):
     exps = exponent(jnp.max(jnp.abs(pair), axis=0, keepdims=True))
     q = rounded(pair, exps)
     row = lax.broadcasted_iota(jnp.int32, (8, WIDE), 0)
     tail = jnp.where(row == 5, exps.astype(F32), q[40:48])
-    tail = jnp.where(row == 6, extra[0:1], tail)
-    tail = jnp.where(row == 7, extra[1:2], tail)
     q = jnp.concatenate([q[0:40], tail], axis=0)
     return q.astype(jnp.int32).astype(I16)
 
@@ -119,8 +100,19 @@
     return [4 * pair, 4 * pair + 1, 4 * pair + 2, 4 * pair + 3, 16 + pair]
 
 
+def edge_rows(fw, fl, first, last, sems):
+    copies = []
+    for k, ref in enumerate((fw, fl)):
+        copies.append(pltpu.make_async_copy(ref.at[0], first.at[k], sems.at[2 * k]))
+        copies.append(pltpu.make_async_copy(ref.at[TH - 1], last.at[k], sems.at[2 * k + 1]))
+    for copy in copies:
+        copy.start()
+    for copy in copies:
+        copy.wait()
+
+
 def stats_and_time(
-    step, fw, fl, nw, nl, time_weight, stats, bias, first, last, here, table, number, sems
+    step, fw, fl, nw, nl, time_weight, stats, bias, here, table, number, sems
 ):
     copies = [
         pltpu.make_async_copy(fw, here.at[0, pl.ds(0, TH)], sems.at[0]),
@@ -139,8 +131,6 @@
     lanes = lax.broadcasted_iota(jnp.int32, (C, 128), 1)
     size = C // GROUPS
     for k in range(2):
-        first[k] = here[k, 0]
-        last[k] = here[k, TH - 1]
         x = here[k, 0:TH].astype(F32).reshape(PIX, C)
         sums = jnp.sum(x, axis=0, keepdims=True)
         squares = jnp.sum(x * x, axis=0, keepdims=True)
@@ -184,22 +174,55 @@
         side[s] = jnp.where(core == 0, column[0], column[1]).astype(BF16)
 
 
-def forward(
-    stats, bias, mine, theirs, my_side, their_side, gain_far, shift_far, ref_gain_far, ref_shift_far,
-    weight_far, ref_far, cols, cot_out, small, field, act, back, weight, ref_weight, gain, shift,
-    ref_gain, ref_shift, sems,
+def valid_pixels(core):
+    row_at = 2 * lax.axis_index("x") + lax.axis_index("zl")
+    col_at = 2 * lax.axis_index("zh") + core
+    column = lax.broadcasted_iota(jnp.int32, (24, C), 0)
+    inside = (column < TW + 2) & ((column > 0) | (col_at > 0))
+    inside = inside & ((column < TW + 1) | (col_at < 7))
+
+    def valid(r):
+        if r == 0:
+            return inside & (row_at > 0)
+        if r == TH + 1:
+            return inside & (row_at < 7)
+        return inside
+
+    return valid
+
+
+def activate(normed, f, valid, g, b, act):
+    for r in range(TH + 2):
+        pre = normed[f, r] * g + b
+        act[r] = jnp.where(valid(r), pre * jax.nn.sigmoid(pre), 0.0)
+
+
+def spread_columns(act, cols, f):
+    for t in range(TAPS):
+        a, c = t // 3, t % 3
+        piece = act[a : a + TH, c : c + TW, :].reshape(PIX, C).astype(BF16)
+        cols[f * PIX : (f + 1) * PIX, C * t : C * (t + 1)] = piece
+
+
+def target(tile, s):
+    noise = tile[s, TH + 2 : 2 * TH + 2].astype(F32)
+    return (tile[s, 1 : TH + 1].astype(F32) - noise).reshape(PIX, C)
+
+
+def signed_squares(resid):
+    return jnp.sum(resid[0] * resid[0] - resid[1] * resid[1], axis=0, keepdims=True)
+
+
+def kernel_gradient(
+    stats, bias, mine, theirs, my_side, their_side, gain_far, shift_far, weight_far,
+    out_far, normed_far, cot_out, margin_out, out, normed, others, act, cols, cot, grad, parts, weight,
+    gain, shift, sems,
 ):
-    pairs = [
-        (ref_gain_far, ref_gain), (ref_shift_far, ref_shift), (gain_far, gain), (shift_far, shift),
-        (ref_far, ref_weight), (weight_far, weight),
-    ]
+    pairs = [(gain_far, gain), (shift_far, shift), (weight_far, weight)]
     copies = [pltpu.make_async_copy(a, b, sems.at[i]) for i, (a, b) in enumerate(pairs)]
     for copy in copies:
         copy.start()
     core = lax.axis_index("core")
-    row_at = 2 * lax.axis_index("x") + lax.axis_index("zl")
-    chip_at = 2 * lax.axis_index("zh")
-    col_at = (chip_at + core, chip_at + 1 - core)
 
     total = jnp.broadcast_to(jnp.sum(stats[...], axis=0, keepdims=True), (8, 128))
     groups = lax.broadcasted_iota(jnp.int32, (128, C), 0)
@@ -222,96 +245,111 @@
 
     tiles = (mine, theirs)
     sides = (my_side, their_side)
+    fields = (normed, others)
     for w in range(2):
+        field = fields[w]
         for s in range(2):
             here, beside = tiles[w], tiles[1 - w]
-            f = 2 * w + s
-            field[f, :, TW + 2 :, :] = jnp.zeros((TH + 2, 22 - TW, C), F32)
-            field[f, :, 1 : TW + 1, :] = here[s, 0 : TH + 2].astype(F32)
-            outer = sides[w][s].astype(F32)
+            field[s, :, TW + 2 :, :] = jnp.zeros((TH + 2, 22 - TW, C), F32)
+            field[s, :, 1 : TW + 1, :] = (here[s, 0 : TH + 2].astype(F32) - means[s]) * scales[s]
+            outer = (sides[w][s].astype(F32) - means[s]) * scales[s]
             is_left = core == w
             for r in range(TH + 2):
-                near = beside[s, r].astype(F32)
-                out = outer[r : r + 1]
-                field[f, r, 0:1, :] = jnp.where(is_left, out, near[TW - 1 : TW])
-                field[f, r, TW + 1 : TW + 2, :] = jnp.where(is_left, near[0:1], out)
-
-    column = lax.broadcasted_iota(jnp.int32, (24, C), 0)
-    inside = []
+                near = (beside[s, r].astype(F32) - means[s]) * scales[s]
+                out_px = outer[r : r + 1]
+                field[s, r, 0:1, :] = jnp.where(is_left, out_px, near[TW - 1 : TW])
+                field[s, r, TW + 1 : TW + 2, :] = jnp.where(is_left, near[0:1], out_px)
+
+    keep = pltpu.make_async_copy(normed, normed_far, sems.at[3])
+    keep.start()
+    copies[0].wait()
+    copies[1].wait()
+    g, b = gain[...].reshape(1, C), shift[...].reshape(1, C) + bias[0:1]
     for w in range(2):
-        ok = (column < TW + 2) & ((column > 0) | (col_at[w] > 0))
-        inside.append(ok & ((column < TW + 1) | (col_at[w] < 7)))
-
-    def valid(w, r):
-        if r == 0:
-            return inside[w] & (row_at > 0)
-        if r == TH + 1:
-            return inside[w] & (row_at < 7)
-        return inside[w]
-
-    def pre_act(f, r, g, b):
-        normed = (field[f, r] - means[f % 2]) * scales[f % 2]
-        return normed, normed * g + b
-
-    def columns_of(fields, g, b):
-        for f in fields:
-            for r in range(TH + 2):
-                _, pre = pre_act(f, r, g, b)
-                act[r] = jnp.where(valid(f // 2, r), pre * jax.nn.sigmoid(pre), 0.0)
-            for t in range(TAPS):
-                a, c = t // 3, t % 3
-                piece = act[a : a + TH, c : c + TW, :].reshape(PIX, C).astype(BF16)
-                cols[f * PIX : (f + 1) * PIX, C * t : C * (t + 1)] = piece
-
-    def base(f):
-        tile, s = tiles[f // 2], f % 2
-        noise = tile[s, TH + 2 : 2 * TH + 2].astype(F32)
-        return (tile[s, 1 : TH + 1].astype(F32) - noise).reshape(PIX, C)
-
-    def residual(fields, kernel):
-        conv = jnp.dot(
-            cols[0 : PIX * len(fields)],
-            kernel[...].reshape(TAPS * C, C),
-            preferred_element_type=F32,
-        )
-        return [base(f) + conv[PIX * f : PIX * (f + 1)] for f in fields]
-
-    def signed_squares(resid):
-        return jnp.sum(resid[0] * resid[0] - resid[1] * resid[1], axis=0, keepdims=True)
-
+        valid = valid_pixels(core if w == 0 else 1 - core)
+        for s in range(2):
+            activate(fields[w], s, valid, g, b, act)
+            spread_columns(act, cols, 2 * w + s)
+    copies[2].wait()
+    conv = jnp.dot(
+        cols[...], weight[...].reshape(TAPS * C, C), preferred_element_type=F32
+    )
+    resid = [target(tiles[f // 2], f % 2) + conv[PIX * f : PIX * (f + 1)] for f in range(4)]
+    margin_out[...] = jnp.broadcast_to(signed_squares(resid[0:2]), (8, C))
+    for f in range(4):
+        cot[PIX * f : PIX * (f + 1)] = (resid[f] if f % 2 == 0 else -resid[f]).astype(BF16)
+    cot_out[...] = cot[0 : 2 * PIX]
+
+    grad[0 : TAPS * C, :] = lax.dot_general(
+        cols[...], cot[...], (((0,), (0,)), ((), ())), preferred_element_type=F32
+    )
+    row = lax.broadcasted_iota(jnp.int32, (48, C), 0)
+    for parity in range(2):
+
+        @pl.when(core == parity)
+        def _():
+            for q in range(32):
+                start = BLK * (2 * q + parity)
+                parts[q] = jnp.where(row < BLK, grad[start : start + 48, :], 0.0)
+
+    def body(dest, carry):
+        for pair in range(4):
+            q = 8 * dest + 2 * pair
+            packed = packed_pair(side_by_side(parts[q], parts[q + 1]))
+            for k, tile in enumerate(tiles_of(pair)):
+                out[dest, tile] = packed[:, 128 * k : 128 * k + 128]
+        pltpu.make_async_copy(out.at[dest], out_far.at[dest], sems.at[4 + dest]).start()
+        return carry
+
+    lax.fori_loop(0, 4, body, 0)
+    for dest in range(4):
+        pltpu.make_async_copy(out.at[dest], out_far.at[dest], sems.at[4 + dest]).wait()
+    keep.wait()
+
+
+def small_sums(*refs):
+    far, small, near = refs[0:11], refs[11], refs[12:23]
+    act, cols, back, sems = refs[23:27]
+    normed, cot, margin_in, bias, mine, gain, shift, ref_gain, ref_shift, weight, ref_weight = near
+    copies = [pltpu.make_async_copy(far[i], near[i], sems.at[i]) for i in range(11)]
+    for copy in copies:
+        copy.start()
+    for i in (0, 3, 4, 7, 8):
+        copies[i].wait()
+    valid = valid_pixels(lax.axis_index("core"))
     time_row = bias[0:1]
-    for copy in copies[0:4]:
-        copy.wait()
-    columns_of((0, 1), ref_gain[...].reshape(1, C), ref_shift[...].reshape(1, C) + time_row)
-    copies[4].wait()
-    resid = residual((0, 1), ref_weight)
-    margin = -signed_squares(resid)
-    g, b = gain[...].reshape(1, C), shift[...].reshape(1, C) + time_row
-    columns_of((0, 1, 2, 3), g, b)
-    copies[5].wait()
-    resid = residual((0, 1, 2, 3), weight)
-    margin = margin + signed_squares(resid)
-    for f in range(4):
-        cot_out[PIX * f : PIX * (f + 1)] = (resid[f] if f % 2 == 0 else -resid[f]).astype(BF16)
-
-    cot = cot_out[0 : 2 * PIX]
+    g, b = ref_gain[...].reshape(1, C), ref_shift[...].reshape(1, C) + time_row
+    for s in range(2):
+        activate(normed, s, valid, g, b, act)
+        spread_columns(act, cols, s)
+    copies[10].wait()
+    conv = jnp.dot(
+        cols[...], ref_weight[...].reshape(TAPS * C, C), preferred_element_type=F32
+    )
+    resid = [target(mine, s) + conv[PIX * s : PIX * (s + 1)] for s in range(2)]
+    copies[2].wait()
+    margin = margin_in[0:1] - signed_squares(resid)
+
     back[...] = jnp.zeros_like(back)
+    for i in (1, 5, 6, 9):
+        copies[i].wait()
     for t in range(TAPS):
         a, c = t // 3, t % 3
         term = lax.dot_general(
-            cot, weight[t], (((1,), (1,)), ((), ())), preferred_element_type=F32
+            cot[...], weight[t], (((1,), (1,)), ((), ())), preferred_element_type=F32
         )
         for s in range(2):
             back[s, a : a + TH, c : c + TW, :] += term[s * PIX : (s + 1) * PIX].reshape(TH, TW, C)
+    g, b = gain[...].reshape(1, C), shift[...].reshape(1, C) + time_row
     gains = jnp.zeros((24, C), F32)
     shifts = jnp.zeros((24, C), F32)
     for s in range(2):
         for r in range(TH + 2):
-            normed, pre = pre_act(s, r, g, b)
+            pre = normed[s, r] * g + b
             gate = jax.nn.sigmoid(pre)
             slope = gate * (1.0 + pre * (1.0 - gate))
-            dpre = jnp.where(valid(0, r), back[s, r] * slope, 0.0)
-            gains = gains + dpre * normed
+            dpre = jnp.where(valid(r), back[s, r] * slope, 0.0)
+            gains = gains + dpre * normed[s, r]
             shifts = shifts + dpre
     gains = jnp.sum(gains, axis=0, keepdims=True)
     shifts = jnp.sum(shifts, axis=0, keepdims=True)
@@ -321,43 +359,16 @@
     )
 
 
-def kernel_gradient(cols, cot, out, grad):
-    grad[0 : TAPS * C, :] = lax.dot_general(
-        cols[...], cot[...], (((0,), (0,)), ((), ())), preferred_element_type=F32
-    )
-    row = lax.broadcasted_iota(jnp.int32, (48, C), 0)
-    for core in range(2):
-
-        @pl.when(lax.axis_index("core") == core)
-        def _():
-            for q in range(32):
-                start = BLK * (2 * q + core)
-                out[q] = jnp.where(row < BLK, grad[start : start + 48, :], 0.0)
-
-
-def pack_blocks(blocks, small, other, out, extra):
-    write_extras(extra, small[...] + other[...])
-
-    def body(dest, carry):
-        for pair in range(4):
-            q = 8 * dest + 2 * pair
-            packed = packed_pair(side_by_side(blocks[q], blocks[q + 1]), extra[pair])
-            for k, tile in enumerate(tiles_of(pair)):
-                out[dest, tile] = packed[:, 128 * k : 128 * k + 128]
-        return carry
-
-    lax.fori_loop(0, 4, body, 0)
-
-
-def chip_sum(blocks, out):
+def core_sum(one, two, out):
+    out[...] = one[...] + two[...]
+
+
+def chip_sum(blocks, small0, small1, small2, small3, out):
     def pair_of(source, pair, rows):
         parts = [blocks[source, tile].astype(jnp.int32)[rows] for tile in tiles_of(pair)]
         return jnp.concatenate(parts, axis=1)
 
-    tail_rows = slice(40, 48)
-    small = jnp.zeros((8, WIDE), F32)
-    for source in range(4):
-        small = small + read_extras([pair_of(source, k, tail_rows) for k in range(3)])
+    small = (small0[...] + small1[...]) + (small2[...] + small3[...])
     high, low, exps = split_small(small[:, 0:128])
     lane = lax.broadcasted_iota(jnp.int32, (1, 128), 1)
     tail = jnp.zeros((1, 128), F32)
@@ -441,27 +452,34 @@
     beyond = [(i, (i + 2) % 8 if i % 2 else (i + 6) % 8) for i in range(8)]
     swap = [(0, 1), (1, 0)]
 
-    stats, bias, first, last, here = call(
+    first, last = call(
+        edge_rows,
+        [(strip, BF16), (strip, BF16)],
+        [pltpu.SemaphoreType.DMA((4,))],
+        far=(0, 1),
+        grant=57,
+    )(fw, fl)
+    top = lax.ppermute(last, rows, down)
+    bottom = lax.ppermute(first, rows, up)
+    stats, bias, here = call(
         stats_and_time,
-        [((64, 128), F32), ((8, C), F32), (strip, BF16), (strip, BF16)]
-        + [((2, 2 * TH, TW, C), BF16)],
+        [((64, 128), F32), ((8, C), F32), ((2, 2 * TH, TW, C), BF16)],
         [
             pltpu.VMEM((C, C), F32),
             pltpu.SMEM((1,), jnp.int32),
             pltpu.SemaphoreType.DMA((6,)),
         ],
-        flops=10**7,
+        flops=10**9,
         nbytes=10**6,
         far=range(6),
         grant=57,
     )(timesteps, fw, fl, noise_win[0], noise_lose[0], time_weight)
-    top = lax.ppermute(last, rows, down)
-    bottom = lax.ppermute(first, rows, up)
     side, mine = call(
         outer_column_and_tile,
         [(strip, BF16), ((2, 2 * TH + 2, TW, C), BF16)],
-        flops=10**10,
+        flops=10**9,
         nbytes=10**6,
+        grant=57,
     )(top, bottom, here)
     stats, side, mine = lax.optimization_barrier((stats, side, mine))
     stats = lax.all_to_all(stats, ("x", "zl", "zh", "core"), 0, 0, tiled=True)
@@ -469,39 +487,55 @@
     their_side = lax.ppermute(side, columns, beyond)
     theirs = lax.ppermute(mine, "core", swap)
 
-    cols, cot, small = call(
-        forward,
-        [((4 * PIX, TAPS * C), BF16), ((4 * PIX, C), BF16), ((8, WIDE), F32)],
+    field = (2, TH + 2, 24, C)
+    blocks, normed, cot, margin = call(
+        kernel_gradient,
+        [((4, 20, 48, 128), I16), (field, F32), ((2 * PIX, C), BF16), ((8, C), F32)],
         [
-            pltpu.VMEM((4, TH + 2, 24, C), F32),
+            pltpu.VMEM((4, 20, 48, 128), I16),
+            pltpu.VMEM(field, F32),
+            pltpu.VMEM(field, F32),
             pltpu.VMEM((TH + 2, 24, C), F32),
-            pltpu.VMEM((2, TH + 2, 24, C), F32),
+            pltpu.VMEM((4 * PIX, TAPS * C), BF16),
+            pltpu.VMEM((4 * PIX, C), BF16),
+            pltpu.VMEM((TAPS * C + 8, C), F32),
+            pltpu.VMEM((32, 48, C), F32),
             pltpu.VMEM((TAPS, C, C), BF16),
-            pltpu.VMEM((TAPS, C, C), BF16),
-        ]
-        + [pltpu.VMEM((C,), F32)] * 4
-        + [pltpu.SemaphoreType.DMA((6,))],
+            pltpu.VMEM((C,), F32),
+            pltpu.VMEM((C,), F32),
+            pltpu.SemaphoreType.DMA((8,)),
+        ],
         flops=2 * 10**9,
         nbytes=10**7,
-        far=range(6, 12),
-    )(
-        stats, bias, mine, theirs, my_side, their_side, norm_gain, norm_shift, ref_gain, ref_shift,
-        conv_weight, ref_weight,
+        far=(6, 7, 8),
+        far_outs=(0, 1),
+        grant=55,
+    )(stats, bias, mine, theirs, my_side, their_side, norm_gain, norm_shift, conv_weight)
+    blocks = lax.all_to_all(blocks, "x", 0, 0, tiled=True)
+    near = (
+        normed, cot, margin, bias, mine, norm_gain, norm_shift, ref_gain, ref_shift, conv_weight,
+        ref_weight,
     )
-    other = lax.ppermute(small, "core", swap)
-    block = (32, 48, C)
-    (blocks,) = call(
-        kernel_gradient,
-        [(block, F32)],
-        [pltpu.VMEM((TAPS * C + 8, C), F32)],
+    (small,) = call(
+        small_sums,
+        [((8, WIDE), F32)],
+        [pltpu.VMEM(v.shape, v.dtype) for v in near]
+        + [
+            pltpu.VMEM((TH + 2, 24, C), F32),
+            pltpu.VMEM((2 * PIX, TAPS * C), BF16),
+            pltpu.VMEM(field, F32),
+            pltpu.SemaphoreType.DMA((11,)),
+        ],
         flops=10**9,
         nbytes=10**7,
-    )(cols, cot)
-    (blocks,) = call(
-        pack_blocks, [((4, 20, 48, 128), I16)], [pltpu.VMEM((4, 8, WIDE), F32)]
-    )(blocks, small, other)
-    blocks = lax.all_to_all(blocks, "x", 0, 0, tiled=True)
-    (sums,) = call(chip_sum, [((8, 8, 24, 128), I16)])(blocks)
+        far=range(11),
+        grant=57,
+    )(*near)
+    (small,) = call(core_sum, [((8, WIDE), F32)])(small, lax.ppermute(small, "core", swap))
+    smalls = [small] + [
+        lax.ppermute(small, "x", [(i, (i + k) % 4) for i in range(4)]) for k in (1, 2, 3)
+    ]
+    (sums,) = call(chip_sum, [((8, 8, 24, 128), I16)])(blocks, *smalls)
     sums = lax.all_to_all(sums.reshape(64, 24, 128), ("y", "zl", "zh"), 0, 0, tiled=True)
     loss, grad, gain, shift = call(
         final_sum, [((1, 1), F32), ((40, BLK), F32), ((C,), F32), ((C,), F32)]

time: 108 us -> 113 us (1.046)
  blocking collectives: 46 us -> 25.8 us
  starting transfers between devices: 33.7 us -> 47 us
  Pallas kernels: 16.1 us -> 24.5 us
  waiting for transfers between devices: 7.13 us -> 11 us
    all_to_all x1 -> x0, blocking collectives: 19.3 us -> none  [local(): blocks = lax.all_to_all(blocks, 'x', 0, 0, tiled=True)]
    ppermute x1 -> x4, starting transfers between devices: 1.92 us -> 12.6 us  [the longest x3 10.7 us: local(): lax.ppermute(small, 'x', [(i, (i + k) % 4) for i in range(4)])]
    pallas_call x7 -> x8, Pallas kernels: 16.1 us -> 24.5 us  [run(): pl.pallas_call(kernel, out_shape=[jax.ShapeDtypeStruct(s, d) for s, d in...]
    ppermute x1 -> x4, waiting for transfers between devices: 0.01 us -> 5.47 us  [the longest x3 4.1 us: local(): lax.ppermute(small, 'x', [(i, (i + k) % 4) for i in range(4)])]
    all_to_all x0 -> x1, starting transfers between devices: none -> 4.39 us  [local(): blocks = lax.all_to_all(blocks, 'x', 0, 0, tiled=True)]
    ppermute x1, waiting for transfers between devices: 1.73 us -> 0.01 us  [local(): bottom = lax.ppermute(first, rows, up)]
    all_to_all x1, starting transfers between devices: 13.8 us -> 12.2 us  [local(): stats = lax.all_to_all(stats, ('x', 'zl', 'zh', 'core'), 0, 0, tiled=True)]
    unnamed x16 -> x14, local copies, waits for them, and re-layouts: 2.64 us -> 2.09 us
  transfers between devices with their start and end apart: 7 -> 11, of which waited for: 3 -> 4; matrix products, arithmetic and copies ran while one was open for 0% -> 0% of each run, Pallas kernels for 2% -> 8%
where the time goes in v4:
time: 113 us; the launch traced here: 112 us
  starting transfers between devices  47 us (42%)
  blocking collectives  25.8 us (23%)
  Pallas kernels  24.5 us (22%)
  waiting for transfers between devices  11 us (10%)
  local copies, waits for them, and re-layouts  2.09 us (2%)
  between operations  1.48 us (1%)
    all_to_all x1, blocking collectives, local(): lax.all_to_all(sums.reshape(64, 24, 128), ('y', 'zl', 'zh'), 0, 0, tiled=...  25.8 us
    pallas_call x8, Pallas kernels, run(): pl.pallas_call(kernel, out_shape=[jax.ShapeDtypeStruct(s, d) for s, d in...  24.5 us
    all_to_all x1, starting transfers between devices, local(): stats = lax.all_to_all(stats, ('x', 'zl', 'zh', 'core'), 0, 0, tiled=True)  12.2 us
    ppermute x3, starting transfers between devices, local(): lax.ppermute(small, 'x', [(i, (i + k) % 4) for i in range(4)])  10.7 us
    ppermute x1, starting transfers between devices, local(): their_side = lax.ppermute(side, columns, beyond)  5.59 us
    ppermute x1, waiting for transfers between devices, local(): my_side = lax.ppermute(side, columns, outward)  5.52 us
    all_to_all x1, starting transfers between devices, local(): blocks = lax.all_to_all(blocks, 'x', 0, 0, tiled=True)  4.39 us
    ppermute x1, starting transfers between devices, local(): top = lax.ppermute(last, rows, down)  4.28 us
  transfers between devices with their start and end apart: 11, of which 4 were waited for; matrix products, arithmetic and copies ran while one was open for 0% of the time, Pallas kernels for 8%

profile of v4, /device:TPU:8, one launch (start us, length us, event | category | flops | bytes accessed | tf_op | source)
XLA Modules:
  0.0 111.9 jit_solution(2005784068036833837)
XLA Ops:
  0.6 1.4 %shard_map.148 = (bf16[2,16,320]{2,1,0:T(8,128)(2,1)}, bf16[2,16,320]{2,1,0:T(8,128)(2,1)}) custom-call(bf16[8,16,320]{2,1,0:T(8,128)(2,1)} %bitcast.13, bf16[8,16,320]{2,1,0:T(8,128)(2,1)} %bitcast.15), custom_call_target="tpu_custom_call" | custom-call | tf_op jit(solution)/shard_map/pallas_call | solution.py:32
  2.1 4.3 %collective-permute-start = (bf16[2,16,320]{2,1,0:T(8,128)(2,1)}, bf16[2,16,320]{2,1,0:T(8,128)(2,1)S(1)}, u32[]{:S(2)}, u32[]{:S(2)}) collective-permute-start(bf16[2,16,320]{2,1,0:T(8,128)(2,1)} %get-tuple-element.23), channel_id=1, source_target_pairs={{0,8},{8,16},{16,24},{24,32},{32,40},{40,48},{48,56},{56,0},{1,9},... | collective-permute-start | bytes 61448 | tf_op jit(solution)/shard_map/ppermute | solution.py:462
  6.4 4.1 %collective-permute-start.1 = (bf16[2,16,320]{2,1,0:T(8,128)(2,1)}, bf16[2,16,320]{2,1,0:T(8,128)(2,1)S(1)}, u32[]{:S(2)}, u32[]{:S(2)}) collective-permute-start(bf16[2,16,320]{2,1,0:T(8,128)(2,1)} %get-tuple-element.24), channel_id=1, source_target_pairs={{8,0},{16,8},{24,16},{32,24},{40,32},{48,40},{56,48},{0,56},{9,1},... | collective-permute-start | bytes 61448 | tf_op jit(solution)/shard_map/ppermute | solution.py:463
  11.1 2.9 %shard_map.147 = (f32[64,128]{1,0:T(8,128)}, f32[8,320]{1,0:T(8,128)}, bf16[2,16,16,320]{3,2,1,0:T(8,128)(2,1)}) custom-call(s32[1]{0:T(128)S(6)} %copy.17.step, bf16[8,16,320]{2,1,0:T(8,128)(2,1)} %bitcast.14, bf16[8,16,320]{2,1,0:T(8,128)(2,1)} %bitcast.16, bf16[8,16,320]{2,1,0:T(8,128)(2,1)} %bitcast.18, bf16[8,16,320]{2,1,0:T(8,128)(2,1)} %bitcast.19, ...), custom_call_target="tpu_custom_call" | custom-call | flops 1000000000 | bytes 1000000 | tf_op jit(solution)/shard_map/pallas_call | solution.py:32
  14.0 0.0 collective-permute-done.top
  14.0 0.0 copy-start.5
  14.0 0.0 collective-permute-done.1.bottom
  14.0 0.0 copy-start.6
  14.0 0.6 copy-done.5
  14.6 0.0 copy-done.6
  14.6 1.8 %shard_map.149 = (bf16[2,16,320]{2,1,0:T(8,128)(2,1)}, bf16[2,18,16,320]{3,2,1,0:T(8,128)(2,1)}) custom-call(bf16[2,16,320]{2,1,0:T(8,128)(2,1)} %copy-done.5, bf16[2,16,320]{2,1,0:T(8,128)(2,1)} %copy-done.6, bf16[2,16,16,320]{3,2,1,0:T(8,128)(2,1)} %get-tuple-element.25.here), custom_call_target="tpu_custom_call" | custom-call | flops 1000000000 | bytes 1000000 | tf_op jit(solution)/shard_map/pallas_call | solution.py:32
  16.5 1.9 %collective-permute-start.2 = (bf16[2,18,16,320]{3,2,1,0:T(8,128)(2,1)}, bf16[2,18,16,320]{3,2,1,0:T(8,128)(2,1)S(1)}, u32[]{:S(2)}, u32[]{:S(2)}) collective-permute-start(bf16[2,18,16,320]{3,2,1,0:T(8,128)(2,1)} %get-tuple-element.30.mine.refs_4_), channel_id=1, source_target_pairs={{0,1},{1,0},{2,3},{3,2},{4,5},{5,4},{6,7},{7,6},{8,9},{9,8},{10,11... | collective-permute-start | bytes 1105928 | tf_op jit(solution)/shard_map/ppermute | solution.py:488
  18.4 12.2 %all-to-all-start = ((f32[64,1,128]{2,1,0:T(1,128)}), f32[64,1,128]{2,1,0:T(1,128)S(1)}, u32[]{:S(2)}, u32[]{:S(2)}) async-start(f32[64,1,128]{2,1,0:T(1,128)} %bitcast.5), calls=%async_computation | async-start | bytes 65536 | tf_op jit(solution)/shard_map/all_to_all | solution.py:485
  30.6 5.6 %collective-permute-start.4 = (bf16[2,16,320]{2,1,0:T(8,128)(2,1)}, bf16[2,16,320]{2,1,0:T(8,128)(2,1)S(1)}, u32[]{:S(2)}, u32[]{:S(2)}) collective-permute-start(bf16[2,16,320]{2,1,0:T(8,128)(2,1)} %get-tuple-element.31), channel_id=1, source_target_pairs={{0,6},{1,3},{2,0},{3,5},{4,2},{5,7},{6,4},{7,1},{8,14},{9,11},{10,... | collective-permute-start | bytes 61448 | tf_op jit(solution)/shard_map/ppermute | solution.py:487
  36.2 1.9 %collective-permute-start.3 = (bf16[2,16,320]{2,1,0:T(8,128)(2,1)}, bf16[2,16,320]{2,1,0:T(8,128)(2,1)S(1)}, u32[]{:S(2)}, u32[]{:S(2)}) collective-permute-start(bf16[2,16,320]{2,1,0:T(8,128)(2,1)} %get-tuple-element.31), channel_id=1, source_target_pairs={{0,7},{1,2},{2,1},{3,4},{4,3},{5,6},{6,5},{7,0},{8,15},{9,10},{10,... | collective-permute-start | bytes 61448 | tf_op jit(solution)/shard_map/ppermute | solution.py:486
  38.2 0.0 collective-permute-done.4.their_side
  38.2 0.0 copy-start.3
  38.2 5.5 %collective-permute-done.3.my_side = bf16[2,16,320]{2,1,0:T(8,128)(2,1)S(1)} collective-permute-done((bf16[2,16,320]{2,1,0:T(8,128)(2,1)}, bf16[2,16,320]{2,1,0:T(8,128)(2,1)S(1)}, u32[]{:S(2)}, u32[]{:S(2)}) %collective-permute-start.3) | collective-permute-done | bytes 20512 | tf_op jit(solution)/shard_map/ppermute | solution.py:486
  43.7 0.0 copy-start.4
  43.7 0.0 all-to-all-done
  43.7 0.0 copy-start.1
  43.7 0.0 collective-permute-done.2.theirs
  43.7 0.0 copy-start.2
  43.7 0.0 copy-done.3
  43.7 0.6 copy-done.4
  44.3 0.0 copy-done.1
  44.3 0.2 copy-done.2
  44.5 9.2 %shard_map.150 = (s16[4,20,48,128]{3,2,1,0:T(8,128)(2,1)}, f32[2,10,24,320]{3,2,1,0:T(8,128)}, bf16[256,320]{1,0:T(8,128)(2,1)}, f32[8,320]{1,0:T(8,128)}) custom-call(f32[64,128]{1,0:T(8,128)} %bitcast.17, f32[8,320]{1,0:T(8,128)} %get-tuple-element.29.bias.refs_3_, bf16[2,18,16,320]{3,2,1,0:T(8,128)(2,1)} %get-tuple-element.30.mine.refs_4_, ...), custom_call_target="tpu_custom_call" | custom-call | flops 2000000000 | bytes 10000000 | tf_op jit(solution)/shard_map/pallas_call | solution.py:32
  53.7 4.4 %all-to-all-start.1 = ((s16[4,20,48,128]{3,2,1,0:T(8,128)(2,1)}), s16[4,20,48,128]{3,2,1,0:T(8,128)(2,1)S(1)}, u32[]{:S(2)}, u32[]{:S(2)}) async-start(s16[4,20,48,128]{3,2,1,0:T(8,128)(2,1)} %get-tuple-element.32), calls=%async_computation.1 | async-start | bytes 1966080 | tf_op jit(solution)/shard_map/all_to_all | solution.py:514
  58.1 6.1 %shard_map.151.one = f32[8,640]{1,0:T(8,128)} custom-call(f32[2,10,24,320]{3,2,1,0:T(8,128)} %get-tuple-element.33.refs_0_, bf16[256,320]{1,0:T(8,128)(2,1)} %get-tuple-element.34.refs_1_, f32[8,320]{1,0:T(8,128)} %get-tuple-element.35.refs_2_, f32[8,320]{1,0:T(8,128)} %get-tuple-element.29.bias.refs_3_, ...), custom_call_target="tpu_custom_call" | custom-call | flops 1000000000 | bytes 10000000 | tf_op jit(solution)/shard_map/pallas_call | solution.py:32
  64.2 1.9 %collective-permute-start.5 = (f32[8,640]{1,0:T(8,128)}, f32[8,640]{1,0:T(8,128)S(1)}, u32[]{:S(2)}, u32[]{:S(2)}) collective-permute-start(f32[8,640]{1,0:T(8,128)} %shard_map.151.one), channel_id=1, source_target_pairs={{0,1},{1,0},{2,3},{3,2},{4,5},{5,4},{6,7},{7,6},{8,9},{9,8},{10,11... | collective-permute-start | bytes 61448 | tf_op jit(solution)/shard_map/ppermute | solution.py:534
  66.1 1.4 %collective-permute-done.5.two = f32[8,640]{1,0:T(8,128)S(1)} collective-permute-done((f32[8,640]{1,0:T(8,128)}, f32[8,640]{1,0:T(8,128)S(1)}, u32[]{:S(2)}, u32[]{:S(2)}) %collective-permute-start.5) | collective-permute-done | bytes 20512 | tf_op jit(solution)/shard_map/ppermute | solution.py:534
  67.5 0.0 copy-start
  67.5 0.7 copy-done
  68.2 5.1 %collective-permute-start.8 = (f32[8,640]{1,0:T(8,128)S(1)}, f32[8,640]{1,0:T(8,128)S(1)}, u32[]{:S(2)}, u32[]{:S(2)}) collective-permute-start(f32[8,640]{1,0:T(8,128)S(1)} %shard_map.152.small0), channel_id=1, source_target_pairs={{0,48},{16,0},{32,16},{48,32},{1,49},{17,1},{33,17},{49,33},{2,50}... | collective-permute-start | bytes 61448 | tf_op jit(solution)/shard_map/ppermute | solution.py:536
  73.4 2.8 %collective-permute-start.7 = (f32[8,640]{1,0:T(8,128)S(1)}, f32[8,640]{1,0:T(8,128)S(1)}, u32[]{:S(2)}, u32[]{:S(2)}) collective-permute-start(f32[8,640]{1,0:T(8,128)S(1)} %shard_map.152.small0), channel_id=1, source_target_pairs={{0,32},{16,48},{32,0},{48,16},{1,33},{17,49},{33,1},{49,17},{2,34}... | collective-permute-start | bytes 61448 | tf_op jit(solution)/shard_map/ppermute | solution.py:536
  76.1 2.8 %collective-permute-start.6 = (f32[8,640]{1,0:T(8,128)S(1)}, f32[8,640]{1,0:T(8,128)S(1)}, u32[]{:S(2)}, u32[]{:S(2)}) collective-permute-start(f32[8,640]{1,0:T(8,128)S(1)} %shard_map.152.small0), channel_id=1, source_target_pairs={{0,16},{16,32},{32,48},{48,0},{1,17},{17,33},{33,49},{49,1},{2,18}... | collective-permute-start | bytes 61448 | tf_op jit(solution)/shard_map/ppermute | solution.py:536
  78.9 0.0 collective-permute-done.8.small3
  78.9 1.6 %collective-permute-done.7.small2 = f32[8,640]{1,0:T(8,128)S(1)} collective-permute-done((f32[8,640]{1,0:T(8,128)S(1)}, f32[8,640]{1,0:T(8,128)S(1)}, u32[]{:S(2)}, u32[]{:S(2)}) %collective-permute-start.7) | collective-permute-done | bytes 20512 | tf_op jit(solution)/shard_map/ppermute | solution.py:536
  80.6 2.5 %collective-permute-done.6.small1 = f32[8,640]{1,0:T(8,128)S(1)} collective-permute-done((f32[8,640]{1,0:T(8,128)S(1)}, f32[8,640]{1,0:T(8,128)S(1)}, u32[]{:S(2)}, u32[]{:S(2)}) %collective-permute-start.6) | collective-permute-done | bytes 20512 | tf_op jit(solution)/shard_map/ppermute | solution.py:536
  83.0 0.0 all-to-all-done.1.blocks
  83.0 1.7 %shard_map.153 = s16[8,8,24,128]{3,2,1,0:T(8,128)(2,1)S(1)} custom-call(s16[4,20,48,128]{3,2,1,0:T(8,128)(2,1)S(1)} %all-to-all-done.1.blocks, f32[8,640]{1,0:T(8,128)S(1)} %shard_map.152.small0, f32[8,640]{1,0:T(8,128)S(1)} %collective-permute-done.6.small1, f32[8,640]{1,0:T(8,128)S(1)} %collective-permute-done.7.small2, ...), custom_call_target="tpu_custom_call" | custom-call | tf_op jit(solution)/shard_map/pallas_call | solution.py:32
  84.7 25.8 %all_to_all.21 = s16[64,24,128]{2,1,0:T(8,128)(2,1)S(1)} all-to-all(s16[64,24,128]{2,1,0:T(8,128)(2,1)S(1)} %bitcast.12), channel_id=1, replica_groups=mesh['y'=8,'x'=4,'zl'=2,'zh'=4,'core'=2] {'y','zl','zh'}, dimensions={0} | all-to-all | bytes 786432 | tf_op jit(solution)/shard_map/all_to_all | solution.py:539
  110.5 1.4 %shard_map.154 = (f32[1,1]{1,0:T(1,128)}, f32[40,45]{1,0:T(8,128)}, f32[320]{0:T(512)}, f32[320]{0:T(512)}) custom-call(s16[8,8,24,128]{3,2,1,0:T(8,128)(2,1)S(1)} %bitcast.11), custom_call_target="tpu_custom_call" | custom-call | tf_op jit(solution)/shard_map/pallas_call | solution.py:32
  (1 shorter events, 0.0 us)
Async XLA Ops:
  2.1 11.9 %collective-permute-start = (bf16[2,16,320]{2,1,0:T(8,128)(2,1)}, bf16[2,16,320]{2,1,0:T(8,128)(2,1)S(1)}, u32[]{:S(2)}, u32[]{:S(2)}) collective-permute-start(bf16[2,16,320]{2,1,0:T(8,128)(2,1)} %get-tuple-element.23), channel_id=1, source_target_pairs={{0,8},{8,16},{16,24},{24,32},{32,40},{40,48},{48,56},{56,0},{1,9},... | collective-permute-start | bytes 61448 | tf_op jit(solution)/shard_map/ppermute | solution.py:462
  6.4 7.7 %collective-permute-start.1 = (bf16[2,16,320]{2,1,0:T(8,128)(2,1)}, bf16[2,16,320]{2,1,0:T(8,128)(2,1)S(1)}, u32[]{:S(2)}, u32[]{:S(2)}) collective-permute-start(bf16[2,16,320]{2,1,0:T(8,128)(2,1)} %get-tuple-element.24), channel_id=1, source_target_pairs={{8,0},{16,8},{24,16},{32,24},{40,32},{48,40},{56,48},{0,56},{9,1},... | collective-permute-start | bytes 61448 | tf_op jit(solution)/shard_map/ppermute | solution.py:463
  14.0 0.6 copy-start.5
  14.0 0.6 copy-start.6
  16.5 27.2 %collective-permute-start.2 = (bf16[2,18,16,320]{3,2,1,0:T(8,128)(2,1)}, bf16[2,18,16,320]{3,2,1,0:T(8,128)(2,1)S(1)}, u32[]{:S(2)}, u32[]{:S(2)}) collective-permute-start(bf16[2,18,16,320]{3,2,1,0:T(8,128)(2,1)} %get-tuple-element.30.mine.refs_4_), channel_id=1, source_target_pairs={{0,1},{1,0},{2,3},{3,2},{4,5},{5,4},{6,7},{7,6},{8,9},{9,8},{10,11... | collective-permute-start | bytes 1105928 | tf_op jit(solution)/shard_map/ppermute | solution.py:488
  18.4 25.3 %all-to-all-start = ((f32[64,1,128]{2,1,0:T(1,128)}), f32[64,1,128]{2,1,0:T(1,128)S(1)}, u32[]{:S(2)}, u32[]{:S(2)}) async-start(f32[64,1,128]{2,1,0:T(1,128)} %bitcast.5), calls=%async_computation | async-start | bytes 65536 | tf_op jit(solution)/shard_map/all_to_all | solution.py:485
  30.6 7.5 %collective-permute-start.4 = (bf16[2,16,320]{2,1,0:T(8,128)(2,1)}, bf16[2,16,320]{2,1,0:T(8,128)(2,1)S(1)}, u32[]{:S(2)}, u32[]{:S(2)}) collective-permute-start(bf16[2,16,320]{2,1,0:T(8,128)(2,1)} %get-tuple-element.31), channel_id=1, source_target_pairs={{0,6},{1,3},{2,0},{3,5},{4,2},{5,7},{6,4},{7,1},{8,14},{9,11},{10,... | collective-permute-start | bytes 61448 | tf_op jit(solution)/shard_map/ppermute | solution.py:487
  36.2 7.5 %collective-permute-start.3 = (bf16[2,16,320]{2,1,0:T(8,128)(2,1)}, bf16[2,16,320]{2,1,0:T(8,128)(2,1)S(1)}, u32[]{:S(2)}, u32[]{:S(2)}) collective-permute-start(bf16[2,16,320]{2,1,0:T(8,128)(2,1)} %get-tuple-element.31), channel_id=1, source_target_pairs={{0,7},{1,2},{2,1},{3,4},{4,3},{5,6},{6,5},{7,0},{8,15},{9,10},{10,... | collective-permute-start | bytes 61448 | tf_op jit(solution)/shard_map/ppermute | solution.py:486
  38.2 5.6 %copy-start.3 = (bf16[2,16,320]{2,1,0:T(8,128)(2,1)}, bf16[2,16,320]{2,1,0:T(8,128)(2,1)S(1)}, u32[]{:S(2)}) copy-start(bf16[2,16,320]{2,1,0:T(8,128)(2,1)S(1)} %collective-permute-done.4.their_side) | copy-start | bytes 61444
  43.7 0.6 copy-start.4
  43.7 0.6 copy-start.1
  43.7 0.8 copy-start.2
  53.7 29.4 %all-to-all-start.1 = ((s16[4,20,48,128]{3,2,1,0:T(8,128)(2,1)}), s16[4,20,48,128]{3,2,1,0:T(8,128)(2,1)S(1)}, u32[]{:S(2)}, u32[]{:S(2)}) async-start(s16[4,20,48,128]{3,2,1,0:T(8,128)(2,1)} %get-tuple-element.32), calls=%async_computation.1 | async-start | bytes 1966080 | tf_op jit(solution)/shard_map/all_to_all | solution.py:514
  64.2 3.3 %collective-permute-start.5 = (f32[8,640]{1,0:T(8,128)}, f32[8,640]{1,0:T(8,128)S(1)}, u32[]{:S(2)}, u32[]{:S(2)}) collective-permute-start(f32[8,640]{1,0:T(8,128)} %shard_map.151.one), channel_id=1, source_target_pairs={{0,1},{1,0},{2,3},{3,2},{4,5},{5,4},{6,7},{7,6},{8,9},{9,8},{10,11... | collective-permute-start | bytes 61448 | tf_op jit(solution)/shard_map/ppermute | solution.py:534
  67.5 0.7 copy-start
  68.2 10.7 %collective-permute-start.8 = (f32[8,640]{1,0:T(8,128)S(1)}, f32[8,640]{1,0:T(8,128)S(1)}, u32[]{:S(2)}, u32[]{:S(2)}) collective-permute-start(f32[8,640]{1,0:T(8,128)S(1)} %shard_map.152.small0), channel_id=1, source_target_pairs={{0,48},{16,0},{32,16},{48,32},{1,49},{17,1},{33,17},{49,33},{2,50}... | collective-permute-start | bytes 61448 | tf_op jit(solution)/shard_map/ppermute | solution.py:536
  73.4 7.2 %collective-permute-start.7 = (f32[8,640]{1,0:T(8,128)S(1)}, f32[8,640]{1,0:T(8,128)S(1)}, u32[]{:S(2)}, u32[]{:S(2)}) collective-permute-start(f32[8,640]{1,0:T(8,128)S(1)} %shard_map.152.small0), channel_id=1, source_target_pairs={{0,32},{16,48},{32,0},{48,16},{1,33},{17,49},{33,1},{49,17},{2,34}... | collective-permute-start | bytes 61448 | tf_op jit(solution)/shard_map/ppermute | solution.py:536
  76.1 6.9 %collective-permute-start.6 = (f32[8,640]{1,0:T(8,128)S(1)}, f32[8,640]{1,0:T(8,128)S(1)}, u32[]{:S(2)}, u32[]{:S(2)}) collective-permute-start(f32[8,640]{1,0:T(8,128)S(1)} %shard_map.152.small0), channel_id=1, source_target_pairs={{0,16},{16,32},{32,48},{48,0},{1,17},{17,33},{33,49},{49,1},{2,18}... | collective-permute-start | bytes 61448 | tf_op jit(solution)/shard_map/ppermute | solution.py:536

commit v5 on v3

--- a/solution.py
+++ b/solution.py
@@ -80,22 +80,23 @@
 
 def write_extras(extra, small):
     high, low, exps = split_small(small)
+    lane = lax.broadcasted_iota(jnp.int32, (1, WIDE), 1)
     extra[...] = jnp.zeros_like(extra)
     extra[0, 0:1] = high[0:1]
     extra[0, 1:2] = low[0:1]
     extra[1, 0:1] = exps[0:1]
-    extra[1, 1:2] = high[1:2]
-    extra[2, 0:1] = low[1:2]
-    extra[2, 1:2] = exps[1:2]
+    margin = jnp.where(lane == 1, low[1:2], exps[1:2])
+    extra[1, 1:2] = jnp.where(lane == 0, high[1:2], margin)
 
 
 def read_extras(tails):
-    rows = [tails[0][6:7], tails[0][7:8], tails[1][6:7], tails[1][7:8], tails[2][6:7], tails[2][7:8]]
-    out = []
-    for high, low, exps in (rows[0:3], rows[3:6]):
-        value = high.astype(F32) + low.astype(F32) * (1.0 / 32768.0)
-        out.append(value * pow2(exps - 15))
-    return jnp.concatenate(out + [jnp.zeros((6, WIDE), F32)], axis=0)
+    high, low, exps = tails[0][6:7], tails[0][7:8], tails[1][6:7]
+    sums = (high.astype(F32) + low.astype(F32) * (1.0 / 32768.0)) * pow2(exps - 15)
+    row = tails[1][7:8]
+    value = row.astype(F32)
+    margin = (value[:, 0:1] + value[:, 1:2] * (1.0 / 32768.0)) * pow2(row[:, 2:3] - 15)
+    margin = jnp.broadcast_to(margin, (1, WIDE))
+    return jnp.concatenate([sums, margin, jnp.zeros((6, WIDE), F32)], axis=0)
 
 
 def packed_pair(pair, extra):
@@ -116,19 +117,15 @@
 
 
 def tiles_of(pair):
-    return [4 * pair, 4 * pair + 1, 4 * pair + 2, 4 * pair + 3, 16 + pair]
-
-
-def stats_and_time(
-    step, fw, fl, nw, nl, time_weight, stats, bias, first, last, here, table, number, sems
-):
+    return [4 * pair, 4 * pair + 1, 4 * pair + 2, 4 * pair + 3, 8 + pair]
+
+
+def statistics(fw, fl, nw, nl, stats, first, last, here, sems):
     copies = [
         pltpu.make_async_copy(fw, here.at[0, pl.ds(0, TH)], sems.at[0]),
         pltpu.make_async_copy(fl, here.at[1, pl.ds(0, TH)], sems.at[1]),
-        pltpu.make_async_copy(step, number, sems.at[2]),
-        pltpu.make_async_copy(time_weight, table, sems.at[3]),
-        pltpu.make_async_copy(nw, here.at[0, pl.ds(TH, TH)], sems.at[4]),
-        pltpu.make_async_copy(nl, here.at[1, pl.ds(TH, TH)], sems.at[5]),
+        pltpu.make_async_copy(nw, here.at[0, pl.ds(TH, TH)], sems.at[2]),
+        pltpu.make_async_copy(nl, here.at[1, pl.ds(TH, TH)], sems.at[3]),
     ]
     for copy in copies:
         copy.start()
@@ -155,22 +152,54 @@
                 preferred_element_type=F32,
             )
     stats[...] = jnp.broadcast_to(total[0:1], stats.shape)
+    copies[2].wait()
+    copies[3].wait()
+
+
+def time_bias(step, time_weight, bias, number, table, sems):
+    copies = [
+        pltpu.make_async_copy(step, number, sems.at[0]),
+        pltpu.make_async_copy(time_weight, table, sems.at[1]),
+    ]
+    for copy in copies:
+        copy.start()
     half = C // 2
     lane = lax.broadcasted_iota(jnp.int32, (8, C), 1)
     place = jnp.where(lane < half, lane, lane - half).astype(F32)
     frequency = jnp.exp(-math.log(10000.0) * place / half)
-    copies[2].wait()
+    copies[0].wait()
     angles = number[0].astype(F32) * frequency
     sinusoid = jnp.where(lane < half, jnp.cos(angles), jnp.sin(angles))
     gate = sinusoid * jax.nn.sigmoid(sinusoid)
-    copies[3].wait()
+    copies[1].wait()
     bias[...] = jnp.dot(gate, table[...], precision=HIGHEST, preferred_element_type=F32)
-    copies[4].wait()
-    copies[5].wait()
-
-
-def outer_column_and_tile(top, bottom, here, side, tile):
+
+
+def moments_and_tile(stats, top, bottom, here, moments, side, tile):
     core = lax.axis_index("core")
+
+    total = jnp.broadcast_to(jnp.sum(stats[...], axis=0, keepdims=True), (8, 128))
+    groups = lax.broadcasted_iota(jnp.int32, (128, C), 0)
+    chans = lax.broadcasted_iota(jnp.int32, (128, C), 1)
+    size = C // GROUPS
+    entries = float(PIXELS * size)
+
+    def by_channel(k):
+        group = groups - GROUPS * k
+        member = (group >= 0) & (group < GROUPS)
+        member = member & (chans >= group * size) & (chans < group * size + size)
+        spread = jnp.dot(total, member.astype(F32), precision=HIGHEST, preferred_element_type=F32)
+        return spread[0:1] / entries
+
+    means, scales = [], []
+    for s in range(2):
+        mean, square = by_channel(2 * s), by_channel(2 * s + 1)
+        means.append(mean)
+        scales.append(lax.rsqrt(square - mean * mean + 1e-05))
+    moments[...] = jnp.concatenate(
+        [means[0], scales[0], means[1], scales[1], jnp.zeros((4, C), F32)], axis=0
+    )
+
     for s in range(2):
         tile[s, 0] = top[s]
         tile[s, 1 : TH + 1] = here[s, 0:TH]
@@ -185,7 +214,7 @@
 
 
 def forward(
-    stats, bias, mine, theirs, my_side, their_side, gain_far, shift_far, ref_gain_far, ref_shift_far,
+    moments, bias, mine, theirs, my_side, their_side, gain_far, shift_far, ref_gain_far, ref_shift_far,
     weight_far, ref_far, cols, cot_out, small, field, act, back, weight, ref_weight, gain, shift,
     ref_gain, ref_shift, sems,
 ):
@@ -201,24 +230,8 @@
     chip_at = 2 * lax.axis_index("zh")
     col_at = (chip_at + core, chip_at + 1 - core)
 
-    total = jnp.broadcast_to(jnp.sum(stats[...], axis=0, keepdims=True), (8, 128))
-    groups = lax.broadcasted_iota(jnp.int32, (128, C), 0)
-    chans = lax.broadcasted_iota(jnp.int32, (128, C), 1)
-    size = C // GROUPS
-    entries = float(PIXELS * size)
-
-    def by_channel(k):
-        group = groups - GROUPS * k
-        member = (group >= 0) & (group < GROUPS)
-        member = member & (chans >= group * size) & (chans < group * size + size)
-        spread = jnp.dot(total, member.astype(F32), precision=HIGHEST, preferred_element_type=F32)
-        return spread[0:1] / entries
-
-    means, scales = [], []
-    for s in range(2):
-        mean, square = by_channel(2 * s), by_channel(2 * s + 1)
-        means.append(mean)
-        scales.append(lax.rsqrt(square - mean * mean + 1e-05))
+    means = [moments[2 * s : 2 * s + 1] for s in range(2)]
+    scales = [moments[2 * s + 1 : 2 * s + 2] for s in range(2)]
 
     tiles = (mine, theirs)
     sides = (my_side, their_side)
@@ -339,14 +352,14 @@
     write_extras(extra, small[...] + other[...])
 
     def body(dest, carry):
-        for pair in range(4):
-            q = 8 * dest + 2 * pair
+        for pair in range(2):
+            q = 4 * dest + 2 * pair
             packed = packed_pair(side_by_side(blocks[q], blocks[q + 1]), extra[pair])
             for k, tile in enumerate(tiles_of(pair)):
                 out[dest, tile] = packed[:, 128 * k : 128 * k + 128]
         return carry
 
-    lax.fori_loop(0, 4, body, 0)
+    lax.fori_loop(0, 8, body, 0)
 
 
 def chip_sum(blocks, out):
@@ -356,8 +369,8 @@
 
     tail_rows = slice(40, 48)
     small = jnp.zeros((8, WIDE), F32)
-    for source in range(4):
-        small = small + read_extras([pair_of(source, k, tail_rows) for k in range(3)])
+    for source in range(8):
+        small = small + read_extras([pair_of(source, k, tail_rows) for k in range(2)])
     high, low, exps = split_small(small[:, 0:128])
     lane = lax.broadcasted_iota(jnp.int32, (1, 128), 1)
     tail = jnp.zeros((1, 128), F32)
@@ -373,7 +386,7 @@
 
     def body(pair, carry):
         both = jnp.zeros((48, WIDE), F32)
-        for source in range(4):
+        for source in range(8):
             both = both + unpacked_pair(pair_of(source, pair, slice(0, 48)))
         e = exponent(jnp.max(jnp.abs(both), axis=0, keepdims=True))
         values = apart(rounded(both, e))
@@ -390,7 +403,7 @@
                 out[y, 2 * pair + k] = full.astype(jnp.int32).astype(I16)
         return carry
 
-    lax.fori_loop(0, 4, body, 0)
+    lax.fori_loop(0, 2, body, 0)
 
 
 def final_sum(blocks, loss, grad, gain, shift):
@@ -403,7 +416,7 @@
         part = jnp.zeros((16, 128), F32)
         vector = jnp.zeros((8, 128), F32)
         margin = jnp.zeros((1, 1), F32)
-        for z in range(8):
+        for z in range(4):
             q = blocks[pair, z].astype(jnp.int32)
             v = q.astype(F32)
             tail = q[16:24]
@@ -441,30 +454,32 @@
     beyond = [(i, (i + 2) % 8 if i % 2 else (i + 6) % 8) for i in range(8)]
     swap = [(0, 1), (1, 0)]
 
-    stats, bias, first, last, here = call(
-        stats_and_time,
-        [((64, 128), F32), ((8, C), F32), (strip, BF16), (strip, BF16)]
-        + [((2, 2 * TH, TW, C), BF16)],
-        [
-            pltpu.VMEM((C, C), F32),
-            pltpu.SMEM((1,), jnp.int32),
-            pltpu.SemaphoreType.DMA((6,)),
-        ],
+    stats, first, last, here = call(
+        statistics,
+        [((64, 128), F32), (strip, BF16), (strip, BF16), ((2, 2 * TH, TW, C), BF16)],
+        [pltpu.SemaphoreType.DMA((4,))],
         flops=10**7,
         nbytes=10**6,
-        far=range(6),
+        far=range(4),
         grant=57,
-    )(timesteps, fw, fl, noise_win[0], noise_lose[0], time_weight)
+    )(fw, fl, noise_win[0], noise_lose[0])
+    stats = lax.all_to_all(stats, ("x", "zl", "zh", "core"), 0, 0, tiled=True)
     top = lax.ppermute(last, rows, down)
     bottom = lax.ppermute(first, rows, up)
-    side, mine = call(
-        outer_column_and_tile,
-        [(strip, BF16), ((2, 2 * TH + 2, TW, C), BF16)],
-        flops=10**10,
+    (bias,) = call(
+        time_bias,
+        [((8, C), F32)],
+        [pltpu.SMEM((1,), jnp.int32), pltpu.VMEM((C, C), F32), pltpu.SemaphoreType.DMA((2,))],
+        flops=10**7,
         nbytes=10**6,
-    )(top, bottom, here)
-    stats, side, mine = lax.optimization_barrier((stats, side, mine))
-    stats = lax.all_to_all(stats, ("x", "zl", "zh", "core"), 0, 0, tiled=True)
+        far=(0, 1),
+    )(timesteps, time_weight)
+    moments, side, mine = call(
+        moments_and_tile,
+        [((8, C), F32), (strip, BF16), ((2, 2 * TH + 2, TW, C), BF16)],
+        flops=2 * 10**10,
+        nbytes=10**6,
+    )(stats, top, bottom, here)
     my_side = lax.ppermute(side, columns, outward)
     their_side = lax.ppermute(side, columns, beyond)
     theirs = lax.ppermute(mine, "core", swap)
@@ -485,7 +500,7 @@
         nbytes=10**7,
         far=range(6, 12),
     )(
-        stats, bias, mine, theirs, my_side, their_side, norm_gain, norm_shift, ref_gain, ref_shift,
+        moments, bias, mine, theirs, my_side, their_side, norm_gain, norm_shift, ref_gain, ref_shift,
         conv_weight, ref_weight,
     )
     other = lax.ppermute(small, "core", swap)
@@ -498,14 +513,14 @@
         nbytes=10**7,
     )(cols, cot)
     (blocks,) = call(
-        pack_blocks, [((4, 20, 48, 128), I16)], [pltpu.VMEM((4, 8, WIDE), F32)]
+        pack_blocks, [((8, 10, 48, 128), I16)], [pltpu.VMEM((2, 8, WIDE), F32)]
     )(blocks, small, other)
-    blocks = lax.all_to_all(blocks, "x", 0, 0, tiled=True)
-    (sums,) = call(chip_sum, [((8, 8, 24, 128), I16)])(blocks)
-    sums = lax.all_to_all(sums.reshape(64, 24, 128), ("y", "zl", "zh"), 0, 0, tiled=True)
+    blocks = lax.all_to_all(blocks, ("x", "zl"), 0, 0, tiled=True)
+    (sums,) = call(chip_sum, [((8, 4, 24, 128), I16)])(blocks)
+    sums = lax.all_to_all(sums.reshape(32, 24, 128), ("y", "zh"), 0, 0, tiled=True)
     loss, grad, gain, shift = call(
         final_sum, [((1, 1), F32), ((40, BLK), F32), ((C,), F32), ((C,), F32)]
-    )(sums.reshape(8, 8, 24, 128))
+    )(sums.reshape(8, 4, 24, 128))
     return loss.reshape(1), grad, gain, shift
 
 

time: 108 us -> 101 us (0.935)
  blocking collectives: 46 us -> 43 us
  waiting for transfers between devices: 7.13 us -> 5.13 us
  local copies, waits for them, and re-layouts: 2.64 us -> 1.03 us
    all_to_all x2, blocking collectives: 46 us -> 43 us  [the longest x1 21.8 us: local(): lax.all_to_all(sums.reshape(32, 24, 128), ('y', 'zh'), 0, 0, tiled=True)]
    ppermute x1, waiting for transfers between devices: 5.32 us -> 3.42 us  [local(): my_side = lax.ppermute(side, columns, outward)]
    unnamed x16, local copies, waits for them, and re-layouts: 2.64 us -> 1.03 us
    pallas_call x7 -> x8, Pallas kernels: 16.1 us -> 16.1 us  [run(): pl.pallas_call(kernel, out_shape=[jax.ShapeDtypeStruct(s, d) for s, d in...]
  transfers between devices with their start and end apart: 7 -> 7, of which waited for: 3 -> 3; matrix products, arithmetic and copies ran while one was open for 0% -> 0% of each run, Pallas kernels for 2% -> 3%
where the time goes in v5:
time: 101 us; the launch traced here: 100 us
  blocking collectives  43 us (43%)
  starting transfers between devices  33.6 us (33%)
  Pallas kernels  16.1 us (16%)
  waiting for transfers between devices  5.13 us (5%)
  between operations  1.47 us (1%)
  local copies, waits for them, and re-layouts  1.03 us (1%)
    all_to_all x1, blocking collectives, local(): lax.all_to_all(sums.reshape(32, 24, 128), ('y', 'zh'), 0, 0, tiled=True)  21.8 us
    all_to_all x1, blocking collectives, local(): blocks = lax.all_to_all(blocks, ('x', 'zl'), 0, 0, tiled=True)  21.2 us
    pallas_call x8, Pallas kernels, run(): pl.pallas_call(kernel, out_shape=[jax.ShapeDtypeStruct(s, d) for s, d in...  16.1 us
    all_to_all x1, starting transfers between devices, local(): stats = lax.all_to_all(stats, ('x', 'zl', 'zh', 'core'), 0, 0, tiled=True)  13.8 us
    ppermute x1, starting transfers between devices, local(): their_side = lax.ppermute(side, columns, beyond)  5.59 us
    ppermute x1, starting transfers between devices, local(): bottom = lax.ppermute(first, rows, up)  4.47 us
    ppermute x1, starting transfers between devices, local(): top = lax.ppermute(last, rows, down)  3.48 us
    ppermute x1, waiting for transfers between devices, local(): my_side = lax.ppermute(side, columns, outward)  3.42 us
  transfers between devices with their start and end apart: 7, of which 3 were waited for; matrix products, arithmetic and copies ran while one was open for 0% of the time, Pallas kernels for 3%

profile of v5, /device:TPU:8, one launch (start us, length us, event | category | flops | bytes accessed | tf_op | source)
XLA Modules:
  0.0 100.5 jit_solution(16797429614960731474)
XLA Ops:
  0.6 2.3 %shard_map.147 = (f32[64,128]{1,0:T(8,128)}, bf16[2,16,320]{2,1,0:T(8,128)(2,1)}, bf16[2,16,320]{2,1,0:T(8,128)(2,1)}, bf16[2,16,16,320]{3,2,1,0:T(8,128)(2,1)}) custom-call(bf16[8,16,320]{2,1,0:T(8,128)(2,1)} %bitcast.14, bf16[8,16,320]{2,1,0:T(8,128)(2,1)} %bitcast.15, bf16[8,16,320]{2,1,0:T(8,128)(2,1)} %bitcast.16, bf16[8,16,320]{2,1,0:T(8,128)(2,1)} %bitcast.17), custom_call_target="tpu_custom_call" | custom-call | flops 10000000 | bytes 1000000 | tf_op jit(solution)/shard_map/pallas_call | solution.py:32
  3.0 13.8 %all-to-all-start = ((f32[64,1,128]{2,1,0:T(1,128)}), f32[64,1,128]{2,1,0:T(1,128)S(1)}, u32[]{:S(2)}, u32[]{:S(2)}) async-start(f32[64,1,128]{2,1,0:T(1,128)} %bitcast.18), calls=%async_computation | async-start | bytes 65536 | tf_op jit(solution)/shard_map/all_to_all | solution.py:466
  16.8 3.5 %collective-permute-start = (bf16[2,16,320]{2,1,0:T(8,128)(2,1)}, bf16[2,16,320]{2,1,0:T(8,128)(2,1)S(1)}, u32[]{:S(2)}, u32[]{:S(2)}) collective-permute-start(bf16[2,16,320]{2,1,0:T(8,128)(2,1)} %get-tuple-element.19), channel_id=1, source_target_pairs={{0,8},{8,16},{16,24},{24,32},{32,40},{40,48},{48,56},{56,0},{1,9},... | collective-permute-start | bytes 61448 | tf_op jit(solution)/shard_map/ppermute | solution.py:467
  20.3 4.5 %collective-permute-start.1 = (bf16[2,16,320]{2,1,0:T(8,128)(2,1)}, bf16[2,16,320]{2,1,0:T(8,128)(2,1)S(1)}, u32[]{:S(2)}, u32[]{:S(2)}) collective-permute-start(bf16[2,16,320]{2,1,0:T(8,128)(2,1)} %get-tuple-element.20), channel_id=1, source_target_pairs={{8,0},{16,8},{24,16},{32,24},{40,32},{48,40},{56,48},{0,56},{9,1},... | collective-permute-start | bytes 61448 | tf_op jit(solution)/shard_map/ppermute | solution.py:468
  24.8 0.1 collective-permute-done.top
  24.8 1.6 %collective-permute-done.1.bottom = bf16[2,16,320]{2,1,0:T(8,128)(2,1)S(1)} collective-permute-done((bf16[2,16,320]{2,1,0:T(8,128)(2,1)}, bf16[2,16,320]{2,1,0:T(8,128)(2,1)S(1)}, u32[]{:S(2)}, u32[]{:S(2)}) %collective-permute-start.1) | collective-permute-done | bytes 20512 | tf_op jit(solution)/shard_map/ppermute | solution.py:468
  26.5 0.0 all-to-all-done
  26.5 0.0 copy-start.3
  26.5 1.0 copy-done.3
  27.5 0.0 copy-start
  27.5 0.0 copy-start.1
  27.5 0.0 copy-start.2
  27.5 0.0 copy-start.4
  27.5 0.0 copy-start.5
  27.5 0.0 copy-start.6
  27.5 0.0 copy-start.7
  27.5 0.4 shard_map.148
  27.9 2.2 %collective-permute-start.2 = (bf16[2,18,16,320]{3,2,1,0:T(8,128)(2,1)S(1)}, bf16[2,18,16,320]{3,2,1,0:T(8,128)(2,1)S(1)}, u32[]{:S(2)}, u32[]{:S(2)}) collective-permute-start(bf16[2,18,16,320]{3,2,1,0:T(8,128)(2,1)S(1)} %get-tuple-element.23.mine), channel_id=1, source_target_pairs={{0,1},{1,0},{2,3},{3,2},{4,5},{5,4},{6,7},{7,6},{8,9},{9,8},{10,11... | collective-permute-start | bytes 1105928 | tf_op jit(solution)/shard_map/ppermute | solution.py:485
  30.1 5.6 %collective-permute-start.4 = (bf16[2,16,320]{2,1,0:T(8,128)(2,1)S(1)}, bf16[2,16,320]{2,1,0:T(8,128)(2,1)S(1)}, u32[]{:S(2)}, u32[]{:S(2)}) collective-permute-start(bf16[2,16,320]{2,1,0:T(8,128)(2,1)S(1)} %get-tuple-element.24), channel_id=1, source_target_pairs={{0,6},{1,3},{2,0},{3,5},{4,2},{5,7},{6,4},{7,1},{8,14},{9,11},{10,... | collective-permute-start | bytes 61448 | tf_op jit(solution)/shard_map/ppermute | solution.py:484
  35.7 2.2 %collective-permute-start.3 = (bf16[2,16,320]{2,1,0:T(8,128)(2,1)S(1)}, bf16[2,16,320]{2,1,0:T(8,128)(2,1)S(1)}, u32[]{:S(2)}, u32[]{:S(2)}) collective-permute-start(bf16[2,16,320]{2,1,0:T(8,128)(2,1)S(1)} %get-tuple-element.24), channel_id=1, source_target_pairs={{0,7},{1,2},{2,1},{3,4},{4,3},{5,6},{6,5},{7,0},{8,15},{9,10},{10,... | collective-permute-start | bytes 61448 | tf_op jit(solution)/shard_map/ppermute | solution.py:483
  38.6 0.0 copy-done
  38.6 1.0 shard_map.149.bias
  39.5 0.0 collective-permute-done.4.their_side
  39.6 3.4 %collective-permute-done.3.my_side = bf16[2,16,320]{2,1,0:T(8,128)(2,1)S(1)} collective-permute-done((bf16[2,16,320]{2,1,0:T(8,128)(2,1)S(1)}, bf16[2,16,320]{2,1,0:T(8,128)(2,1)S(1)}, u32[]{:S(2)}, u32[]{:S(2)}) %collective-permute-start.3) | collective-permute-done | bytes 20512 | tf_op jit(solution)/shard_map/ppermute | solution.py:483
  43.0 0.0 collective-permute-done.2.theirs
  43.0 0.0 copy-done.1
  43.0 0.0 copy-done.2
  43.0 0.0 copy-done.4
  43.0 0.0 copy-done.5
  43.0 0.0 copy-done.6
  43.0 0.0 copy-done.7
  43.0 6.7 %shard_map.150 = (bf16[512,2880]{1,0:T(8,128)(2,1)S(1)}, bf16[512,320]{1,0:T(8,128)(2,1)S(1)}, f32[8,640]{1,0:T(8,128)S(1)}) custom-call(f32[8,320]{1,0:T(8,128)S(1)} %get-tuple-element.22.moments, f32[8,320]{1,0:T(8,128)S(1)} %shard_map.149.bias, bf16[2,18,16,320]{3,2,1,0:T(8,128)(2,1)S(1)} %get-tuple-element.23.mine, ...), custom_call_target="tpu_custom_call" | custom-call | flops 2000000000 | bytes 10000000 | tf_op jit(solution)/shard_map/pallas_call | solution.py:32
  49.7 1.9 %collective-permute-start.5 = (f32[8,640]{1,0:T(8,128)S(1)}, f32[8,640]{1,0:T(8,128)S(1)}, u32[]{:S(2)}, u32[]{:S(2)}) collective-permute-start(f32[8,640]{1,0:T(8,128)S(1)} %get-tuple-element.27.small), channel_id=1, source_target_pairs={{0,1},{1,0},{2,3},{3,2},{4,5},{5,4},{6,7},{7,6},{8,9},{9,8},{10,11... | collective-permute-start | bytes 61448 | tf_op jit(solution)/shard_map/ppermute | solution.py:506
  51.6 1.9 %shard_map.151.blocks = f32[32,48,320]{2,1,0:T(8,128)S(1)} custom-call(bf16[512,2880]{1,0:T(8,128)(2,1)S(1)} %get-tuple-element.25.cols, bf16[512,320]{1,0:T(8,128)(2,1)S(1)} %get-tuple-element.26.cot), custom_call_target="tpu_custom_call" | custom-call | flops 1000000000 | bytes 10000000 | tf_op jit(solution)/shard_map/pallas_call | solution.py:32
  53.6 0.0 collective-permute-done.5.other
  53.6 1.2 %shard_map.152 = s16[8,10,48,128]{3,2,1,0:T(8,128)(2,1)S(1)} custom-call(f32[32,48,320]{2,1,0:T(8,128)S(1)} %shard_map.151.blocks, f32[8,640]{1,0:T(8,128)S(1)} %get-tuple-element.27.small, f32[8,640]{1,0:T(8,128)S(1)} %collective-permute-done.5.other), custom_call_target="tpu_custom_call" | custom-call | tf_op jit(solution)/shard_map/pallas_call | solution.py:32
  54.7 21.2 %all_to_all.21.blocks = s16[8,10,48,128]{3,2,1,0:T(8,128)(2,1)S(1)} all-to-all(s16[8,10,48,128]{3,2,1,0:T(8,128)(2,1)S(1)} %shard_map.152), channel_id=1, replica_groups=mesh['y'=8,'x'=4,'zl'=2,'zh'=4,'core'=2] {'x','zl'}, dimensions={0} | all-to-all | bytes 1966080 | tf_op jit(solution)/shard_map/all_to_all | solution.py:518
  76.0 1.5 %shard_map.153 = s16[8,4,24,128]{3,2,1,0:T(8,128)(2,1)S(1)} custom-call(s16[8,10,48,128]{3,2,1,0:T(8,128)(2,1)S(1)} %all_to_all.21.blocks), custom_call_target="tpu_custom_call" | custom-call | tf_op jit(solution)/shard_map/pallas_call | solution.py:32
  77.5 21.8 %all_to_all.22 = s16[32,24,128]{2,1,0:T(8,128)(2,1)S(1)} all-to-all(s16[32,24,128]{2,1,0:T(8,128)(2,1)S(1)} %bitcast.11), channel_id=1, replica_groups=mesh['y'=8,'x'=4,'zl'=2,'zh'=4,'core'=2] {'y','zh'}, dimensions={0} | all-to-all | bytes 393216 | tf_op jit(solution)/shard_map/all_to_all | solution.py:520
  99.3 1.1 %shard_map.154 = (f32[1,1]{1,0:T(1,128)}, f32[40,45]{1,0:T(8,128)}, f32[320]{0:T(512)}, f32[320]{0:T(512)}) custom-call(s16[8,4,24,128]{3,2,1,0:T(8,128)(2,1)S(1)} %bitcast.12), custom_call_target="tpu_custom_call" | custom-call | tf_op jit(solution)/shard_map/pallas_call | solution.py:32
Async XLA Ops:
  3.0 23.5 %all-to-all-start = ((f32[64,1,128]{2,1,0:T(1,128)}), f32[64,1,128]{2,1,0:T(1,128)S(1)}, u32[]{:S(2)}, u32[]{:S(2)}) async-start(f32[64,1,128]{2,1,0:T(1,128)} %bitcast.18), calls=%async_computation | async-start | bytes 65536 | tf_op jit(solution)/shard_map/all_to_all | solution.py:466
  16.8 8.1 %collective-permute-start = (bf16[2,16,320]{2,1,0:T(8,128)(2,1)}, bf16[2,16,320]{2,1,0:T(8,128)(2,1)S(1)}, u32[]{:S(2)}, u32[]{:S(2)}) collective-permute-start(bf16[2,16,320]{2,1,0:T(8,128)(2,1)} %get-tuple-element.19), channel_id=1, source_target_pairs={{0,8},{8,16},{16,24},{24,32},{32,40},{40,48},{48,56},{56,0},{1,9},... | collective-permute-start | bytes 61448 | tf_op jit(solution)/shard_map/ppermute | solution.py:467
  20.3 6.2 %collective-permute-start.1 = (bf16[2,16,320]{2,1,0:T(8,128)(2,1)}, bf16[2,16,320]{2,1,0:T(8,128)(2,1)S(1)}, u32[]{:S(2)}, u32[]{:S(2)}) collective-permute-start(bf16[2,16,320]{2,1,0:T(8,128)(2,1)} %get-tuple-element.20), channel_id=1, source_target_pairs={{8,0},{16,8},{24,16},{32,24},{40,32},{48,40},{56,48},{0,56},{9,1},... | collective-permute-start | bytes 61448 | tf_op jit(solution)/shard_map/ppermute | solution.py:468
  26.5 1.0 copy-start.3
  27.5 11.1 %copy-start = (f32[320,320]{1,0:T(8,128)S(1)}, f32[320,320]{1,0:T(8,128)}, u32[]{:S(2)}) copy-start(f32[320,320]{1,0:T(8,128)} %time_weight.1) | copy-start | bytes 1228804
  27.5 15.5 %copy-start.1 = (bf16[9,320,320]{2,1,0:T(8,128)(2,1)S(1)}, bf16[9,320,320]{2,1,0:T(8,128)(2,1)}, u32[]{:S(2)}) copy-start(bf16[9,320,320]{2,1,0:T(8,128)(2,1)} %weight_far.1) | copy-start | bytes 5529604
  27.5 15.5 %copy-start.2 = (bf16[9,320,320]{2,1,0:T(8,128)(2,1)S(1)}, bf16[9,320,320]{2,1,0:T(8,128)(2,1)}, u32[]{:S(2)}) copy-start(bf16[9,320,320]{2,1,0:T(8,128)(2,1)} %ref_far.1) | copy-start | bytes 5529604
  27.5 15.5 %copy-start.4 = (f32[320]{0:T(512)S(1)}, f32[320]{0:T(512)}, u32[]{:S(2)}) copy-start(f32[320]{0:T(512)} %gain_far.1) | copy-start | bytes 3844
  27.5 15.5 %copy-start.5 = (f32[320]{0:T(512)S(1)}, f32[320]{0:T(512)}, u32[]{:S(2)}) copy-start(f32[320]{0:T(512)} %shift_far.1) | copy-start | bytes 3844
  27.5 15.5 %copy-start.6 = (f32[320]{0:T(512)S(1)}, f32[320]{0:T(512)}, u32[]{:S(2)}) copy-start(f32[320]{0:T(512)} %ref_gain_far.1) | copy-start | bytes 3844
  27.5 15.5 %copy-start.7 = (f32[320]{0:T(512)S(1)}, f32[320]{0:T(512)}, u32[]{:S(2)}) copy-start(f32[320]{0:T(512)} %ref_shift_far.1) | copy-start | bytes 3844
  27.9 15.0 %collective-permute-start.2 = (bf16[2,18,16,320]{3,2,1,0:T(8,128)(2,1)S(1)}, bf16[2,18,16,320]{3,2,1,0:T(8,128)(2,1)S(1)}, u32[]{:S(2)}, u32[]{:S(2)}) collective-permute-start(bf16[2,18,16,320]{3,2,1,0:T(8,128)(2,1)S(1)} %get-tuple-element.23.mine), channel_id=1, source_target_pairs={{0,1},{1,0},{2,3},{3,2},{4,5},{5,4},{6,7},{7,6},{8,9},{9,8},{10,11... | collective-permute-start | bytes 1105928 | tf_op jit(solution)/shard_map/ppermute | solution.py:485
  30.1 9.4 %collective-permute-start.4 = (bf16[2,16,320]{2,1,0:T(8,128)(2,1)S(1)}, bf16[2,16,320]{2,1,0:T(8,128)(2,1)S(1)}, u32[]{:S(2)}, u32[]{:S(2)}) collective-permute-start(bf16[2,16,320]{2,1,0:T(8,128)(2,1)S(1)} %get-tuple-element.24), channel_id=1, source_target_pairs={{0,6},{1,3},{2,0},{3,5},{4,2},{5,7},{6,4},{7,1},{8,14},{9,11},{10,... | collective-permute-start | bytes 61448 | tf_op jit(solution)/shard_map/ppermute | solution.py:484
  35.7 7.3 %collective-permute-start.3 = (bf16[2,16,320]{2,1,0:T(8,128)(2,1)S(1)}, bf16[2,16,320]{2,1,0:T(8,128)(2,1)S(1)}, u32[]{:S(2)}, u32[]{:S(2)}) collective-permute-start(bf16[2,16,320]{2,1,0:T(8,128)(2,1)S(1)} %get-tuple-element.24), channel_id=1, source_target_pairs={{0,7},{1,2},{2,1},{3,4},{4,3},{5,6},{6,5},{7,0},{8,15},{9,10},{10,... | collective-permute-start | bytes 61448 | tf_op jit(solution)/shard_map/ppermute | solution.py:483
  49.7 3.9 %collective-permute-start.5 = (f32[8,640]{1,0:T(8,128)S(1)}, f32[8,640]{1,0:T(8,128)S(1)}, u32[]{:S(2)}, u32[]{:S(2)}) collective-permute-start(f32[8,640]{1,0:T(8,128)S(1)} %get-tuple-element.27.small), channel_id=1, source_target_pairs={{0,1},{1,0},{2,3},{3,2},{4,5},{5,4},{6,7},{7,6},{8,9},{9,8},{10,11... | collective-permute-start | bytes 61448 | tf_op jit(solution)/shard_map/ppermute | solution.py:506

commit v6 on v5

--- a/solution.py
+++ b/solution.py
@@ -120,7 +120,7 @@
     return [4 * pair, 4 * pair + 1, 4 * pair + 2, 4 * pair + 3, 8 + pair]
 
 
-def statistics(fw, fl, nw, nl, stats, first, last, here, sems):
+def statistics(fw, fl, nw, nl, stats, first, last, edge, here, sems):
     copies = [
         pltpu.make_async_copy(fw, here.at[0, pl.ds(0, TH)], sems.at[0]),
         pltpu.make_async_copy(fl, here.at[1, pl.ds(0, TH)], sems.at[1]),
@@ -138,7 +138,8 @@
     for k in range(2):
         first[k] = here[k, 0]
         last[k] = here[k, TH - 1]
-        x = here[k, 0:TH].astype(F32).reshape(PIX, C)
+        field = here[k, 0:TH].astype(F32)
+        x = field.reshape(PIX, C)
         sums = jnp.sum(x, axis=0, keepdims=True)
         squares = jnp.sum(x * x, axis=0, keepdims=True)
         for j, part in enumerate((sums, squares)):
@@ -151,6 +152,12 @@
                 precision=HIGHEST,
                 preferred_element_type=F32,
             )
+        column = [
+            jnp.concatenate([field[r, col : col + 1] for r in range(TH)], axis=0)
+            for col in (0, TW - 1)
+        ]
+        column = jnp.where(lax.axis_index("core") == 0, column[0], column[1])
+        edge[k] = jnp.concatenate([column, jnp.zeros((8, C), F32)], axis=0).astype(BF16)
     stats[...] = jnp.broadcast_to(total[0:1], stats.shape)
     copies[2].wait()
     copies[3].wait()
@@ -175,9 +182,17 @@
     bias[...] = jnp.dot(gate, table[...], precision=HIGHEST, preferred_element_type=F32)
 
 
-def moments_and_tile(stats, top, bottom, here, moments, side, tile):
+def outer_column(top, bottom, edge, side):
     core = lax.axis_index("core")
-
+    for s in range(2):
+        above, below = top[s].astype(F32), bottom[s].astype(F32)
+        above = jnp.where(core == 0, above[0:1], above[TW - 1 : TW])
+        below = jnp.where(core == 0, below[0:1], below[TW - 1 : TW])
+        column = [above, edge[s].astype(F32)[0:TH], below, jnp.zeros((6, C), F32)]
+        side[s] = jnp.concatenate(column, axis=0).astype(BF16)
+
+
+def moments_and_tile(stats, top, bottom, side, here, moments, tile):
     total = jnp.broadcast_to(jnp.sum(stats[...], axis=0, keepdims=True), (8, 128))
     groups = lax.broadcasted_iota(jnp.int32, (128, C), 0)
     chans = lax.broadcasted_iota(jnp.int32, (128, C), 1)
@@ -204,17 +219,12 @@
         tile[s, 0] = top[s]
         tile[s, 1 : TH + 1] = here[s, 0:TH]
         tile[s, TH + 1] = bottom[s]
-        tile[s, TH + 2 :] = here[s, TH:]
-        x = [tile[s, r].astype(F32) for r in range(TH + 2)]
-        column = [
-            jnp.concatenate([v[col : col + 1] for v in x] + [jnp.zeros((6, C), F32)], axis=0)
-            for col in (0, TW - 1)
-        ]
-        side[s] = jnp.where(core == 0, column[0], column[1]).astype(BF16)
+        tile[s, TH + 2 : 2 * TH + 2] = here[s, TH:]
+        tile[s, 2 * TH + 2] = side[s]
 
 
 def forward(
-    moments, bias, mine, theirs, my_side, their_side, gain_far, shift_far, ref_gain_far, ref_shift_far,
+    moments, bias, mine, theirs, gain_far, shift_far, ref_gain_far, ref_shift_far,
     weight_far, ref_far, cols, cot_out, small, field, act, back, weight, ref_weight, gain, shift,
     ref_gain, ref_shift, sems,
 ):
@@ -234,14 +244,13 @@
     scales = [moments[2 * s + 1 : 2 * s + 2] for s in range(2)]
 
     tiles = (mine, theirs)
-    sides = (my_side, their_side)
     for w in range(2):
         for s in range(2):
             here, beside = tiles[w], tiles[1 - w]
             f = 2 * w + s
             field[f, :, TW + 2 :, :] = jnp.zeros((TH + 2, 22 - TW, C), F32)
             field[f, :, 1 : TW + 1, :] = here[s, 0 : TH + 2].astype(F32)
-            outer = sides[w][s].astype(F32)
+            outer = here[s, 2 * TH + 2].astype(F32)
             is_left = core == w
             for r in range(TH + 2):
                 near = beside[s, r].astype(F32)
@@ -451,12 +460,11 @@
     up = [((i + 1) % 8, i) for i in range(8)]
     down = [(i, (i + 1) % 8) for i in range(8)]
     outward = [(i, (i + 1) % 8 if i % 2 else (i + 7) % 8) for i in range(8)]
-    beyond = [(i, (i + 2) % 8 if i % 2 else (i + 6) % 8) for i in range(8)]
     swap = [(0, 1), (1, 0)]
 
-    stats, first, last, here = call(
+    stats, first, last, edge, here = call(
         statistics,
-        [((64, 128), F32), (strip, BF16), (strip, BF16), ((2, 2 * TH, TW, C), BF16)],
+        [((64, 128), F32)] + [(strip, BF16)] * 3 + [((2, 2 * TH, TW, C), BF16)],
         [pltpu.SemaphoreType.DMA((4,))],
         flops=10**7,
         nbytes=10**6,
@@ -474,14 +482,14 @@
         nbytes=10**6,
         far=(0, 1),
     )(timesteps, time_weight)
-    moments, side, mine = call(
+    (side,) = call(outer_column, [(strip, BF16)])(top, bottom, edge)
+    side = lax.ppermute(side, columns, outward)
+    moments, mine = call(
         moments_and_tile,
-        [((8, C), F32), (strip, BF16), ((2, 2 * TH + 2, TW, C), BF16)],
+        [((8, C), F32), ((2, 2 * TH + 3, TW, C), BF16)],
         flops=2 * 10**10,
         nbytes=10**6,
-    )(stats, top, bottom, here)
-    my_side = lax.ppermute(side, columns, outward)
-    their_side = lax.ppermute(side, columns, beyond)
+    )(stats, top, bottom, side, here)
     theirs = lax.ppermute(mine, "core", swap)
 
     cols, cot, small = call(
@@ -498,9 +506,9 @@
         + [pltpu.SemaphoreType.DMA((6,))],
         flops=2 * 10**9,
         nbytes=10**7,
-        far=range(6, 12),
+        far=range(4, 10),
     )(
-        moments, bias, mine, theirs, my_side, their_side, norm_gain, norm_shift, ref_gain, ref_shift,
+        moments, bias, mine, theirs, norm_gain, norm_shift, ref_gain, ref_shift,
         conv_weight, ref_weight,
     )
     other = lax.ppermute(small, "core", swap)

time: 101 us -> 101 us (level)
  starting transfers between devices: 33.6 us -> 30.4 us
  blocking collectives: 43 us -> 45.8 us
    ppermute x2 -> x1, starting transfers between devices: 7.77 us -> 4.21 us  [local(): side = lax.ppermute(side, columns, outward)]
    all_to_all x1, blocking collectives: 21.8 us -> 24.9 us  [local(): lax.all_to_all(sums.reshape(32, 24, 128), ('y', 'zh'), 0, 0, tiled=True)]
    ppermute x2 -> x1, waiting for transfers between devices: 3.42 us -> 3.04 us  [local(): side = lax.ppermute(side, columns, outward)]
    pallas_call x8 -> x9, Pallas kernels: 16.1 us -> 16.2 us  [run(): pl.pallas_call(kernel, out_shape=[jax.ShapeDtypeStruct(s, d) for s, d in...]
  transfers between devices with their start and end apart: 7 -> 6, of which waited for: 3 -> 4; matrix products, arithmetic and copies ran while one was open for 0% -> 0% of each run, Pallas kernels for 3% -> 3%
where the time goes in v6:
time: 101 us
  blocking collectives  45.8 us (45%)
  starting transfers between devices  30.4 us (30%)
  Pallas kernels  16.2 us (16%)
  waiting for transfers between devices  4.91 us (5%)
  local copies, waits for them, and re-layouts  1.77 us (2%)
  between operations  1.46 us (1%)
    all_to_all x1, blocking collectives, local(): lax.all_to_all(sums.reshape(32, 24, 128), ('y', 'zh'), 0, 0, tiled=True)  24.9 us
    all_to_all x1, blocking collectives, local(): blocks = lax.all_to_all(blocks, ('x', 'zl'), 0, 0, tiled=True)  20.9 us
    pallas_call x9, Pallas kernels, run(): pl.pallas_call(kernel, out_shape=[jax.ShapeDtypeStruct(s, d) for s, d in...  16.2 us
    all_to_all x1, starting transfers between devices, local(): stats = lax.all_to_all(stats, ('x', 'zl', 'zh', 'core'), 0, 0, tiled=True)  13.8 us
    ppermute x1, starting transfers between devices, local(): bottom = lax.ppermute(first, rows, up)  4.47 us
    ppermute x1, starting transfers between devices, local(): side = lax.ppermute(side, columns, outward)  4.21 us
    ppermute x1, starting transfers between devices, local(): top = lax.ppermute(last, rows, down)  3.48 us
    ppermute x1, waiting for transfers between devices, local(): side = lax.ppermute(side, columns, outward)  3.04 us
  transfers between devices with their start and end apart: 6, of which 4 were waited for; matrix products, arithmetic and copies ran while one was open for 0% of the time, Pallas kernels for 3%

profile of v6, /device:TPU:8, one launch (start us, length us, event | category | flops | bytes accessed | tf_op | source)
XLA Modules:
  0.0 100.6 jit_solution(8123978605545614095)
XLA Ops:
  0.6 2.4 %shard_map.147 = (f32[64,128]{1,0:T(8,128)}, bf16[2,16,320]{2,1,0:T(8,128)(2,1)}, bf16[2,16,320]{2,1,0:T(8,128)(2,1)}, bf16[2,16,320]{2,1,0:T(8,128)(2,1)}, bf16[2,16,16,320]{3,2,1,0:T(8,128)(2,1)}) custom-call(bf16[8,16,320]{2,1,0:T(8,128)(2,1)} %bitcast.14, bf16[8,16,320]{2,1,0:T(8,128)(2,1)} %bitcast.15, bf16[8,16,320]{2,1,0:T(8,128)(2,1)} %bitcast.16, ...), custom_call_target="tpu_custom_call" | custom-call | flops 10000000 | bytes 1000000 | tf_op jit(solution)/shard_map/pallas_call | solution.py:32
  3.0 13.8 %all-to-all-start = ((f32[64,1,128]{2,1,0:T(1,128)}), f32[64,1,128]{2,1,0:T(1,128)S(1)}, u32[]{:S(2)}, u32[]{:S(2)}) async-start(f32[64,1,128]{2,1,0:T(1,128)} %bitcast.18), calls=%async_computation | async-start | bytes 65536 | tf_op jit(solution)/shard_map/all_to_all | solution.py:474
  16.8 3.5 %collective-permute-start = (bf16[2,16,320]{2,1,0:T(8,128)(2,1)}, bf16[2,16,320]{2,1,0:T(8,128)(2,1)S(1)}, u32[]{:S(2)}, u32[]{:S(2)}) collective-permute-start(bf16[2,16,320]{2,1,0:T(8,128)(2,1)} %get-tuple-element.19), channel_id=1, source_target_pairs={{0,8},{8,16},{16,24},{24,32},{32,40},{40,48},{48,56},{56,0},{1,9},... | collective-permute-start | bytes 61448 | tf_op jit(solution)/shard_map/ppermute | solution.py:475
  20.3 4.5 %collective-permute-start.1 = (bf16[2,16,320]{2,1,0:T(8,128)(2,1)}, bf16[2,16,320]{2,1,0:T(8,128)(2,1)S(1)}, u32[]{:S(2)}, u32[]{:S(2)}) collective-permute-start(bf16[2,16,320]{2,1,0:T(8,128)(2,1)} %get-tuple-element.20), channel_id=1, source_target_pairs={{8,0},{16,8},{24,16},{32,24},{40,32},{48,40},{56,48},{0,56},{9,1},... | collective-permute-start | bytes 61448 | tf_op jit(solution)/shard_map/ppermute | solution.py:476
  24.8 0.1 collective-permute-done.top
  24.9 1.6 %collective-permute-done.1.bottom = bf16[2,16,320]{2,1,0:T(8,128)(2,1)S(1)} collective-permute-done((bf16[2,16,320]{2,1,0:T(8,128)(2,1)}, bf16[2,16,320]{2,1,0:T(8,128)(2,1)S(1)}, u32[]{:S(2)}, u32[]{:S(2)}) %collective-permute-start.1) | collective-permute-done | bytes 20512 | tf_op jit(solution)/shard_map/ppermute | solution.py:476
  26.5 0.0 copy-start.1
  26.5 0.7 copy-done.1
  27.3 4.2 %collective-permute-start.2 = (bf16[2,16,320]{2,1,0:T(8,128)(2,1)S(1)}, bf16[2,16,320]{2,1,0:T(8,128)(2,1)S(1)}, u32[]{:S(2)}, u32[]{:S(2)}) collective-permute-start(bf16[2,16,320]{2,1,0:T(8,128)(2,1)S(1)} %shard_map.148), channel_id=1, source_target_pairs={{0,7},{1,2},{2,1},{3,4},{4,3},{5,6},{6,5},{7,0},{8,15},{9,10},{10,... | collective-permute-start | bytes 61448 | tf_op jit(solution)/shard_map/ppermute | solution.py:486
  31.5 3.0 %collective-permute-done.2.side = bf16[2,16,320]{2,1,0:T(8,128)(2,1)S(1)} collective-permute-done((bf16[2,16,320]{2,1,0:T(8,128)(2,1)S(1)}, bf16[2,16,320]{2,1,0:T(8,128)(2,1)S(1)}, u32[]{:S(2)}, u32[]{:S(2)}) %collective-permute-start.2) | collective-permute-done | bytes 20512 | tf_op jit(solution)/shard_map/ppermute | solution.py:486
  34.5 0.0 all-to-all-done
  34.5 0.0 copy-start.4
  34.5 1.0 copy-done.4
  35.5 0.0 copy-start
  35.5 0.0 copy-start.2
  35.5 0.0 copy-start.3
  35.5 0.0 copy-start.5
  35.5 0.0 copy-start.6
  35.6 0.0 copy-start.7
  35.6 0.0 copy-start.8
  35.6 0.4 shard_map.149
  36.0 2.2 %collective-permute-start.3 = (bf16[2,19,16,320]{3,2,1,0:T(8,128)(2,1)S(1)}, bf16[2,19,16,320]{3,2,1,0:T(8,128)(2,1)S(1)}, u32[]{:S(2)}, u32[]{:S(2)}) collective-permute-start(bf16[2,19,16,320]{3,2,1,0:T(8,128)(2,1)S(1)} %get-tuple-element.24.mine), channel_id=1, source_target_pairs={{0,1},{1,0},{2,3},{3,2},{4,5},{5,4},{6,7},{7,6},{8,9},{9,8},{10,11... | collective-permute-start | bytes 1167368 | tf_op jit(solution)/shard_map/ppermute | solution.py:493
  38.8 0.0 copy-done
  38.8 1.0 shard_map.150.bias
  39.8 0.2 collective-permute-done.3.theirs
  40.0 0.0 copy-done.2
  40.0 0.0 copy-done.3
  40.0 0.0 copy-done.5
  40.0 0.0 copy-done.6
  40.0 0.0 copy-done.7
  40.0 0.0 copy-done.8
  40.0 6.7 %shard_map.151 = (bf16[512,2880]{1,0:T(8,128)(2,1)S(1)}, bf16[512,320]{1,0:T(8,128)(2,1)S(1)}, f32[8,640]{1,0:T(8,128)S(1)}) custom-call(f32[8,320]{1,0:T(8,128)S(1)} %get-tuple-element.23.moments, f32[8,320]{1,0:T(8,128)S(1)} %shard_map.150.bias, bf16[2,19,16,320]{3,2,1,0:T(8,128)(2,1)S(1)} %get-tuple-element.24.mine, ...), custom_call_target="tpu_custom_call" | custom-call | flops 2000000000 | bytes 10000000 | tf_op jit(solution)/shard_map/pallas_call | solution.py:32
  46.7 2.3 %collective-permute-start.4 = (f32[8,640]{1,0:T(8,128)S(1)}, f32[8,640]{1,0:T(8,128)S(1)}, u32[]{:S(2)}, u32[]{:S(2)}) collective-permute-start(f32[8,640]{1,0:T(8,128)S(1)} %get-tuple-element.27.small), channel_id=1, source_target_pairs={{0,1},{1,0},{2,3},{3,2},{4,5},{5,4},{6,7},{7,6},{8,9},{9,8},{10,11... | collective-permute-start | bytes 61448 | tf_op jit(solution)/shard_map/ppermute | solution.py:514
  49.0 1.9 %shard_map.152.blocks = f32[32,48,320]{2,1,0:T(8,128)S(1)} custom-call(bf16[512,2880]{1,0:T(8,128)(2,1)S(1)} %get-tuple-element.25.cols, bf16[512,320]{1,0:T(8,128)(2,1)S(1)} %get-tuple-element.26.cot), custom_call_target="tpu_custom_call" | custom-call | flops 1000000000 | bytes 10000000 | tf_op jit(solution)/shard_map/pallas_call | solution.py:32
  50.9 0.0 collective-permute-done.4.other
  50.9 1.2 %shard_map.153 = s16[8,10,48,128]{3,2,1,0:T(8,128)(2,1)S(1)} custom-call(f32[32,48,320]{2,1,0:T(8,128)S(1)} %shard_map.152.blocks, f32[8,640]{1,0:T(8,128)S(1)} %get-tuple-element.27.small, f32[8,640]{1,0:T(8,128)S(1)} %collective-permute-done.4.other), custom_call_target="tpu_custom_call" | custom-call | tf_op jit(solution)/shard_map/pallas_call | solution.py:32
  52.1 20.9 %all_to_all.21.blocks = s16[8,10,48,128]{3,2,1,0:T(8,128)(2,1)S(1)} all-to-all(s16[8,10,48,128]{3,2,1,0:T(8,128)(2,1)S(1)} %shard_map.153), channel_id=1, replica_groups=mesh['y'=8,'x'=4,'zl'=2,'zh'=4,'core'=2] {'x','zl'}, dimensions={0} | all-to-all | bytes 1966080 | tf_op jit(solution)/shard_map/all_to_all | solution.py:526
  73.0 1.5 %shard_map.154 = s16[8,4,24,128]{3,2,1,0:T(8,128)(2,1)S(1)} custom-call(s16[8,10,48,128]{3,2,1,0:T(8,128)(2,1)S(1)} %all_to_all.21.blocks), custom_call_target="tpu_custom_call" | custom-call | tf_op jit(solution)/shard_map/pallas_call | solution.py:32
  74.5 24.9 %all_to_all.22 = s16[32,24,128]{2,1,0:T(8,128)(2,1)S(1)} all-to-all(s16[32,24,128]{2,1,0:T(8,128)(2,1)S(1)} %bitcast.11), channel_id=1, replica_groups=mesh['y'=8,'x'=4,'zl'=2,'zh'=4,'core'=2] {'y','zh'}, dimensions={0} | all-to-all | bytes 393216 | tf_op jit(solution)/shard_map/all_to_all | solution.py:528
  99.4 1.1 %shard_map.155 = (f32[1,1]{1,0:T(1,128)}, f32[40,45]{1,0:T(8,128)}, f32[320]{0:T(512)}, f32[320]{0:T(512)}) custom-call(s16[8,4,24,128]{3,2,1,0:T(8,128)(2,1)S(1)} %bitcast.12), custom_call_target="tpu_custom_call" | custom-call | tf_op jit(solution)/shard_map/pallas_call | solution.py:32
  (1 shorter events, 0.0 us)
Async XLA Ops:
  3.0 31.5 %all-to-all-start = ((f32[64,1,128]{2,1,0:T(1,128)}), f32[64,1,128]{2,1,0:T(1,128)S(1)}, u32[]{:S(2)}, u32[]{:S(2)}) async-start(f32[64,1,128]{2,1,0:T(1,128)} %bitcast.18), calls=%async_computation | async-start | bytes 65536 | tf_op jit(solution)/shard_map/all_to_all | solution.py:474
  16.8 8.1 %collective-permute-start = (bf16[2,16,320]{2,1,0:T(8,128)(2,1)}, bf16[2,16,320]{2,1,0:T(8,128)(2,1)S(1)}, u32[]{:S(2)}, u32[]{:S(2)}) collective-permute-start(bf16[2,16,320]{2,1,0:T(8,128)(2,1)} %get-tuple-element.19), channel_id=1, source_target_pairs={{0,8},{8,16},{16,24},{24,32},{32,40},{40,48},{48,56},{56,0},{1,9},... | collective-permute-start | bytes 61448 | tf_op jit(solution)/shard_map/ppermute | solution.py:475
  20.3 6.2 %collective-permute-start.1 = (bf16[2,16,320]{2,1,0:T(8,128)(2,1)}, bf16[2,16,320]{2,1,0:T(8,128)(2,1)S(1)}, u32[]{:S(2)}, u32[]{:S(2)}) collective-permute-start(bf16[2,16,320]{2,1,0:T(8,128)(2,1)} %get-tuple-element.20), channel_id=1, source_target_pairs={{8,0},{16,8},{24,16},{32,24},{40,32},{48,40},{56,48},{0,56},{9,1},... | collective-permute-start | bytes 61448 | tf_op jit(solution)/shard_map/ppermute | solution.py:476
  26.5 0.7 copy-start.1
  27.3 7.3 %collective-permute-start.2 = (bf16[2,16,320]{2,1,0:T(8,128)(2,1)S(1)}, bf16[2,16,320]{2,1,0:T(8,128)(2,1)S(1)}, u32[]{:S(2)}, u32[]{:S(2)}) collective-permute-start(bf16[2,16,320]{2,1,0:T(8,128)(2,1)S(1)} %shard_map.148), channel_id=1, source_target_pairs={{0,7},{1,2},{2,1},{3,4},{4,3},{5,6},{6,5},{7,0},{8,15},{9,10},{10,... | collective-permute-start | bytes 61448 | tf_op jit(solution)/shard_map/ppermute | solution.py:486
  34.5 1.0 copy-start.4
  35.5 3.3 %copy-start = (f32[320,320]{1,0:T(8,128)S(1)}, f32[320,320]{1,0:T(8,128)}, u32[]{:S(2)}) copy-start(f32[320,320]{1,0:T(8,128)} %time_weight.1) | copy-start | bytes 1228804
  35.5 4.4 %copy-start.2 = (bf16[9,320,320]{2,1,0:T(8,128)(2,1)S(1)}, bf16[9,320,320]{2,1,0:T(8,128)(2,1)}, u32[]{:S(2)}) copy-start(bf16[9,320,320]{2,1,0:T(8,128)(2,1)} %weight_far.1) | copy-start | bytes 5529604
  35.5 4.4 %copy-start.3 = (bf16[9,320,320]{2,1,0:T(8,128)(2,1)S(1)}, bf16[9,320,320]{2,1,0:T(8,128)(2,1)}, u32[]{:S(2)}) copy-start(bf16[9,320,320]{2,1,0:T(8,128)(2,1)} %ref_far.1) | copy-start | bytes 5529604
  35.5 4.4 %copy-start.5 = (f32[320]{0:T(512)S(1)}, f32[320]{0:T(512)}, u32[]{:S(2)}) copy-start(f32[320]{0:T(512)} %gain_far.1) | copy-start | bytes 3844
  35.5 4.4 %copy-start.6 = (f32[320]{0:T(512)S(1)}, f32[320]{0:T(512)}, u32[]{:S(2)}) copy-start(f32[320]{0:T(512)} %shift_far.1) | copy-start | bytes 3844
  35.6 4.4 %copy-start.7 = (f32[320]{0:T(512)S(1)}, f32[320]{0:T(512)}, u32[]{:S(2)}) copy-start(f32[320]{0:T(512)} %ref_gain_far.1) | copy-start | bytes 3844
  35.6 4.4 %copy-start.8 = (f32[320]{0:T(512)S(1)}, f32[320]{0:T(512)}, u32[]{:S(2)}) copy-start(f32[320]{0:T(512)} %ref_shift_far.1) | copy-start | bytes 3844
  36.0 4.0 %collective-permute-start.3 = (bf16[2,19,16,320]{3,2,1,0:T(8,128)(2,1)S(1)}, bf16[2,19,16,320]{3,2,1,0:T(8,128)(2,1)S(1)}, u32[]{:S(2)}, u32[]{:S(2)}) collective-permute-start(bf16[2,19,16,320]{3,2,1,0:T(8,128)(2,1)S(1)} %get-tuple-element.24.mine), channel_id=1, source_target_pairs={{0,1},{1,0},{2,3},{3,2},{4,5},{5,4},{6,7},{7,6},{8,9},{9,8},{10,11... | collective-permute-start | bytes 1167368 | tf_op jit(solution)/shard_map/ppermute | solution.py:493
  46.7 4.2 %collective-permute-start.4 = (f32[8,640]{1,0:T(8,128)S(1)}, f32[8,640]{1,0:T(8,128)S(1)}, u32[]{:S(2)}, u32[]{:S(2)}) collective-permute-start(f32[8,640]{1,0:T(8,128)S(1)} %get-tuple-element.27.small), channel_id=1, source_target_pairs={{0,1},{1,0},{2,3},{3,2},{4,5},{5,4},{6,7},{7,6},{8,9},{9,8},{10,11... | collective-permute-start | bytes 61448 | tf_op jit(solution)/shard_map/ppermute | solution.py:514

commit v7 on v6

--- a/solution.py
+++ b/solution.py
@@ -120,7 +120,18 @@
     return [4 * pair, 4 * pair + 1, 4 * pair + 2, 4 * pair + 3, 8 + pair]
 
 
-def statistics(fw, fl, nw, nl, stats, first, last, edge, here, sems):
+def edge_rows(fw, fl, first, last, sems):
+    copies = []
+    for k, ref in enumerate((fw, fl)):
+        copies.append(pltpu.make_async_copy(ref.at[0], first.at[k], sems.at[2 * k]))
+        copies.append(pltpu.make_async_copy(ref.at[TH - 1], last.at[k], sems.at[2 * k + 1]))
+    for copy in copies:
+        copy.start()
+    for copy in copies:
+        copy.wait()
+
+
+def statistics(fw, fl, nw, nl, stats, edge, here, sems):
     copies = [
         pltpu.make_async_copy(fw, here.at[0, pl.ds(0, TH)], sems.at[0]),
         pltpu.make_async_copy(fl, here.at[1, pl.ds(0, TH)], sems.at[1]),
@@ -136,8 +147,6 @@
     lanes = lax.broadcasted_iota(jnp.int32, (C, 128), 1)
     size = C // GROUPS
     for k in range(2):
-        first[k] = here[k, 0]
-        last[k] = here[k, TH - 1]
         field = here[k, 0:TH].astype(F32)
         x = field.reshape(PIX, C)
         sums = jnp.sum(x, axis=0, keepdims=True)
@@ -192,40 +201,27 @@
         side[s] = jnp.concatenate(column, axis=0).astype(BF16)
 
 
-def moments_and_tile(stats, top, bottom, side, here, moments, tile):
-    total = jnp.broadcast_to(jnp.sum(stats[...], axis=0, keepdims=True), (8, 128))
-    groups = lax.broadcasted_iota(jnp.int32, (128, C), 0)
-    chans = lax.broadcasted_iota(jnp.int32, (128, C), 1)
-    size = C // GROUPS
-    entries = float(PIXELS * size)
-
-    def by_channel(k):
-        group = groups - GROUPS * k
-        member = (group >= 0) & (group < GROUPS)
-        member = member & (chans >= group * size) & (chans < group * size + size)
-        spread = jnp.dot(total, member.astype(F32), precision=HIGHEST, preferred_element_type=F32)
-        return spread[0:1] / entries
-
-    means, scales = [], []
-    for s in range(2):
-        mean, square = by_channel(2 * s), by_channel(2 * s + 1)
-        means.append(mean)
-        scales.append(lax.rsqrt(square - mean * mean + 1e-05))
-    moments[...] = jnp.concatenate(
-        [means[0], scales[0], means[1], scales[1], jnp.zeros((4, C), F32)], axis=0
-    )
-
+def sums_and_tile(stats, top, bottom, side, here, totals, tile):
+    total = jnp.sum(stats[...], axis=0, keepdims=True)
+    totals[...] = jnp.broadcast_to(total, (8, 128))
+    high = total.astype(BF16).astype(F32)
+    middle = (total - high).astype(BF16).astype(F32)
+    low = total - high - middle
+    parts = jnp.concatenate([high, middle, low, jnp.zeros((3, 128), F32)], axis=0)
+    parts = jnp.concatenate([parts, jnp.zeros((6, C - 128), F32)], axis=1)
+    column = side[0].astype(F32)[0 : TH + 2]
+    tile[0, 2 * TH + 2] = jnp.concatenate([column, parts], axis=0).astype(BF16)
+    tile[1, 2 * TH + 2] = side[1]
     for s in range(2):
         tile[s, 0] = top[s]
         tile[s, 1 : TH + 1] = here[s, 0:TH]
         tile[s, TH + 1] = bottom[s]
         tile[s, TH + 2 : 2 * TH + 2] = here[s, TH:]
-        tile[s, 2 * TH + 2] = side[s]
 
 
 def forward(
-    moments, bias, mine, theirs, gain_far, shift_far, ref_gain_far, ref_shift_far,
-    weight_far, ref_far, cols, cot_out, small, field, act, back, weight, ref_weight, gain, shift,
+    totals, bias, mine, theirs, gain_far, shift_far, ref_gain_far, ref_shift_far,
+    weight_far, ref_far, cols, cot_out, small, field, act, back, slope, shifted, weight, ref_weight, gain, shift,
     ref_gain, ref_shift, sems,
 ):
     pairs = [
@@ -240,8 +236,25 @@
     chip_at = 2 * lax.axis_index("zh")
     col_at = (chip_at + core, chip_at + 1 - core)
 
-    means = [moments[2 * s : 2 * s + 1] for s in range(2)]
-    scales = [moments[2 * s + 1 : 2 * s + 2] for s in range(2)]
+    parts = theirs[0, 2 * TH + 2].astype(F32)[TH + 2 : TH + 5, 0:128]
+    total = totals[...] + ((parts[0:1] + parts[1:2]) + parts[2:3])
+    groups = lax.broadcasted_iota(jnp.int32, (128, C), 0)
+    chans = lax.broadcasted_iota(jnp.int32, (128, C), 1)
+    size = C // GROUPS
+    entries = float(PIXELS * size)
+
+    def by_channel(k):
+        group = groups - GROUPS * k
+        member = (group >= 0) & (group < GROUPS)
+        member = member & (chans >= group * size) & (chans < group * size + size)
+        spread = jnp.dot(total, member.astype(F32), precision=HIGHEST, preferred_element_type=F32)
+        return spread[0:1] / entries
+
+    means, scales = [], []
+    for s in range(2):
+        mean, square = by_channel(2 * s), by_channel(2 * s + 1)
+        means.append(mean)
+        scales.append(lax.rsqrt(square - mean * mean + 1e-05))
 
     tiles = (mine, theirs)
     for w in range(2):
@@ -249,11 +262,11 @@
             here, beside = tiles[w], tiles[1 - w]
             f = 2 * w + s
             field[f, :, TW + 2 :, :] = jnp.zeros((TH + 2, 22 - TW, C), F32)
-            field[f, :, 1 : TW + 1, :] = here[s, 0 : TH + 2].astype(F32)
-            outer = here[s, 2 * TH + 2].astype(F32)
+            field[f, :, 1 : TW + 1, :] = (here[s, 0 : TH + 2].astype(F32) - means[s]) * scales[s]
+            outer = (here[s, 2 * TH + 2].astype(F32) - means[s]) * scales[s]
             is_left = core == w
             for r in range(TH + 2):
-                near = beside[s, r].astype(F32)
+                near = (beside[s, r].astype(F32) - means[s]) * scales[s]
                 out = outer[r : r + 1]
                 field[f, r, 0:1, :] = jnp.where(is_left, out, near[TW - 1 : TW])
                 field[f, r, TW + 1 : TW + 2, :] = jnp.where(is_left, near[0:1], out)
@@ -271,19 +284,21 @@
             return inside[w] & (row_at < 7)
         return inside[w]
 
-    def pre_act(f, r, g, b):
-        normed = (field[f, r] - means[f % 2]) * scales[f % 2]
-        return normed, normed * g + b
-
-    def columns_of(fields, g, b):
+    def columns_of(fields, g, b, slope=None):
         for f in fields:
             for r in range(TH + 2):
-                _, pre = pre_act(f, r, g, b)
-                act[r] = jnp.where(valid(f // 2, r), pre * jax.nn.sigmoid(pre), 0.0)
-            for t in range(TAPS):
-                a, c = t // 3, t % 3
-                piece = act[a : a + TH, c : c + TW, :].reshape(PIX, C).astype(BF16)
-                cols[f * PIX : (f + 1) * PIX, C * t : C * (t + 1)] = piece
+                pre = field[f, r] * g + b
+                gate = jax.nn.sigmoid(pre)
+                value = pre * gate
+                act[r] = jnp.where(valid(f // 2, r), value, 0.0)
+                if slope is not None and f < 2:
+                    slope[f, r] = jnp.where(valid(0, r), gate + value * (1.0 - gate), 0.0)
+                for c in range(3):
+                    piece = act[r, c : c + TW, :].astype(BF16)
+                    for a in range(3):
+                        if 0 <= r - a < TH:
+                            at, t = f * PIX + TW * (r - a), 3 * a + c
+                            cols[at : at + TW, C * t : C * (t + 1)] = piece
 
     def base(f):
         tile, s = tiles[f // 2], f % 2
@@ -309,7 +324,7 @@
     resid = residual((0, 1), ref_weight)
     margin = -signed_squares(resid)
     g, b = gain[...].reshape(1, C), shift[...].reshape(1, C) + time_row
-    columns_of((0, 1, 2, 3), g, b)
+    columns_of((0, 1, 2, 3), g, b, slope)
     copies[5].wait()
     resid = residual((0, 1, 2, 3), weight)
     margin = margin + signed_squares(resid)
@@ -318,22 +333,21 @@
 
     cot = cot_out[0 : 2 * PIX]
     back[...] = jnp.zeros_like(back)
-    for t in range(TAPS):
-        a, c = t // 3, t % 3
-        term = lax.dot_general(
-            cot, weight[t], (((1,), (1,)), ((), ())), preferred_element_type=F32
-        )
-        for s in range(2):
-            back[s, a : a + TH, c : c + TW, :] += term[s * PIX : (s + 1) * PIX].reshape(TH, TW, C)
+    for c in range(3):
+        shifted[...] = jnp.zeros_like(shifted)
+        for a in range(3):
+            term = lax.dot_general(
+                cot, weight[3 * a + c], (((1,), (1,)), ((), ())), preferred_element_type=F32
+            )
+            for s in range(2):
+                shifted[s, a : a + TH] += term[s * PIX : (s + 1) * PIX].reshape(TH, TW, C)
+        back[:, :, c : c + TW, :] += shifted[...]
     gains = jnp.zeros((24, C), F32)
     shifts = jnp.zeros((24, C), F32)
     for s in range(2):
         for r in range(TH + 2):
-            normed, pre = pre_act(s, r, g, b)
-            gate = jax.nn.sigmoid(pre)
-            slope = gate * (1.0 + pre * (1.0 - gate))
-            dpre = jnp.where(valid(0, r), back[s, r] * slope, 0.0)
-            gains = gains + dpre * normed
+            dpre = back[s, r] * slope[s, r]
+            gains = gains + dpre * field[s, r]
             shifts = shifts + dpre
     gains = jnp.sum(gains, axis=0, keepdims=True)
     shifts = jnp.sum(shifts, axis=0, keepdims=True)
@@ -462,18 +476,25 @@
     outward = [(i, (i + 1) % 8 if i % 2 else (i + 7) % 8) for i in range(8)]
     swap = [(0, 1), (1, 0)]
 
-    stats, first, last, edge, here = call(
+    first, last = call(
+        edge_rows,
+        [(strip, BF16), (strip, BF16)],
+        [pltpu.SemaphoreType.DMA((4,))],
+        far=(0, 1),
+        grant=57,
+    )(fw, fl)
+    top = lax.ppermute(last, rows, down)
+    bottom = lax.ppermute(first, rows, up)
+    stats, edge, here = call(
         statistics,
-        [((64, 128), F32)] + [(strip, BF16)] * 3 + [((2, 2 * TH, TW, C), BF16)],
+        [((32, 128), F32), (strip, BF16), ((2, 2 * TH, TW, C), BF16)],
         [pltpu.SemaphoreType.DMA((4,))],
         flops=10**7,
         nbytes=10**6,
         far=range(4),
         grant=57,
     )(fw, fl, noise_win[0], noise_lose[0])
-    stats = lax.all_to_all(stats, ("x", "zl", "zh", "core"), 0, 0, tiled=True)
-    top = lax.ppermute(last, rows, down)
-    bottom = lax.ppermute(first, rows, up)
+    stats = lax.all_to_all(stats, ("x", "zl", "zh"), 0, 0, tiled=True)
     (bias,) = call(
         time_bias,
         [((8, C), F32)],
@@ -484,9 +505,9 @@
     )(timesteps, time_weight)
     (side,) = call(outer_column, [(strip, BF16)])(top, bottom, edge)
     side = lax.ppermute(side, columns, outward)
-    moments, mine = call(
-        moments_and_tile,
-        [((8, C), F32), ((2, 2 * TH + 3, TW, C), BF16)],
+    totals, mine = call(
+        sums_and_tile,
+        [((8, 128), F32), ((2, 2 * TH + 3, TW, C), BF16)],
         flops=2 * 10**10,
         nbytes=10**6,
     )(stats, top, bottom, side, here)
@@ -499,6 +520,8 @@
             pltpu.VMEM((4, TH + 2, 24, C), F32),
             pltpu.VMEM((TH + 2, 24, C), F32),
             pltpu.VMEM((2, TH + 2, 24, C), F32),
+            pltpu.VMEM((2, TH + 2, 24, C), F32),
+            pltpu.VMEM((2, TH + 2, TW, C), F32),
             pltpu.VMEM((TAPS, C, C), BF16),
             pltpu.VMEM((TAPS, C, C), BF16),
         ]
@@ -508,7 +531,7 @@
         nbytes=10**7,
         far=range(4, 10),
     )(
-        moments, bias, mine, theirs, norm_gain, norm_shift, ref_gain, ref_shift,
+        totals, bias, mine, theirs, norm_gain, norm_shift, ref_gain, ref_shift,
         conv_weight, ref_weight,
     )
     other = lax.ppermute(small, "core", swap)

time: 101 us -> 97.2 us (0.962)
  blocking collectives: 45.8 us -> 43 us
  starting transfers between devices: 30.4 us -> 28.5 us
    all_to_all x1, waiting for transfers between devices: 0.01 us -> 4.75 us  [local(): stats = lax.all_to_all(stats, ('x', 'zl', 'zh'), 0, 0, tiled=True)]
    ppermute x1, waiting for transfers between devices: 3.04 us -> 0.01 us  [local(): side = lax.ppermute(side, columns, outward)]
    all_to_all x1, starting transfers between devices: 13.8 us -> 11.5 us  [local(): stats = lax.all_to_all(stats, ('x', 'zl', 'zh'), 0, 0, tiled=True)]
    ppermute x1, waiting for transfers between devices: 1.62 us -> 0.01 us  [local(): bottom = lax.ppermute(first, rows, up)]
    all_to_all x1, blocking collectives: 20.9 us -> 19.3 us  [local(): blocks = lax.all_to_all(blocks, ('x', 'zl'), 0, 0, tiled=True)]
    all_to_all x1, blocking collectives: 24.9 us -> 23.7 us  [local(): lax.all_to_all(sums.reshape(32, 24, 128), ('y', 'zh'), 0, 0, tiled=True)]
    pallas_call x9 -> x10, Pallas kernels: 16.2 us -> 17.1 us  [run(): pl.pallas_call(kernel, out_shape=[jax.ShapeDtypeStruct(s, d) for s, d in...]
  transfers between devices with their start and end apart: 6 -> 6, of which waited for: 4 -> 2; matrix products, arithmetic and copies ran while one was open for 0% -> 0% of each run, Pallas kernels for 3% -> 5%
where the time goes in v7:
time: 97.2 us; the launch traced here: 96.7 us
  blocking collectives  43 us (44%)
  starting transfers between devices  28.5 us (29%)
  Pallas kernels  17.1 us (18%)
  waiting for transfers between devices  4.91 us (5%)
  local copies, waits for them, and re-layouts  1.76 us (2%)
  between operations  1.49 us (2%)
    all_to_all x1, blocking collectives, local(): lax.all_to_all(sums.reshape(32, 24, 128), ('y', 'zh'), 0, 0, tiled=True)  23.7 us
    all_to_all x1, blocking collectives, local(): blocks = lax.all_to_all(blocks, ('x', 'zl'), 0, 0, tiled=True)  19.3 us
    pallas_call x10, Pallas kernels, run(): pl.pallas_call(kernel, out_shape=[jax.ShapeDtypeStruct(s, d) for s, d in...  17.1 us
    all_to_all x1, starting transfers between devices, local(): stats = lax.all_to_all(stats, ('x', 'zl', 'zh'), 0, 0, tiled=True)  11.5 us
    all_to_all x1, waiting for transfers between devices, local(): stats = lax.all_to_all(stats, ('x', 'zl', 'zh'), 0, 0, tiled=True)  4.75 us
    ppermute x1, starting transfers between devices, local(): top = lax.ppermute(last, rows, down)  4.28 us
    ppermute x1, starting transfers between devices, local(): side = lax.ppermute(side, columns, outward)  4.13 us
    ppermute x1, starting transfers between devices, local(): bottom = lax.ppermute(first, rows, up)  4.11 us
  transfers between devices with their start and end apart: 6, of which 2 were waited for; matrix products, arithmetic and copies ran while one was open for 0% of the time, Pallas kernels for 5%

profile of v7, /device:TPU:8, one launch (start us, length us, event | category | flops | bytes accessed | tf_op | source)
XLA Modules:
  0.0 96.7 jit_solution(1058155718407310550)
XLA Ops:
  0.6 1.4 %shard_map.148 = (bf16[2,16,320]{2,1,0:T(8,128)(2,1)}, bf16[2,16,320]{2,1,0:T(8,128)(2,1)}) custom-call(bf16[8,16,320]{2,1,0:T(8,128)(2,1)} %bitcast.14, bf16[8,16,320]{2,1,0:T(8,128)(2,1)} %bitcast.16), custom_call_target="tpu_custom_call" | custom-call | tf_op jit(solution)/shard_map/pallas_call | solution.py:32
  2.0 4.3 %collective-permute-start = (bf16[2,16,320]{2,1,0:T(8,128)(2,1)}, bf16[2,16,320]{2,1,0:T(8,128)(2,1)S(1)}, u32[]{:S(2)}, u32[]{:S(2)}) collective-permute-start(bf16[2,16,320]{2,1,0:T(8,128)(2,1)} %get-tuple-element.19), channel_id=1, source_target_pairs={{0,8},{8,16},{16,24},{24,32},{32,40},{40,48},{48,56},{56,0},{1,9},... | collective-permute-start | bytes 61448 | tf_op jit(solution)/shard_map/ppermute | solution.py:486
  6.3 4.1 %collective-permute-start.1 = (bf16[2,16,320]{2,1,0:T(8,128)(2,1)}, bf16[2,16,320]{2,1,0:T(8,128)(2,1)S(1)}, u32[]{:S(2)}, u32[]{:S(2)}) collective-permute-start(bf16[2,16,320]{2,1,0:T(8,128)(2,1)} %get-tuple-element.20), channel_id=1, source_target_pairs={{8,0},{16,8},{24,16},{32,24},{40,32},{48,40},{56,48},{0,56},{9,1},... | collective-permute-start | bytes 61448 | tf_op jit(solution)/shard_map/ppermute | solution.py:487
  10.5 2.4 %shard_map.147 = (f32[32,128]{1,0:T(8,128)}, bf16[2,16,320]{2,1,0:T(8,128)(2,1)}, bf16[2,16,16,320]{3,2,1,0:T(8,128)(2,1)}) custom-call(bf16[8,16,320]{2,1,0:T(8,128)(2,1)} %bitcast.15, bf16[8,16,320]{2,1,0:T(8,128)(2,1)} %bitcast.17, bf16[8,16,320]{2,1,0:T(8,128)(2,1)} %bitcast.18, bf16[8,16,320]{2,1,0:T(8,128)(2,1)} %bitcast.19), custom_call_target="tpu_custom_call" | custom-call | flops 10000000 | bytes 1000000 | tf_op jit(solution)/shard_map/pallas_call | solution.py:32
  12.8 11.5 %all-to-all-start = ((f32[32,1,128]{2,1,0:T(1,128)}), f32[32,1,128]{2,1,0:T(1,128)S(1)}, u32[]{:S(2)}, u32[]{:S(2)}) async-start(f32[32,1,128]{2,1,0:T(1,128)} %bitcast.20), calls=%async_computation | async-start | bytes 32768 | tf_op jit(solution)/shard_map/all_to_all | solution.py:497
  24.4 0.0 collective-permute-done.top
  24.4 0.0 collective-permute-done.1.bottom
  24.4 0.0 copy-start.1
  24.4 0.7 copy-done.1
  25.1 4.1 %collective-permute-start.2 = (bf16[2,16,320]{2,1,0:T(8,128)(2,1)S(1)}, bf16[2,16,320]{2,1,0:T(8,128)(2,1)S(1)}, u32[]{:S(2)}, u32[]{:S(2)}) collective-permute-start(bf16[2,16,320]{2,1,0:T(8,128)(2,1)S(1)} %shard_map.149), channel_id=1, source_target_pairs={{0,7},{1,2},{2,1},{3,4},{4,3},{5,6},{6,5},{7,0},{8,15},{9,10},{10,... | collective-permute-start | bytes 61448 | tf_op jit(solution)/shard_map/ppermute | solution.py:507
  29.3 4.7 %all-to-all-done = f32[32,1,128]{2,1,0:T(1,128)S(1)} async-done(((f32[32,1,128]{2,1,0:T(1,128)}), f32[32,1,128]{2,1,0:T(1,128)S(1)}, u32[]{:S(2)}, u32[]{:S(2)}) %all-to-all-start) | async-done | bytes 16416 | tf_op jit(solution)/shard_map/all_to_all | solution.py:497
  34.0 0.0 collective-permute-done.2.side
  34.0 0.0 copy-start.4
  34.0 1.0 %copy-done.4 = bf16[2,16,16,320]{3,2,1,0:T(8,128)(2,1)S(1)} copy-done((bf16[2,16,16,320]{3,2,1,0:T(8,128)(2,1)S(1)}, bf16[2,16,16,320]{3,2,1,0:T(8,128)(2,1)}, u32[]{:S(2)}) %copy-start.4) | copy-done | bytes 327704
  35.0 0.0 copy-start
  35.0 0.0 copy-start.2
  35.0 0.0 copy-start.3
  35.0 0.0 copy-start.5
  35.0 0.0 copy-start.6
  35.0 0.0 copy-start.7
  35.1 0.0 copy-start.8
  35.1 2.2 %collective-permute-start.3 = (bf16[2,19,16,320]{3,2,1,0:T(8,128)(2,1)S(1)}, bf16[2,19,16,320]{3,2,1,0:T(8,128)(2,1)S(1)}, u32[]{:S(2)}, u32[]{:S(2)}) collective-permute-start(bf16[2,19,16,320]{3,2,1,0:T(8,128)(2,1)S(1)} %get-tuple-element.24.mine), channel_id=1, source_target_pairs={{0,1},{1,0},{2,3},{3,2},{4,5},{5,4},{6,7},{7,6},{8,9},{9,8},{10,11... | collective-permute-start | bytes 1167368 | tf_op jit(solution)/shard_map/ppermute | solution.py:514
  38.0 0.0 copy-done
  38.0 1.0 %shard_map.151.bias = f32[8,320]{1,0:T(8,128)S(1)} custom-call(s32[1]{0:T(128)S(6)} %copy.17.step, f32[320,320]{1,0:T(8,128)S(1)} %copy-done), custom_call_target="tpu_custom_call" | custom-call | flops 10000000 | bytes 1000000 | tf_op jit(solution)/shard_map/pallas_call | solution.py:32
  39.0 0.2 collective-permute-done.3.theirs
  39.1 0.0 copy-done.2
  39.1 0.0 copy-done.3
  39.1 0.0 copy-done.5
  39.1 0.0 copy-done.6
  39.1 0.0 copy-done.7
  39.1 0.0 copy-done.8
  39.1 6.5 %shard_map.152 = (bf16[512,2880]{1,0:T(8,128)(2,1)S(1)}, bf16[512,320]{1,0:T(8,128)(2,1)S(1)}, f32[8,640]{1,0:T(8,128)S(1)}) custom-call(f32[8,128]{1,0:T(8,128)S(1)} %get-tuple-element.23.totals, f32[8,320]{1,0:T(8,128)S(1)} %shard_map.151.bias, bf16[2,19,16,320]{3,2,1,0:T(8,128)(2,1)S(1)} %get-tuple-element.24.mine, ...), custom_call_target="tpu_custom_call" | custom-call | flops 2000000000 | bytes 10000000 | tf_op jit(solution)/shard_map/pallas_call | solution.py:32
  45.7 2.3 %collective-permute-start.4 = (f32[8,640]{1,0:T(8,128)S(1)}, f32[8,640]{1,0:T(8,128)S(1)}, u32[]{:S(2)}, u32[]{:S(2)}) collective-permute-start(f32[8,640]{1,0:T(8,128)S(1)} %get-tuple-element.27.small), channel_id=1, source_target_pairs={{0,1},{1,0},{2,3},{3,2},{4,5},{5,4},{6,7},{7,6},{8,9},{9,8},{10,11... | collective-permute-start | bytes 61448 | tf_op jit(solution)/shard_map/ppermute | solution.py:537
  48.0 1.9 %shard_map.153.blocks = f32[32,48,320]{2,1,0:T(8,128)S(1)} custom-call(bf16[512,2880]{1,0:T(8,128)(2,1)S(1)} %get-tuple-element.25.cols, bf16[512,320]{1,0:T(8,128)(2,1)S(1)} %get-tuple-element.26.cot), custom_call_target="tpu_custom_call" | custom-call | flops 1000000000 | bytes 10000000 | tf_op jit(solution)/shard_map/pallas_call | solution.py:32
  49.9 0.0 collective-permute-done.4.other
  49.9 1.2 %shard_map.154 = s16[8,10,48,128]{3,2,1,0:T(8,128)(2,1)S(1)} custom-call(f32[32,48,320]{2,1,0:T(8,128)S(1)} %shard_map.153.blocks, f32[8,640]{1,0:T(8,128)S(1)} %get-tuple-element.27.small, f32[8,640]{1,0:T(8,128)S(1)} %collective-permute-done.4.other), custom_call_target="tpu_custom_call" | custom-call | tf_op jit(solution)/shard_map/pallas_call | solution.py:32
  51.1 19.3 %all_to_all.21.blocks = s16[8,10,48,128]{3,2,1,0:T(8,128)(2,1)S(1)} all-to-all(s16[8,10,48,128]{3,2,1,0:T(8,128)(2,1)S(1)} %shard_map.154), channel_id=1, replica_groups=mesh['y'=8,'x'=4,'zl'=2,'zh'=4,'core'=2] {'x','zl'}, dimensions={0} | all-to-all | bytes 1966080 | tf_op jit(solution)/shard_map/all_to_all | solution.py:549
  70.3 1.5 %shard_map.155 = s16[8,4,24,128]{3,2,1,0:T(8,128)(2,1)S(1)} custom-call(s16[8,10,48,128]{3,2,1,0:T(8,128)(2,1)S(1)} %all_to_all.21.blocks), custom_call_target="tpu_custom_call" | custom-call | tf_op jit(solution)/shard_map/pallas_call | solution.py:32
  71.8 23.7 %all_to_all.22 = s16[32,24,128]{2,1,0:T(8,128)(2,1)S(1)} all-to-all(s16[32,24,128]{2,1,0:T(8,128)(2,1)S(1)} %bitcast.11), channel_id=1, replica_groups=mesh['y'=8,'x'=4,'zl'=2,'zh'=4,'core'=2] {'y','zh'}, dimensions={0} | all-to-all | bytes 393216 | tf_op jit(solution)/shard_map/all_to_all | solution.py:551
  95.5 1.1 %shard_map.156 = (f32[1,1]{1,0:T(1,128)}, f32[40,45]{1,0:T(8,128)}, f32[320]{0:T(512)}, f32[320]{0:T(512)}) custom-call(s16[8,4,24,128]{3,2,1,0:T(8,128)(2,1)S(1)} %bitcast.12), custom_call_target="tpu_custom_call" | custom-call | tf_op jit(solution)/shard_map/pallas_call | solution.py:32
  (2 shorter events, 0.1 us)
Async XLA Ops:
  2.0 22.3 %collective-permute-start = (bf16[2,16,320]{2,1,0:T(8,128)(2,1)}, bf16[2,16,320]{2,1,0:T(8,128)(2,1)S(1)}, u32[]{:S(2)}, u32[]{:S(2)}) collective-permute-start(bf16[2,16,320]{2,1,0:T(8,128)(2,1)} %get-tuple-element.19), channel_id=1, source_target_pairs={{0,8},{8,16},{16,24},{24,32},{32,40},{40,48},{48,56},{56,0},{1,9},... | collective-permute-start | bytes 61448 | tf_op jit(solution)/shard_map/ppermute | solution.py:486
  6.3 18.0 %collective-permute-start.1 = (bf16[2,16,320]{2,1,0:T(8,128)(2,1)}, bf16[2,16,320]{2,1,0:T(8,128)(2,1)S(1)}, u32[]{:S(2)}, u32[]{:S(2)}) collective-permute-start(bf16[2,16,320]{2,1,0:T(8,128)(2,1)} %get-tuple-element.20), channel_id=1, source_target_pairs={{8,0},{16,8},{24,16},{32,24},{40,32},{48,40},{56,48},{0,56},{9,1},... | collective-permute-start | bytes 61448 | tf_op jit(solution)/shard_map/ppermute | solution.py:487
  12.8 21.2 %all-to-all-start = ((f32[32,1,128]{2,1,0:T(1,128)}), f32[32,1,128]{2,1,0:T(1,128)S(1)}, u32[]{:S(2)}, u32[]{:S(2)}) async-start(f32[32,1,128]{2,1,0:T(1,128)} %bitcast.20), calls=%async_computation | async-start | bytes 32768 | tf_op jit(solution)/shard_map/all_to_all | solution.py:497
  24.4 0.7 copy-start.1
  25.1 8.9 %collective-permute-start.2 = (bf16[2,16,320]{2,1,0:T(8,128)(2,1)S(1)}, bf16[2,16,320]{2,1,0:T(8,128)(2,1)S(1)}, u32[]{:S(2)}, u32[]{:S(2)}) collective-permute-start(bf16[2,16,320]{2,1,0:T(8,128)(2,1)S(1)} %shard_map.149), channel_id=1, source_target_pairs={{0,7},{1,2},{2,1},{3,4},{4,3},{5,6},{6,5},{7,0},{8,15},{9,10},{10,... | collective-permute-start | bytes 61448 | tf_op jit(solution)/shard_map/ppermute | solution.py:507
  34.0 1.0 %copy-start.4 = (bf16[2,16,16,320]{3,2,1,0:T(8,128)(2,1)S(1)}, bf16[2,16,16,320]{3,2,1,0:T(8,128)(2,1)}, u32[]{:S(2)}) copy-start(bf16[2,16,16,320]{3,2,1,0:T(8,128)(2,1)} %get-tuple-element.22.here) | copy-start | bytes 983044
  35.0 2.9 %copy-start = (f32[320,320]{1,0:T(8,128)S(1)}, f32[320,320]{1,0:T(8,128)}, u32[]{:S(2)}) copy-start(f32[320,320]{1,0:T(8,128)} %time_weight.1) | copy-start | bytes 1228804
  35.0 4.1 %copy-start.2 = (bf16[9,320,320]{2,1,0:T(8,128)(2,1)S(1)}, bf16[9,320,320]{2,1,0:T(8,128)(2,1)}, u32[]{:S(2)}) copy-start(bf16[9,320,320]{2,1,0:T(8,128)(2,1)} %weight_far.1) | copy-start | bytes 5529604
  35.0 4.1 %copy-start.3 = (bf16[9,320,320]{2,1,0:T(8,128)(2,1)S(1)}, bf16[9,320,320]{2,1,0:T(8,128)(2,1)}, u32[]{:S(2)}) copy-start(bf16[9,320,320]{2,1,0:T(8,128)(2,1)} %ref_far.1) | copy-start | bytes 5529604
  35.0 4.1 %copy-start.5 = (f32[320]{0:T(512)S(1)}, f32[320]{0:T(512)}, u32[]{:S(2)}) copy-start(f32[320]{0:T(512)} %gain_far.1) | copy-start | bytes 3844
  35.0 4.1 %copy-start.6 = (f32[320]{0:T(512)S(1)}, f32[320]{0:T(512)}, u32[]{:S(2)}) copy-start(f32[320]{0:T(512)} %shift_far.1) | copy-start | bytes 3844
  35.0 4.1 %copy-start.7 = (f32[320]{0:T(512)S(1)}, f32[320]{0:T(512)}, u32[]{:S(2)}) copy-start(f32[320]{0:T(512)} %ref_gain_far.1) | copy-start | bytes 3844
  35.1 4.1 %copy-start.8 = (f32[320]{0:T(512)S(1)}, f32[320]{0:T(512)}, u32[]{:S(2)}) copy-start(f32[320]{0:T(512)} %ref_shift_far.1) | copy-start | bytes 3844
  35.1 4.0 %collective-permute-start.3 = (bf16[2,19,16,320]{3,2,1,0:T(8,128)(2,1)S(1)}, bf16[2,19,16,320]{3,2,1,0:T(8,128)(2,1)S(1)}, u32[]{:S(2)}, u32[]{:S(2)}) collective-permute-start(bf16[2,19,16,320]{3,2,1,0:T(8,128)(2,1)S(1)} %get-tuple-element.24.mine), channel_id=1, source_target_pairs={{0,1},{1,0},{2,3},{3,2},{4,5},{5,4},{6,7},{7,6},{8,9},{9,8},{10,11... | collective-permute-start | bytes 1167368 | tf_op jit(solution)/shard_map/ppermute | solution.py:514
  45.7 4.2 %collective-permute-start.4 = (f32[8,640]{1,0:T(8,128)S(1)}, f32[8,640]{1,0:T(8,128)S(1)}, u32[]{:S(2)}, u32[]{:S(2)}) collective-permute-start(f32[8,640]{1,0:T(8,128)S(1)} %get-tuple-element.27.small), channel_id=1, source_target_pairs={{0,1},{1,0},{2,3},{3,2},{4,5},{5,4},{6,7},{7,6},{8,9},{9,8},{10,11... | collective-permute-start | bytes 61448 | tf_op jit(solution)/shard_map/ppermute | solution.py:537

commit v8 on v7

--- a/solution.py
+++ b/solution.py
@@ -24,7 +24,7 @@
 HIGHEST = lax.Precision.HIGHEST
 
 
-def call(kernel, outs, scratch=(), flops=0, nbytes=0, far=(), grant=28):
+def call(kernel, outs, scratch=(), flops=0, nbytes=0, far=(), far_outs=(), grant=28):
     def run(*args):
         specs = [
             pl.BlockSpec(memory_space=pltpu.HBM if i in far else pltpu.VMEM) for i in range(len(args))
@@ -33,7 +33,10 @@
             kernel,
             out_shape=[jax.ShapeDtypeStruct(s, d) for s, d in outs],
             in_specs=specs,
-            out_specs=[pl.BlockSpec(memory_space=pltpu.VMEM) for _ in outs],
+            out_specs=[
+                pl.BlockSpec(memory_space=pltpu.HBM if i in far_outs else pltpu.VMEM)
+                for i in range(len(outs))
+            ],
             scratch_shapes=list(scratch),
             compiler_params=pltpu.CompilerParams(vmem_limit_bytes=grant * 2**20),
             cost_estimate=pl.CostEstimate(flops=flops, bytes_accessed=nbytes, transcendentals=0),
@@ -131,13 +134,15 @@
         copy.wait()
 
 
-def statistics(fw, fl, nw, nl, stats, edge, here, sems):
-    copies = [
-        pltpu.make_async_copy(fw, here.at[0, pl.ds(0, TH)], sems.at[0]),
-        pltpu.make_async_copy(fl, here.at[1, pl.ds(0, TH)], sems.at[1]),
-        pltpu.make_async_copy(nw, here.at[0, pl.ds(TH, TH)], sems.at[2]),
-        pltpu.make_async_copy(nl, here.at[1, pl.ds(TH, TH)], sems.at[3]),
-    ]
+def statistics(fw, fl, nw, nl, stats, edge, here, near, sems):
+    copies = [pltpu.make_async_copy(f, near.at[k], sems.at[k]) for k, f in enumerate((fw, fl))]
+    for k, (f, n) in enumerate(((fw, nw), (fl, nl))):
+        copies.append(
+            pltpu.make_async_copy(f, here.at[k, pl.ds(0, TH)], sems.at[2 + 2 * k])
+        )
+        copies.append(
+            pltpu.make_async_copy(n, here.at[k, pl.ds(TH, TH)], sems.at[3 + 2 * k])
+        )
     for copy in copies:
         copy.start()
     copies[0].wait()
@@ -147,7 +152,7 @@
     lanes = lax.broadcasted_iota(jnp.int32, (C, 128), 1)
     size = C // GROUPS
     for k in range(2):
-        field = here[k, 0:TH].astype(F32)
+        field = near[k].astype(F32)
         x = field.reshape(PIX, C)
         sums = jnp.sum(x, axis=0, keepdims=True)
         squares = jnp.sum(x * x, axis=0, keepdims=True)
@@ -168,8 +173,8 @@
         column = jnp.where(lax.axis_index("core") == 0, column[0], column[1])
         edge[k] = jnp.concatenate([column, jnp.zeros((8, C), F32)], axis=0).astype(BF16)
     stats[...] = jnp.broadcast_to(total[0:1], stats.shape)
-    copies[2].wait()
-    copies[3].wait()
+    for copy in copies[2:]:
+        copy.wait()
 
 
 def time_bias(step, time_weight, bias, number, table, sems):
@@ -481,6 +486,7 @@
         [(strip, BF16), (strip, BF16)],
         [pltpu.SemaphoreType.DMA((4,))],
         far=(0, 1),
+        far_outs=(0, 1),
         grant=57,
     )(fw, fl)
     top = lax.ppermute(last, rows, down)
@@ -488,10 +494,11 @@
     stats, edge, here = call(
         statistics,
         [((32, 128), F32), (strip, BF16), ((2, 2 * TH, TW, C), BF16)],
-        [pltpu.SemaphoreType.DMA((4,))],
+        [pltpu.VMEM((2, TH, TW, C), BF16), pltpu.SemaphoreType.DMA((6,))],
         flops=10**7,
         nbytes=10**6,
         far=range(4),
+        far_outs=(2,),
         grant=57,
     )(fw, fl, noise_win[0], noise_lose[0])
     stats = lax.all_to_all(stats, ("x", "zl", "zh"), 0, 0, tiled=True)

time: 97.2 us -> 110 us (1.13)
  Pallas kernels: 17.1 us -> 29.6 us
    pallas_call x10, Pallas kernels: 17.1 us -> 29.6 us  [run(): pl.pallas_call(kernel, out_shape=[jax.ShapeDtypeStruct(s, d) for s, d in...]
  transfers between devices with their start and end apart: 6 -> 6, of which waited for: 2 -> 2; matrix products, arithmetic and copies ran while one was open for 0% -> 0% of each run, Pallas kernels for 5% -> 15%
where the time goes in v8:
time: 110 us; the launch traced here: 109 us
  blocking collectives  43 us (39%)
  Pallas kernels  29.6 us (27%)
  starting transfers between devices  28.5 us (26%)
  waiting for transfers between devices  4.91 us (4%)
  local copies, waits for them, and re-layouts  1.76 us (2%)
  between operations  1.49 us (1%)
    pallas_call x10, Pallas kernels, run(): pl.pallas_call(kernel, out_shape=[jax.ShapeDtypeStruct(s, d) for s, d in...  29.6 us
    all_to_all x1, blocking collectives, local(): lax.all_to_all(sums.reshape(32, 24, 128), ('y', 'zh'), 0, 0, tiled=True)  23.7 us
    all_to_all x1, blocking collectives, local(): blocks = lax.all_to_all(blocks, ('x', 'zl'), 0, 0, tiled=True)  19.3 us
    all_to_all x1, starting transfers between devices, local(): stats = lax.all_to_all(stats, ('x', 'zl', 'zh'), 0, 0, tiled=True)  11.5 us
    all_to_all x1, waiting for transfers between devices, local(): stats = lax.all_to_all(stats, ('x', 'zl', 'zh'), 0, 0, tiled=True)  4.75 us
    ppermute x1, starting transfers between devices, local(): top = lax.ppermute(last, rows, down)  4.28 us
    ppermute x1, starting transfers between devices, local(): side = lax.ppermute(side, columns, outward)  4.13 us
    ppermute x1, starting transfers between devices, local(): bottom = lax.ppermute(first, rows, up)  4.11 us
  transfers between devices with their start and end apart: 6, of which 2 were waited for; matrix products, arithmetic and copies ran while one was open for 0% of the time, Pallas kernels for 15%

profile of v8, /device:TPU:8, one launch (start us, length us, event | category | flops | bytes accessed | tf_op | source)
XLA Modules:
  0.0 109.2 jit_solution(17534087166216494893)
XLA Ops:
  0.6 2.6 %shard_map.148 = (bf16[2,16,320]{2,1,0:T(8,128)(2,1)}, bf16[2,16,320]{2,1,0:T(8,128)(2,1)}) custom-call(bf16[8,16,320]{2,1,0:T(8,128)(2,1)} %bitcast.14, bf16[8,16,320]{2,1,0:T(8,128)(2,1)} %bitcast.16), custom_call_target="tpu_custom_call" | custom-call | tf_op jit(solution)/shard_map/pallas_call | solution.py:32
  3.3 4.3 %collective-permute-start = (bf16[2,16,320]{2,1,0:T(8,128)(2,1)}, bf16[2,16,320]{2,1,0:T(8,128)(2,1)S(1)}, u32[]{:S(2)}, u32[]{:S(2)}) collective-permute-start(bf16[2,16,320]{2,1,0:T(8,128)(2,1)} %get-tuple-element.19), channel_id=1, source_target_pairs={{0,8},{8,16},{16,24},{24,32},{32,40},{40,48},{48,56},{56,0},{1,9},... | collective-permute-start | bytes 61448 | tf_op jit(solution)/shard_map/ppermute | solution.py:492
  7.6 4.1 %collective-permute-start.1 = (bf16[2,16,320]{2,1,0:T(8,128)(2,1)}, bf16[2,16,320]{2,1,0:T(8,128)(2,1)S(1)}, u32[]{:S(2)}, u32[]{:S(2)}) collective-permute-start(bf16[2,16,320]{2,1,0:T(8,128)(2,1)} %get-tuple-element.20), channel_id=1, source_target_pairs={{8,0},{16,8},{24,16},{32,24},{40,32},{48,40},{56,48},{0,56},{9,1},... | collective-permute-start | bytes 61448 | tf_op jit(solution)/shard_map/ppermute | solution.py:493
  11.7 13.7 %shard_map.147 = (f32[32,128]{1,0:T(8,128)}, bf16[2,16,320]{2,1,0:T(8,128)(2,1)}, bf16[2,16,16,320]{3,2,1,0:T(8,128)(2,1)}) custom-call(bf16[8,16,320]{2,1,0:T(8,128)(2,1)} %bitcast.15, bf16[8,16,320]{2,1,0:T(8,128)(2,1)} %bitcast.17, bf16[8,16,320]{2,1,0:T(8,128)(2,1)} %bitcast.18, bf16[8,16,320]{2,1,0:T(8,128)(2,1)} %bitcast.19), custom_call_target="tpu_custom_call" | custom-call | flops 10000000 | bytes 1000000 | tf_op jit(solution)/shard_map/pallas_call | solution.py:32
  25.4 11.5 %all-to-all-start = ((f32[32,1,128]{2,1,0:T(1,128)}), f32[32,1,128]{2,1,0:T(1,128)S(1)}, u32[]{:S(2)}, u32[]{:S(2)}) async-start(f32[32,1,128]{2,1,0:T(1,128)} %bitcast.20), calls=%async_computation | async-start | bytes 32768 | tf_op jit(solution)/shard_map/all_to_all | solution.py:504
  36.9 0.0 collective-permute-done.top
  36.9 0.0 collective-permute-done.1.bottom
  36.9 0.0 copy-start.1
  36.9 0.7 copy-done.1
  37.7 4.1 %collective-permute-start.2 = (bf16[2,16,320]{2,1,0:T(8,128)(2,1)S(1)}, bf16[2,16,320]{2,1,0:T(8,128)(2,1)S(1)}, u32[]{:S(2)}, u32[]{:S(2)}) collective-permute-start(bf16[2,16,320]{2,1,0:T(8,128)(2,1)S(1)} %shard_map.149), channel_id=1, source_target_pairs={{0,7},{1,2},{2,1},{3,4},{4,3},{5,6},{6,5},{7,0},{8,15},{9,10},{10,... | collective-permute-start | bytes 61448 | tf_op jit(solution)/shard_map/ppermute | solution.py:514
  41.8 4.7 %all-to-all-done = f32[32,1,128]{2,1,0:T(1,128)S(1)} async-done(((f32[32,1,128]{2,1,0:T(1,128)}), f32[32,1,128]{2,1,0:T(1,128)S(1)}, u32[]{:S(2)}, u32[]{:S(2)}) %all-to-all-start) | async-done | bytes 16416 | tf_op jit(solution)/shard_map/all_to_all | solution.py:504
  46.6 0.0 collective-permute-done.2.side
  46.6 0.0 copy-start.4
  46.6 1.0 copy-done.4
  47.6 0.0 copy-start
  47.6 0.0 copy-start.2
  47.6 0.0 copy-start.3
  47.6 0.0 copy-start.5
  47.6 0.0 copy-start.6
  47.6 0.0 copy-start.7
  47.6 0.0 copy-start.8
  47.7 2.2 %collective-permute-start.3 = (bf16[2,19,16,320]{3,2,1,0:T(8,128)(2,1)S(1)}, bf16[2,19,16,320]{3,2,1,0:T(8,128)(2,1)S(1)}, u32[]{:S(2)}, u32[]{:S(2)}) collective-permute-start(bf16[2,19,16,320]{3,2,1,0:T(8,128)(2,1)S(1)} %get-tuple-element.24.mine), channel_id=1, source_target_pairs={{0,1},{1,0},{2,3},{3,2},{4,5},{5,4},{6,7},{7,6},{8,9},{9,8},{10,11... | collective-permute-start | bytes 1167368 | tf_op jit(solution)/shard_map/ppermute | solution.py:521
  50.5 0.0 copy-done
  50.5 1.0 shard_map.151.bias
  51.5 0.2 collective-permute-done.3.theirs
  51.6 0.0 copy-done.2
  51.6 0.0 copy-done.3
  51.6 0.0 copy-done.5
  51.6 0.0 copy-done.6
  51.7 0.0 copy-done.7
  51.7 0.0 copy-done.8
  51.7 6.5 %shard_map.152 = (bf16[512,2880]{1,0:T(8,128)(2,1)S(1)}, bf16[512,320]{1,0:T(8,128)(2,1)S(1)}, f32[8,640]{1,0:T(8,128)S(1)}) custom-call(f32[8,128]{1,0:T(8,128)S(1)} %get-tuple-element.23.totals, f32[8,320]{1,0:T(8,128)S(1)} %shard_map.151.bias, bf16[2,19,16,320]{3,2,1,0:T(8,128)(2,1)S(1)} %get-tuple-element.24.mine, ...), custom_call_target="tpu_custom_call" | custom-call | flops 2000000000 | bytes 10000000 | tf_op jit(solution)/shard_map/pallas_call | solution.py:32
  58.2 2.3 %collective-permute-start.4 = (f32[8,640]{1,0:T(8,128)S(1)}, f32[8,640]{1,0:T(8,128)S(1)}, u32[]{:S(2)}, u32[]{:S(2)}) collective-permute-start(f32[8,640]{1,0:T(8,128)S(1)} %get-tuple-element.27.small), channel_id=1, source_target_pairs={{0,1},{1,0},{2,3},{3,2},{4,5},{5,4},{6,7},{7,6},{8,9},{9,8},{10,11... | collective-permute-start | bytes 61448 | tf_op jit(solution)/shard_map/ppermute | solution.py:544
  60.5 1.9 %shard_map.153.blocks = f32[32,48,320]{2,1,0:T(8,128)S(1)} custom-call(bf16[512,2880]{1,0:T(8,128)(2,1)S(1)} %get-tuple-element.25.cols, bf16[512,320]{1,0:T(8,128)(2,1)S(1)} %get-tuple-element.26.cot), custom_call_target="tpu_custom_call" | custom-call | flops 1000000000 | bytes 10000000 | tf_op jit(solution)/shard_map/pallas_call | solution.py:32
  62.4 0.0 collective-permute-done.4.other
  62.4 1.2 %shard_map.154 = s16[8,10,48,128]{3,2,1,0:T(8,128)(2,1)S(1)} custom-call(f32[32,48,320]{2,1,0:T(8,128)S(1)} %shard_map.153.blocks, f32[8,640]{1,0:T(8,128)S(1)} %get-tuple-element.27.small, f32[8,640]{1,0:T(8,128)S(1)} %collective-permute-done.4.other), custom_call_target="tpu_custom_call" | custom-call | tf_op jit(solution)/shard_map/pallas_call | solution.py:32
  63.6 19.3 %all_to_all.21.blocks = s16[8,10,48,128]{3,2,1,0:T(8,128)(2,1)S(1)} all-to-all(s16[8,10,48,128]{3,2,1,0:T(8,128)(2,1)S(1)} %shard_map.154), channel_id=1, replica_groups=mesh['y'=8,'x'=4,'zl'=2,'zh'=4,'core'=2] {'x','zl'}, dimensions={0} | all-to-all | bytes 1966080 | tf_op jit(solution)/shard_map/all_to_all | solution.py:556
  82.9 1.5 %shard_map.155 = s16[8,4,24,128]{3,2,1,0:T(8,128)(2,1)S(1)} custom-call(s16[8,10,48,128]{3,2,1,0:T(8,128)(2,1)S(1)} %all_to_all.21.blocks), custom_call_target="tpu_custom_call" | custom-call | tf_op jit(solution)/shard_map/pallas_call | solution.py:32
  84.4 23.7 %all_to_all.22 = s16[32,24,128]{2,1,0:T(8,128)(2,1)S(1)} all-to-all(s16[32,24,128]{2,1,0:T(8,128)(2,1)S(1)} %bitcast.11), channel_id=1, replica_groups=mesh['y'=8,'x'=4,'zl'=2,'zh'=4,'core'=2] {'y','zh'}, dimensions={0} | all-to-all | bytes 393216 | tf_op jit(solution)/shard_map/all_to_all | solution.py:558
  108.1 1.1 %shard_map.156 = (f32[1,1]{1,0:T(1,128)}, f32[40,45]{1,0:T(8,128)}, f32[320]{0:T(512)}, f32[320]{0:T(512)}) custom-call(s16[8,4,24,128]{3,2,1,0:T(8,128)(2,1)S(1)} %bitcast.12), custom_call_target="tpu_custom_call" | custom-call | tf_op jit(solution)/shard_map/pallas_call | solution.py:32
  (2 shorter events, 0.1 us)
Async XLA Ops:
  3.3 33.6 %collective-permute-start = (bf16[2,16,320]{2,1,0:T(8,128)(2,1)}, bf16[2,16,320]{2,1,0:T(8,128)(2,1)S(1)}, u32[]{:S(2)}, u32[]{:S(2)}) collective-permute-start(bf16[2,16,320]{2,1,0:T(8,128)(2,1)} %get-tuple-element.19), channel_id=1, source_target_pairs={{0,8},{8,16},{16,24},{24,32},{32,40},{40,48},{48,56},{56,0},{1,9},... | collective-permute-start | bytes 61448 | tf_op jit(solution)/shard_map/ppermute | solution.py:492
  7.6 29.3 %collective-permute-start.1 = (bf16[2,16,320]{2,1,0:T(8,128)(2,1)}, bf16[2,16,320]{2,1,0:T(8,128)(2,1)S(1)}, u32[]{:S(2)}, u32[]{:S(2)}) collective-permute-start(bf16[2,16,320]{2,1,0:T(8,128)(2,1)} %get-tuple-element.20), channel_id=1, source_target_pairs={{8,0},{16,8},{24,16},{32,24},{40,32},{48,40},{56,48},{0,56},{9,1},... | collective-permute-start | bytes 61448 | tf_op jit(solution)/shard_map/ppermute | solution.py:493
  25.4 21.2 %all-to-all-start = ((f32[32,1,128]{2,1,0:T(1,128)}), f32[32,1,128]{2,1,0:T(1,128)S(1)}, u32[]{:S(2)}, u32[]{:S(2)}) async-start(f32[32,1,128]{2,1,0:T(1,128)} %bitcast.20), calls=%async_computation | async-start | bytes 32768 | tf_op jit(solution)/shard_map/all_to_all | solution.py:504
  36.9 0.7 copy-start.1
  37.7 8.9 %collective-permute-start.2 = (bf16[2,16,320]{2,1,0:T(8,128)(2,1)S(1)}, bf16[2,16,320]{2,1,0:T(8,128)(2,1)S(1)}, u32[]{:S(2)}, u32[]{:S(2)}) collective-permute-start(bf16[2,16,320]{2,1,0:T(8,128)(2,1)S(1)} %shard_map.149), channel_id=1, source_target_pairs={{0,7},{1,2},{2,1},{3,4},{4,3},{5,6},{6,5},{7,0},{8,15},{9,10},{10,... | collective-permute-start | bytes 61448 | tf_op jit(solution)/shard_map/ppermute | solution.py:514
  46.6 1.0 copy-start.4
  47.6 2.9 %copy-start = (f32[320,320]{1,0:T(8,128)S(1)}, f32[320,320]{1,0:T(8,128)}, u32[]{:S(2)}) copy-start(f32[320,320]{1,0:T(8,128)} %time_weight.1) | copy-start | bytes 1228804
  47.6 4.1 %copy-start.2 = (bf16[9,320,320]{2,1,0:T(8,128)(2,1)S(1)}, bf16[9,320,320]{2,1,0:T(8,128)(2,1)}, u32[]{:S(2)}) copy-start(bf16[9,320,320]{2,1,0:T(8,128)(2,1)} %weight_far.1) | copy-start | bytes 5529604
  47.6 4.1 %copy-start.3 = (bf16[9,320,320]{2,1,0:T(8,128)(2,1)S(1)}, bf16[9,320,320]{2,1,0:T(8,128)(2,1)}, u32[]{:S(2)}) copy-start(bf16[9,320,320]{2,1,0:T(8,128)(2,1)} %ref_far.1) | copy-start | bytes 5529604
  47.6 4.1 %copy-start.5 = (f32[320]{0:T(512)S(1)}, f32[320]{0:T(512)}, u32[]{:S(2)}) copy-start(f32[320]{0:T(512)} %gain_far.1) | copy-start | bytes 3844
  47.6 4.1 %copy-start.6 = (f32[320]{0:T(512)S(1)}, f32[320]{0:T(512)}, u32[]{:S(2)}) copy-start(f32[320]{0:T(512)} %shift_far.1) | copy-start | bytes 3844
  47.6 4.1 %copy-start.7 = (f32[320]{0:T(512)S(1)}, f32[320]{0:T(512)}, u32[]{:S(2)}) copy-start(f32[320]{0:T(512)} %ref_gain_far.1) | copy-start | bytes 3844
  47.6 4.1 %copy-start.8 = (f32[320]{0:T(512)S(1)}, f32[320]{0:T(512)}, u32[]{:S(2)}) copy-start(f32[320]{0:T(512)} %ref_shift_far.1) | copy-start | bytes 3844
  47.7 4.0 %collective-permute-start.3 = (bf16[2,19,16,320]{3,2,1,0:T(8,128)(2,1)S(1)}, bf16[2,19,16,320]{3,2,1,0:T(8,128)(2,1)S(1)}, u32[]{:S(2)}, u32[]{:S(2)}) collective-permute-start(bf16[2,19,16,320]{3,2,1,0:T(8,128)(2,1)S(1)} %get-tuple-element.24.mine), channel_id=1, source_target_pairs={{0,1},{1,0},{2,3},{3,2},{4,5},{5,4},{6,7},{7,6},{8,9},{9,8},{10,11... | collective-permute-start | bytes 1167368 | tf_op jit(solution)/shard_map/ppermute | solution.py:521
  58.2 4.2 %collective-permute-start.4 = (f32[8,640]{1,0:T(8,128)S(1)}, f32[8,640]{1,0:T(8,128)S(1)}, u32[]{:S(2)}, u32[]{:S(2)}) collective-permute-start(f32[8,640]{1,0:T(8,128)S(1)} %get-tuple-element.27.small), channel_id=1, source_target_pairs={{0,1},{1,0},{2,3},{3,2},{4,5},{5,4},{6,7},{7,6},{8,9},{9,8},{10,11... | collective-permute-start | bytes 61448 | tf_op jit(solution)/shard_map/ppermute | solution.py:544

commit v9 on v7

--- a/solution.py
+++ b/solution.py
@@ -499,11 +499,13 @@
         time_bias,
         [((8, C), F32)],
         [pltpu.SMEM((1,), jnp.int32), pltpu.VMEM((C, C), F32), pltpu.SemaphoreType.DMA((2,))],
-        flops=10**7,
+        flops=10**10,
         nbytes=10**6,
         far=(0, 1),
     )(timesteps, time_weight)
-    (side,) = call(outer_column, [(strip, BF16)])(top, bottom, edge)
+    (side,) = call(outer_column, [(strip, BF16)], flops=10**10, nbytes=10**6)(
+        top, bottom, edge
+    )
     side = lax.ppermute(side, columns, outward)
     totals, mine = call(
         sums_and_tile,

time: 97.2 us -> 96.4 us (level)
  local copies, waits for them, and re-layouts: 1.76 us -> 0.78 us
    unnamed x18, local copies, waits for them, and re-layouts: 1.76 us -> 0.78 us
where the time goes in v9:
time: 96.4 us; the launch traced here: 95.9 us
  blocking collectives  43.4 us (45%)
  starting transfers between devices  28.4 us (29%)
  Pallas kernels  17.1 us (18%)
  waiting for transfers between devices  4.78 us (5%)
  between operations  1.51 us (2%)
    all_to_all x1, blocking collectives, local(): lax.all_to_all(sums.reshape(32, 24, 128), ('y', 'zh'), 0, 0, tiled=True)  23.7 us
    all_to_all x1, blocking collectives, local(): blocks = lax.all_to_all(blocks, ('x', 'zl'), 0, 0, tiled=True)  19.7 us
    pallas_call x10, Pallas kernels, run(): pl.pallas_call(kernel, out_shape=[jax.ShapeDtypeStruct(s, d) for s, d in...  17.1 us
    all_to_all x1, starting transfers between devices, local(): stats = lax.all_to_all(stats, ('x', 'zl', 'zh'), 0, 0, tiled=True)  11.5 us
    ppermute x1, starting transfers between devices, local(): top = lax.ppermute(last, rows, down)  4.28 us
    ppermute x1, starting transfers between devices, local(): side = lax.ppermute(side, columns, outward)  4.26 us
    ppermute x1, starting transfers between devices, local(): bottom = lax.ppermute(first, rows, up)  4.11 us
    all_to_all x1, waiting for transfers between devices, local(): stats = lax.all_to_all(stats, ('x', 'zl', 'zh'), 0, 0, tiled=True)  3.97 us
  transfers between devices with their start and end apart: 6, of which 2 were waited for; matrix products, arithmetic and copies ran while one was open for 0% of the time, Pallas kernels for 5%

profile of v9, /device:TPU:8, one launch (start us, length us, event | category | flops | bytes accessed | tf_op | source)
XLA Modules:
  0.0 95.9 jit_solution(1575363799542278383)
XLA Ops:
  0.6 1.4 %shard_map.148 = (bf16[2,16,320]{2,1,0:T(8,128)(2,1)}, bf16[2,16,320]{2,1,0:T(8,128)(2,1)}) custom-call(bf16[8,16,320]{2,1,0:T(8,128)(2,1)} %bitcast.14, bf16[8,16,320]{2,1,0:T(8,128)(2,1)} %bitcast.16), custom_call_target="tpu_custom_call" | custom-call | tf_op jit(solution)/shard_map/pallas_call | solution.py:32
  2.0 4.3 %collective-permute-start = (bf16[2,16,320]{2,1,0:T(8,128)(2,1)}, bf16[2,16,320]{2,1,0:T(8,128)(2,1)S(1)}, u32[]{:S(2)}, u32[]{:S(2)}) collective-permute-start(bf16[2,16,320]{2,1,0:T(8,128)(2,1)} %get-tuple-element.19), channel_id=1, source_target_pairs={{0,8},{8,16},{16,24},{24,32},{32,40},{40,48},{48,56},{56,0},{1,9},... | collective-permute-start | bytes 61448 | tf_op jit(solution)/shard_map/ppermute | solution.py:486
  6.3 4.1 %collective-permute-start.1 = (bf16[2,16,320]{2,1,0:T(8,128)(2,1)}, bf16[2,16,320]{2,1,0:T(8,128)(2,1)S(1)}, u32[]{:S(2)}, u32[]{:S(2)}) collective-permute-start(bf16[2,16,320]{2,1,0:T(8,128)(2,1)} %get-tuple-element.20), channel_id=1, source_target_pairs={{8,0},{16,8},{24,16},{32,24},{40,32},{48,40},{56,48},{0,56},{9,1},... | collective-permute-start | bytes 61448 | tf_op jit(solution)/shard_map/ppermute | solution.py:487
  10.5 2.4 %shard_map.147 = (f32[32,128]{1,0:T(8,128)}, bf16[2,16,320]{2,1,0:T(8,128)(2,1)}, bf16[2,16,16,320]{3,2,1,0:T(8,128)(2,1)}) custom-call(bf16[8,16,320]{2,1,0:T(8,128)(2,1)} %bitcast.15, bf16[8,16,320]{2,1,0:T(8,128)(2,1)} %bitcast.17, bf16[8,16,320]{2,1,0:T(8,128)(2,1)} %bitcast.18, bf16[8,16,320]{2,1,0:T(8,128)(2,1)} %bitcast.19), custom_call_target="tpu_custom_call" | custom-call | flops 10000000 | bytes 1000000 | tf_op jit(solution)/shard_map/pallas_call | solution.py:32
  12.8 11.5 %all-to-all-start = ((f32[32,1,128]{2,1,0:T(1,128)}), f32[32,1,128]{2,1,0:T(1,128)S(1)}, u32[]{:S(2)}, u32[]{:S(2)}) async-start(f32[32,1,128]{2,1,0:T(1,128)} %bitcast.20), calls=%async_computation | async-start | bytes 32768 | tf_op jit(solution)/shard_map/all_to_all | solution.py:497
  24.4 0.0 collective-permute-done.top
  24.4 0.0 collective-permute-done.1.bottom
  24.4 0.0 copy-start.4
  24.4 0.7 copy-done.4
  25.1 0.0 copy-start.3
  25.1 4.3 %collective-permute-start.2 = (bf16[2,16,320]{2,1,0:T(8,128)(2,1)S(1)}, bf16[2,16,320]{2,1,0:T(8,128)(2,1)S(1)}, u32[]{:S(2)}, u32[]{:S(2)}) collective-permute-start(bf16[2,16,320]{2,1,0:T(8,128)(2,1)S(1)} %shard_map.149), channel_id=1, source_target_pairs={{0,7},{1,2},{2,1},{3,4},{4,3},{5,6},{6,5},{7,0},{8,15},{9,10},{10,... | collective-permute-start | bytes 61448 | tf_op jit(solution)/shard_map/ppermute | solution.py:509
  30.1 4.0 %all-to-all-done = f32[32,1,128]{2,1,0:T(1,128)S(1)} async-done(((f32[32,1,128]{2,1,0:T(1,128)}), f32[32,1,128]{2,1,0:T(1,128)S(1)}, u32[]{:S(2)}, u32[]{:S(2)}) %all-to-all-start) | async-done | bytes 16416 | tf_op jit(solution)/shard_map/all_to_all | solution.py:497
  34.0 0.0 collective-permute-done.2.side
  34.0 0.0 copy-done.3
  34.0 0.0 copy-start.2
  34.1 0.0 copy-start
  34.1 0.0 copy-start.1
  34.1 0.0 copy-start.5
  34.1 0.0 copy-start.6
  34.1 0.0 copy-start.7
  34.1 0.0 copy-start.8
  34.2 2.2 %collective-permute-start.3 = (bf16[2,19,16,320]{3,2,1,0:T(8,128)(2,1)S(1)}, bf16[2,19,16,320]{3,2,1,0:T(8,128)(2,1)S(1)}, u32[]{:S(2)}, u32[]{:S(2)}) collective-permute-start(bf16[2,19,16,320]{3,2,1,0:T(8,128)(2,1)S(1)} %get-tuple-element.24.mine), channel_id=1, source_target_pairs={{0,1},{1,0},{2,3},{3,2},{4,5},{5,4},{6,7},{7,6},{8,9},{9,8},{10,11... | collective-permute-start | bytes 1167368 | tf_op jit(solution)/shard_map/ppermute | solution.py:516
  36.3 0.0 copy-done.2
  36.4 1.0 %shard_map.151.bias = f32[8,320]{1,0:T(8,128)S(1)} custom-call(s32[1]{0:T(128)S(6)} %copy.17.step, f32[320,320]{1,0:T(8,128)S(1)} %copy-done.2), custom_call_target="tpu_custom_call" | custom-call | flops 10000000000 | bytes 1000000 | tf_op jit(solution)/shard_map/pallas_call | solution.py:32
  37.3 0.8 collective-permute-done.3.theirs
  38.1 0.0 copy-done
  38.1 0.0 copy-done.1
  38.1 0.0 copy-done.5
  38.2 0.0 copy-done.6
  38.2 0.0 copy-done.7
  38.2 0.0 copy-done.8
  38.2 6.5 %shard_map.152 = (bf16[512,2880]{1,0:T(8,128)(2,1)S(1)}, bf16[512,320]{1,0:T(8,128)(2,1)S(1)}, f32[8,640]{1,0:T(8,128)S(1)}) custom-call(f32[8,128]{1,0:T(8,128)S(1)} %get-tuple-element.23.totals, f32[8,320]{1,0:T(8,128)S(1)} %shard_map.151.bias, bf16[2,19,16,320]{3,2,1,0:T(8,128)(2,1)S(1)} %get-tuple-element.24.mine, ...), custom_call_target="tpu_custom_call" | custom-call | flops 2000000000 | bytes 10000000 | tf_op jit(solution)/shard_map/pallas_call | solution.py:32
  44.7 2.0 %collective-permute-start.4 = (f32[8,640]{1,0:T(8,128)S(1)}, f32[8,640]{1,0:T(8,128)S(1)}, u32[]{:S(2)}, u32[]{:S(2)}) collective-permute-start(f32[8,640]{1,0:T(8,128)S(1)} %get-tuple-element.27.small), channel_id=1, source_target_pairs={{0,1},{1,0},{2,3},{3,2},{4,5},{5,4},{6,7},{7,6},{8,9},{9,8},{10,11... | collective-permute-start | bytes 61448 | tf_op jit(solution)/shard_map/ppermute | solution.py:539
  46.8 1.9 %shard_map.153.blocks = f32[32,48,320]{2,1,0:T(8,128)S(1)} custom-call(bf16[512,2880]{1,0:T(8,128)(2,1)S(1)} %get-tuple-element.25.cols, bf16[512,320]{1,0:T(8,128)(2,1)S(1)} %get-tuple-element.26.cot), custom_call_target="tpu_custom_call" | custom-call | flops 1000000000 | bytes 10000000 | tf_op jit(solution)/shard_map/pallas_call | solution.py:32
  48.7 0.0 collective-permute-done.4.other
  48.7 1.2 %shard_map.154 = s16[8,10,48,128]{3,2,1,0:T(8,128)(2,1)S(1)} custom-call(f32[32,48,320]{2,1,0:T(8,128)S(1)} %shard_map.153.blocks, f32[8,640]{1,0:T(8,128)S(1)} %get-tuple-element.27.small, f32[8,640]{1,0:T(8,128)S(1)} %collective-permute-done.4.other), custom_call_target="tpu_custom_call" | custom-call | tf_op jit(solution)/shard_map/pallas_call | solution.py:32
  49.9 19.7 %all_to_all.21.blocks = s16[8,10,48,128]{3,2,1,0:T(8,128)(2,1)S(1)} all-to-all(s16[8,10,48,128]{3,2,1,0:T(8,128)(2,1)S(1)} %shard_map.154), channel_id=1, replica_groups=mesh['y'=8,'x'=4,'zl'=2,'zh'=4,'core'=2] {'x','zl'}, dimensions={0} | all-to-all | bytes 1966080 | tf_op jit(solution)/shard_map/all_to_all | solution.py:551
  69.5 1.5 %shard_map.155 = s16[8,4,24,128]{3,2,1,0:T(8,128)(2,1)S(1)} custom-call(s16[8,10,48,128]{3,2,1,0:T(8,128)(2,1)S(1)} %all_to_all.21.blocks), custom_call_target="tpu_custom_call" | custom-call | tf_op jit(solution)/shard_map/pallas_call | solution.py:32
  71.0 23.7 %all_to_all.22 = s16[32,24,128]{2,1,0:T(8,128)(2,1)S(1)} all-to-all(s16[32,24,128]{2,1,0:T(8,128)(2,1)S(1)} %bitcast.11), channel_id=1, replica_groups=mesh['y'=8,'x'=4,'zl'=2,'zh'=4,'core'=2] {'y','zh'}, dimensions={0} | all-to-all | bytes 393216 | tf_op jit(solution)/shard_map/all_to_all | solution.py:553
  94.7 1.1 %shard_map.156 = (f32[1,1]{1,0:T(1,128)}, f32[40,45]{1,0:T(8,128)}, f32[320]{0:T(512)}, f32[320]{0:T(512)}) custom-call(s16[8,4,24,128]{3,2,1,0:T(8,128)(2,1)S(1)} %bitcast.12), custom_call_target="tpu_custom_call" | custom-call | tf_op jit(solution)/shard_map/pallas_call | solution.py:32
  (2 shorter events, 0.1 us)
Async XLA Ops:
  2.0 22.3 %collective-permute-start = (bf16[2,16,320]{2,1,0:T(8,128)(2,1)}, bf16[2,16,320]{2,1,0:T(8,128)(2,1)S(1)}, u32[]{:S(2)}, u32[]{:S(2)}) collective-permute-start(bf16[2,16,320]{2,1,0:T(8,128)(2,1)} %get-tuple-element.19), channel_id=1, source_target_pairs={{0,8},{8,16},{16,24},{24,32},{32,40},{40,48},{48,56},{56,0},{1,9},... | collective-permute-start | bytes 61448 | tf_op jit(solution)/shard_map/ppermute | solution.py:486
  6.3 18.0 %collective-permute-start.1 = (bf16[2,16,320]{2,1,0:T(8,128)(2,1)}, bf16[2,16,320]{2,1,0:T(8,128)(2,1)S(1)}, u32[]{:S(2)}, u32[]{:S(2)}) collective-permute-start(bf16[2,16,320]{2,1,0:T(8,128)(2,1)} %get-tuple-element.20), channel_id=1, source_target_pairs={{8,0},{16,8},{24,16},{32,24},{40,32},{48,40},{56,48},{0,56},{9,1},... | collective-permute-start | bytes 61448 | tf_op jit(solution)/shard_map/ppermute | solution.py:487
  12.8 21.2 %all-to-all-start = ((f32[32,1,128]{2,1,0:T(1,128)}), f32[32,1,128]{2,1,0:T(1,128)S(1)}, u32[]{:S(2)}, u32[]{:S(2)}) async-start(f32[32,1,128]{2,1,0:T(1,128)} %bitcast.20), calls=%async_computation | async-start | bytes 32768 | tf_op jit(solution)/shard_map/all_to_all | solution.py:497
  24.4 0.7 copy-start.4
  25.1 8.9 %copy-start.3 = (bf16[2,16,16,320]{3,2,1,0:T(8,128)(2,1)S(1)}, bf16[2,16,16,320]{3,2,1,0:T(8,128)(2,1)}, u32[]{:S(2)}) copy-start(bf16[2,16,16,320]{3,2,1,0:T(8,128)(2,1)} %get-tuple-element.22.here) | copy-start | bytes 983044
  25.1 8.9 %collective-permute-start.2 = (bf16[2,16,320]{2,1,0:T(8,128)(2,1)S(1)}, bf16[2,16,320]{2,1,0:T(8,128)(2,1)S(1)}, u32[]{:S(2)}, u32[]{:S(2)}) collective-permute-start(bf16[2,16,320]{2,1,0:T(8,128)(2,1)S(1)} %shard_map.149), channel_id=1, source_target_pairs={{0,7},{1,2},{2,1},{3,4},{4,3},{5,6},{6,5},{7,0},{8,15},{9,10},{10,... | collective-permute-start | bytes 61448 | tf_op jit(solution)/shard_map/ppermute | solution.py:509
  34.0 2.3 %copy-start.2 = (f32[320,320]{1,0:T(8,128)S(1)}, f32[320,320]{1,0:T(8,128)}, u32[]{:S(2)}) copy-start(f32[320,320]{1,0:T(8,128)} %time_weight.1) | copy-start | bytes 1228804
  34.1 4.1 %copy-start = (bf16[9,320,320]{2,1,0:T(8,128)(2,1)S(1)}, bf16[9,320,320]{2,1,0:T(8,128)(2,1)}, u32[]{:S(2)}) copy-start(bf16[9,320,320]{2,1,0:T(8,128)(2,1)} %weight_far.1) | copy-start | bytes 5529604
  34.1 4.1 %copy-start.1 = (bf16[9,320,320]{2,1,0:T(8,128)(2,1)S(1)}, bf16[9,320,320]{2,1,0:T(8,128)(2,1)}, u32[]{:S(2)}) copy-start(bf16[9,320,320]{2,1,0:T(8,128)(2,1)} %ref_far.1) | copy-start | bytes 5529604
  34.1 4.0 %copy-start.5 = (f32[320]{0:T(512)S(1)}, f32[320]{0:T(512)}, u32[]{:S(2)}) copy-start(f32[320]{0:T(512)} %gain_far.1) | copy-start | bytes 3844
  34.1 4.0 %copy-start.6 = (f32[320]{0:T(512)S(1)}, f32[320]{0:T(512)}, u32[]{:S(2)}) copy-start(f32[320]{0:T(512)} %shift_far.1) | copy-start | bytes 3844
  34.1 4.0 %copy-start.7 = (f32[320]{0:T(512)S(1)}, f32[320]{0:T(512)}, u32[]{:S(2)}) copy-start(f32[320]{0:T(512)} %ref_gain_far.1) | copy-start | bytes 3844
  34.1 4.0 %copy-start.8 = (f32[320]{0:T(512)S(1)}, f32[320]{0:T(512)}, u32[]{:S(2)}) copy-start(f32[320]{0:T(512)} %ref_shift_far.1) | copy-start | bytes 3844
  34.2 4.0 %collective-permute-start.3 = (bf16[2,19,16,320]{3,2,1,0:T(8,128)(2,1)S(1)}, bf16[2,19,16,320]{3,2,1,0:T(8,128)(2,1)S(1)}, u32[]{:S(2)}, u32[]{:S(2)}) collective-permute-start(bf16[2,19,16,320]{3,2,1,0:T(8,128)(2,1)S(1)} %get-tuple-element.24.mine), channel_id=1, source_target_pairs={{0,1},{1,0},{2,3},{3,2},{4,5},{5,4},{6,7},{7,6},{8,9},{9,8},{10,11... | collective-permute-start | bytes 1167368 | tf_op jit(solution)/shard_map/ppermute | solution.py:516
  44.7 3.9 %collective-permute-start.4 = (f32[8,640]{1,0:T(8,128)S(1)}, f32[8,640]{1,0:T(8,128)S(1)}, u32[]{:S(2)}, u32[]{:S(2)}) collective-permute-start(f32[8,640]{1,0:T(8,128)S(1)} %get-tuple-element.27.small), channel_id=1, source_target_pairs={{0,1},{1,0},{2,3},{3,2},{4,5},{5,4},{6,7},{7,6},{8,9},{9,8},{10,11... | collective-permute-start | bytes 61448 | tf_op jit(solution)/shard_map/ppermute | solution.py:539

commit v10 on v9

--- a/solution.py
+++ b/solution.py
@@ -333,14 +333,19 @@
 
     cot = cot_out[0 : 2 * PIX]
     back[...] = jnp.zeros_like(back)
+    terms = lax.dot_general(
+        cot, weight[...].reshape(TAPS * C, C), (((1,), (1,)), ((), ())), preferred_element_type=F32
+    )
     for c in range(3):
-        shifted[...] = jnp.zeros_like(shifted)
         for a in range(3):
-            term = lax.dot_general(
-                cot, weight[3 * a + c], (((1,), (1,)), ((), ())), preferred_element_type=F32
-            )
+            term = terms[:, C * (3 * a + c) : C * (3 * a + c + 1)]
             for s in range(2):
-                shifted[s, a : a + TH] += term[s * PIX : (s + 1) * PIX].reshape(TH, TW, C)
+                part = term[s * PIX : (s + 1) * PIX].reshape(TH, TW, C)
+                if a == 0:
+                    shifted[s, 0:TH] = part
+                    shifted[s, TH:] = jnp.zeros((2, TW, C), F32)
+                else:
+                    shifted[s, a : a + TH] += part
         back[:, :, c : c + TW, :] += shifted[...]
     gains = jnp.zeros((24, C), F32)
     shifts = jnp.zeros((24, C), F32)
@@ -407,7 +412,7 @@
     for k, part in enumerate((high, low, exps)):
         tail = jnp.where(lane == 2 + k, part[1:2], tail)
 
-    def body(pair, carry):
+    for pair in range(2):
         both = jnp.zeros((48, WIDE), F32)
         for source in range(8):
             both = both + unpacked_pair(pair_of(source, pair, slice(0, 48)))
@@ -424,9 +429,6 @@
                 ey = jnp.concatenate([ey, ey, ey, jnp.zeros((1, 8), F32)], axis=1)
                 full = jnp.concatenate([tile] + vectors + [ey, tail], axis=0)
                 out[y, 2 * pair + k] = full.astype(jnp.int32).astype(I16)
-        return carry
-
-    lax.fori_loop(0, 2, body, 0)
 
 
 def final_sum(blocks, loss, grad, gain, shift):

time: 96.4 us -> 95.8 us (level)
  transfers between devices with their start and end apart: 6 -> 6, of which waited for: 2 -> 2; matrix products, arithmetic and copies ran while one was open for 0% -> 0% of each run, Pallas kernels for 5% -> 6%
where the time goes in v10:
time: 95.8 us; the launch traced here: 95.3 us
  blocking collectives  43.4 us (45%)
  starting transfers between devices  28.4 us (30%)
  Pallas kernels  16.5 us (17%)
  waiting for transfers between devices  4.78 us (5%)
  between operations  1.51 us (2%)
    all_to_all x1, blocking collectives, local(): lax.all_to_all(sums.reshape(32, 24, 128), ('y', 'zh'), 0, 0, tiled=True)  23.7 us
    all_to_all x1, blocking collectives, local(): blocks = lax.all_to_all(blocks, ('x', 'zl'), 0, 0, tiled=True)  19.7 us
    pallas_call x10, Pallas kernels, run(): pl.pallas_call(kernel, out_shape=[jax.ShapeDtypeStruct(s, d) for s, d in...  16.5 us
    all_to_all x1, starting transfers between devices, local(): stats = lax.all_to_all(stats, ('x', 'zl', 'zh'), 0, 0, tiled=True)  11.5 us
    ppermute x1, starting transfers between devices, local(): top = lax.ppermute(last, rows, down)  4.28 us
    ppermute x1, starting transfers between devices, local(): side = lax.ppermute(side, columns, outward)  4.26 us
    ppermute x1, starting transfers between devices, local(): bottom = lax.ppermute(first, rows, up)  4.11 us
    all_to_all x1, waiting for transfers between devices, local(): stats = lax.all_to_all(stats, ('x', 'zl', 'zh'), 0, 0, tiled=True)  3.97 us
  transfers between devices with their start and end apart: 6, of which 2 were waited for; matrix products, arithmetic and copies ran while one was open for 0% of the time, Pallas kernels for 6%

profile of v10, /device:TPU:8, one launch (start us, length us, event | category | flops | bytes accessed | tf_op | source)
XLA Modules:
  0.0 95.3 jit_solution(6402050460401594550)
XLA Ops:
  0.6 1.4 %shard_map.148 = (bf16[2,16,320]{2,1,0:T(8,128)(2,1)}, bf16[2,16,320]{2,1,0:T(8,128)(2,1)}) custom-call(bf16[8,16,320]{2,1,0:T(8,128)(2,1)} %bitcast.14, bf16[8,16,320]{2,1,0:T(8,128)(2,1)} %bitcast.16), custom_call_target="tpu_custom_call" | custom-call | tf_op jit(solution)/shard_map/pallas_call | solution.py:32
  2.0 4.3 %collective-permute-start = (bf16[2,16,320]{2,1,0:T(8,128)(2,1)}, bf16[2,16,320]{2,1,0:T(8,128)(2,1)S(1)}, u32[]{:S(2)}, u32[]{:S(2)}) collective-permute-start(bf16[2,16,320]{2,1,0:T(8,128)(2,1)} %get-tuple-element.19), channel_id=1, source_target_pairs={{0,8},{8,16},{16,24},{24,32},{32,40},{40,48},{48,56},{56,0},{1,9},... | collective-permute-start | bytes 61448 | tf_op jit(solution)/shard_map/ppermute | solution.py:488
  6.3 4.1 %collective-permute-start.1 = (bf16[2,16,320]{2,1,0:T(8,128)(2,1)}, bf16[2,16,320]{2,1,0:T(8,128)(2,1)S(1)}, u32[]{:S(2)}, u32[]{:S(2)}) collective-permute-start(bf16[2,16,320]{2,1,0:T(8,128)(2,1)} %get-tuple-element.20), channel_id=1, source_target_pairs={{8,0},{16,8},{24,16},{32,24},{40,32},{48,40},{56,48},{0,56},{9,1},... | collective-permute-start | bytes 61448 | tf_op jit(solution)/shard_map/ppermute | solution.py:489
  10.5 2.4 %shard_map.147 = (f32[32,128]{1,0:T(8,128)}, bf16[2,16,320]{2,1,0:T(8,128)(2,1)}, bf16[2,16,16,320]{3,2,1,0:T(8,128)(2,1)}) custom-call(bf16[8,16,320]{2,1,0:T(8,128)(2,1)} %bitcast.15, bf16[8,16,320]{2,1,0:T(8,128)(2,1)} %bitcast.17, bf16[8,16,320]{2,1,0:T(8,128)(2,1)} %bitcast.18, bf16[8,16,320]{2,1,0:T(8,128)(2,1)} %bitcast.19), custom_call_target="tpu_custom_call" | custom-call | flops 10000000 | bytes 1000000 | tf_op jit(solution)/shard_map/pallas_call | solution.py:32
  12.8 11.5 %all-to-all-start = ((f32[32,1,128]{2,1,0:T(1,128)}), f32[32,1,128]{2,1,0:T(1,128)S(1)}, u32[]{:S(2)}, u32[]{:S(2)}) async-start(f32[32,1,128]{2,1,0:T(1,128)} %bitcast.20), calls=%async_computation | async-start | bytes 32768 | tf_op jit(solution)/shard_map/all_to_all | solution.py:499
  24.4 0.0 collective-permute-done.top
  24.4 0.0 collective-permute-done.1.bottom
  24.4 0.0 copy-start.4
  24.4 0.7 copy-done.4
  25.1 0.0 copy-start.3
  25.1 4.3 %collective-permute-start.2 = (bf16[2,16,320]{2,1,0:T(8,128)(2,1)S(1)}, bf16[2,16,320]{2,1,0:T(8,128)(2,1)S(1)}, u32[]{:S(2)}, u32[]{:S(2)}) collective-permute-start(bf16[2,16,320]{2,1,0:T(8,128)(2,1)S(1)} %shard_map.149), channel_id=1, source_target_pairs={{0,7},{1,2},{2,1},{3,4},{4,3},{5,6},{6,5},{7,0},{8,15},{9,10},{10,... | collective-permute-start | bytes 61448 | tf_op jit(solution)/shard_map/ppermute | solution.py:511
  30.1 4.0 %all-to-all-done = f32[32,1,128]{2,1,0:T(1,128)S(1)} async-done(((f32[32,1,128]{2,1,0:T(1,128)}), f32[32,1,128]{2,1,0:T(1,128)S(1)}, u32[]{:S(2)}, u32[]{:S(2)}) %all-to-all-start) | async-done | bytes 16416 | tf_op jit(solution)/shard_map/all_to_all | solution.py:499
  34.0 0.0 collective-permute-done.2.side
  34.0 0.0 copy-done.3
  34.0 0.0 copy-start.2
  34.1 0.0 copy-start
  34.1 0.0 copy-start.1
  34.1 0.0 copy-start.5
  34.1 0.0 copy-start.6
  34.1 0.0 copy-start.7
  34.1 0.0 copy-start.8
  34.2 2.2 %collective-permute-start.3 = (bf16[2,19,16,320]{3,2,1,0:T(8,128)(2,1)S(1)}, bf16[2,19,16,320]{3,2,1,0:T(8,128)(2,1)S(1)}, u32[]{:S(2)}, u32[]{:S(2)}) collective-permute-start(bf16[2,19,16,320]{3,2,1,0:T(8,128)(2,1)S(1)} %get-tuple-element.24.mine), channel_id=1, source_target_pairs={{0,1},{1,0},{2,3},{3,2},{4,5},{5,4},{6,7},{7,6},{8,9},{9,8},{10,11... | collective-permute-start | bytes 1167368 | tf_op jit(solution)/shard_map/ppermute | solution.py:518
  36.3 0.0 copy-done.2
  36.4 1.0 %shard_map.151.bias = f32[8,320]{1,0:T(8,128)S(1)} custom-call(s32[1]{0:T(128)S(6)} %copy.17.step, f32[320,320]{1,0:T(8,128)S(1)} %copy-done.2), custom_call_target="tpu_custom_call" | custom-call | flops 10000000000 | bytes 1000000 | tf_op jit(solution)/shard_map/pallas_call | solution.py:32
  37.3 0.8 collective-permute-done.3.theirs
  38.1 0.0 copy-done
  38.1 0.0 copy-done.1
  38.1 0.0 copy-done.5
  38.2 0.0 copy-done.6
  38.2 0.0 copy-done.7
  38.2 0.0 copy-done.8
  38.2 6.2 %shard_map.152 = (bf16[512,2880]{1,0:T(8,128)(2,1)S(1)}, bf16[512,320]{1,0:T(8,128)(2,1)S(1)}, f32[8,640]{1,0:T(8,128)S(1)}) custom-call(f32[8,128]{1,0:T(8,128)S(1)} %get-tuple-element.23.totals, f32[8,320]{1,0:T(8,128)S(1)} %shard_map.151.bias, bf16[2,19,16,320]{3,2,1,0:T(8,128)(2,1)S(1)} %get-tuple-element.24.mine, ...), custom_call_target="tpu_custom_call" | custom-call | flops 2000000000 | bytes 10000000 | tf_op jit(solution)/shard_map/pallas_call | solution.py:32
  44.4 2.0 %collective-permute-start.4 = (f32[8,640]{1,0:T(8,128)S(1)}, f32[8,640]{1,0:T(8,128)S(1)}, u32[]{:S(2)}, u32[]{:S(2)}) collective-permute-start(f32[8,640]{1,0:T(8,128)S(1)} %get-tuple-element.27.small), channel_id=1, source_target_pairs={{0,1},{1,0},{2,3},{3,2},{4,5},{5,4},{6,7},{7,6},{8,9},{9,8},{10,11... | collective-permute-start | bytes 61448 | tf_op jit(solution)/shard_map/ppermute | solution.py:541
  46.5 1.9 %shard_map.153.blocks = f32[32,48,320]{2,1,0:T(8,128)S(1)} custom-call(bf16[512,2880]{1,0:T(8,128)(2,1)S(1)} %get-tuple-element.25.cols, bf16[512,320]{1,0:T(8,128)(2,1)S(1)} %get-tuple-element.26.cot), custom_call_target="tpu_custom_call" | custom-call | flops 1000000000 | bytes 10000000 | tf_op jit(solution)/shard_map/pallas_call | solution.py:32
  48.4 0.0 collective-permute-done.4.other
  48.4 1.2 %shard_map.154 = s16[8,10,48,128]{3,2,1,0:T(8,128)(2,1)S(1)} custom-call(f32[32,48,320]{2,1,0:T(8,128)S(1)} %shard_map.153.blocks, f32[8,640]{1,0:T(8,128)S(1)} %get-tuple-element.27.small, f32[8,640]{1,0:T(8,128)S(1)} %collective-permute-done.4.other), custom_call_target="tpu_custom_call" | custom-call | tf_op jit(solution)/shard_map/pallas_call | solution.py:32
  49.6 19.7 %all_to_all.21.blocks = s16[8,10,48,128]{3,2,1,0:T(8,128)(2,1)S(1)} all-to-all(s16[8,10,48,128]{3,2,1,0:T(8,128)(2,1)S(1)} %shard_map.154), channel_id=1, replica_groups=mesh['y'=8,'x'=4,'zl'=2,'zh'=4,'core'=2] {'x','zl'}, dimensions={0} | all-to-all | bytes 1966080 | tf_op jit(solution)/shard_map/all_to_all | solution.py:553
  69.2 1.3 %shard_map.155 = s16[8,4,24,128]{3,2,1,0:T(8,128)(2,1)S(1)} custom-call(s16[8,10,48,128]{3,2,1,0:T(8,128)(2,1)S(1)} %all_to_all.21.blocks), custom_call_target="tpu_custom_call" | custom-call | tf_op jit(solution)/shard_map/pallas_call | solution.py:32
  70.5 23.7 %all_to_all.22 = s16[32,24,128]{2,1,0:T(8,128)(2,1)S(1)} all-to-all(s16[32,24,128]{2,1,0:T(8,128)(2,1)S(1)} %bitcast.11), channel_id=1, replica_groups=mesh['y'=8,'x'=4,'zl'=2,'zh'=4,'core'=2] {'y','zh'}, dimensions={0} | all-to-all | bytes 393216 | tf_op jit(solution)/shard_map/all_to_all | solution.py:555
  94.2 1.1 %shard_map.156 = (f32[1,1]{1,0:T(1,128)}, f32[40,45]{1,0:T(8,128)}, f32[320]{0:T(512)}, f32[320]{0:T(512)}) custom-call(s16[8,4,24,128]{3,2,1,0:T(8,128)(2,1)S(1)} %bitcast.12), custom_call_target="tpu_custom_call" | custom-call | tf_op jit(solution)/shard_map/pallas_call | solution.py:32
  (2 shorter events, 0.1 us)
Async XLA Ops:
  2.0 22.3 %collective-permute-start = (bf16[2,16,320]{2,1,0:T(8,128)(2,1)}, bf16[2,16,320]{2,1,0:T(8,128)(2,1)S(1)}, u32[]{:S(2)}, u32[]{:S(2)}) collective-permute-start(bf16[2,16,320]{2,1,0:T(8,128)(2,1)} %get-tuple-element.19), channel_id=1, source_target_pairs={{0,8},{8,16},{16,24},{24,32},{32,40},{40,48},{48,56},{56,0},{1,9},... | collective-permute-start | bytes 61448 | tf_op jit(solution)/shard_map/ppermute | solution.py:488
  6.3 18.0 %collective-permute-start.1 = (bf16[2,16,320]{2,1,0:T(8,128)(2,1)}, bf16[2,16,320]{2,1,0:T(8,128)(2,1)S(1)}, u32[]{:S(2)}, u32[]{:S(2)}) collective-permute-start(bf16[2,16,320]{2,1,0:T(8,128)(2,1)} %get-tuple-element.20), channel_id=1, source_target_pairs={{8,0},{16,8},{24,16},{32,24},{40,32},{48,40},{56,48},{0,56},{9,1},... | collective-permute-start | bytes 61448 | tf_op jit(solution)/shard_map/ppermute | solution.py:489
  12.8 21.2 %all-to-all-start = ((f32[32,1,128]{2,1,0:T(1,128)}), f32[32,1,128]{2,1,0:T(1,128)S(1)}, u32[]{:S(2)}, u32[]{:S(2)}) async-start(f32[32,1,128]{2,1,0:T(1,128)} %bitcast.20), calls=%async_computation | async-start | bytes 32768 | tf_op jit(solution)/shard_map/all_to_all | solution.py:499
  24.4 0.7 copy-start.4
  25.1 8.9 %copy-start.3 = (bf16[2,16,16,320]{3,2,1,0:T(8,128)(2,1)S(1)}, bf16[2,16,16,320]{3,2,1,0:T(8,128)(2,1)}, u32[]{:S(2)}) copy-start(bf16[2,16,16,320]{3,2,1,0:T(8,128)(2,1)} %get-tuple-element.22.here) | copy-start | bytes 983044
  25.1 8.9 %collective-permute-start.2 = (bf16[2,16,320]{2,1,0:T(8,128)(2,1)S(1)}, bf16[2,16,320]{2,1,0:T(8,128)(2,1)S(1)}, u32[]{:S(2)}, u32[]{:S(2)}) collective-permute-start(bf16[2,16,320]{2,1,0:T(8,128)(2,1)S(1)} %shard_map.149), channel_id=1, source_target_pairs={{0,7},{1,2},{2,1},{3,4},{4,3},{5,6},{6,5},{7,0},{8,15},{9,10},{10,... | collective-permute-start | bytes 61448 | tf_op jit(solution)/shard_map/ppermute | solution.py:511
  34.0 2.3 %copy-start.2 = (f32[320,320]{1,0:T(8,128)S(1)}, f32[320,320]{1,0:T(8,128)}, u32[]{:S(2)}) copy-start(f32[320,320]{1,0:T(8,128)} %time_weight.1) | copy-start | bytes 1228804
  34.1 4.1 %copy-start = (bf16[9,320,320]{2,1,0:T(8,128)(2,1)S(1)}, bf16[9,320,320]{2,1,0:T(8,128)(2,1)}, u32[]{:S(2)}) copy-start(bf16[9,320,320]{2,1,0:T(8,128)(2,1)} %weight_far.1) | copy-start | bytes 5529604
  34.1 4.1 %copy-start.1 = (bf16[9,320,320]{2,1,0:T(8,128)(2,1)S(1)}, bf16[9,320,320]{2,1,0:T(8,128)(2,1)}, u32[]{:S(2)}) copy-start(bf16[9,320,320]{2,1,0:T(8,128)(2,1)} %ref_far.1) | copy-start | bytes 5529604
  34.1 4.0 %copy-start.5 = (f32[320]{0:T(512)S(1)}, f32[320]{0:T(512)}, u32[]{:S(2)}) copy-start(f32[320]{0:T(512)} %gain_far.1) | copy-start | bytes 3844
  34.1 4.0 %copy-start.6 = (f32[320]{0:T(512)S(1)}, f32[320]{0:T(512)}, u32[]{:S(2)}) copy-start(f32[320]{0:T(512)} %shift_far.1) | copy-start | bytes 3844
  34.1 4.0 %copy-start.7 = (f32[320]{0:T(512)S(1)}, f32[320]{0:T(512)}, u32[]{:S(2)}) copy-start(f32[320]{0:T(512)} %ref_gain_far.1) | copy-start | bytes 3844
  34.1 4.0 %copy-start.8 = (f32[320]{0:T(512)S(1)}, f32[320]{0:T(512)}, u32[]{:S(2)}) copy-start(f32[320]{0:T(512)} %ref_shift_far.1) | copy-start | bytes 3844
  34.2 4.0 %collective-permute-start.3 = (bf16[2,19,16,320]{3,2,1,0:T(8,128)(2,1)S(1)}, bf16[2,19,16,320]{3,2,1,0:T(8,128)(2,1)S(1)}, u32[]{:S(2)}, u32[]{:S(2)}) collective-permute-start(bf16[2,19,16,320]{3,2,1,0:T(8,128)(2,1)S(1)} %get-tuple-element.24.mine), channel_id=1, source_target_pairs={{0,1},{1,0},{2,3},{3,2},{4,5},{5,4},{6,7},{7,6},{8,9},{9,8},{10,11... | collective-permute-start | bytes 1167368 | tf_op jit(solution)/shard_map/ppermute | solution.py:518
  44.4 3.9 %collective-permute-start.4 = (f32[8,640]{1,0:T(8,128)S(1)}, f32[8,640]{1,0:T(8,128)S(1)}, u32[]{:S(2)}, u32[]{:S(2)}) collective-permute-start(f32[8,640]{1,0:T(8,128)S(1)} %get-tuple-element.27.small), channel_id=1, source_target_pairs={{0,1},{1,0},{2,3},{3,2},{4,5},{5,4},{6,7},{7,6},{8,9},{9,8},{10,11... | collective-permute-start | bytes 61448 | tf_op jit(solution)/shard_map/ppermute | solution.py:541

commit v11 on v10

--- a/solution.py
+++ b/solution.py
@@ -379,15 +379,12 @@
 def pack_blocks(blocks, small, other, out, extra):
     write_extras(extra, small[...] + other[...])
 
-    def body(dest, carry):
+    for dest in range(8):
         for pair in range(2):
             q = 4 * dest + 2 * pair
             packed = packed_pair(side_by_side(blocks[q], blocks[q + 1]), extra[pair])
             for k, tile in enumerate(tiles_of(pair)):
                 out[dest, tile] = packed[:, 128 * k : 128 * k + 128]
-        return carry
-
-    lax.fori_loop(0, 8, body, 0)
 
 
 def chip_sum(blocks, out):

time: 95.8 us -> 95.6 us (level)
  no operation moved by 1% of the time
where the time goes in v11:
time: 95.6 us; the launch traced here: 95.1 us
  blocking collectives  43.4 us (45%)
  starting transfers between devices  28.4 us (30%)
  Pallas kernels  16.3 us (17%)
  waiting for transfers between devices  4.78 us (5%)
  between operations  1.51 us (2%)
    all_to_all x1, blocking collectives, local(): lax.all_to_all(sums.reshape(32, 24, 128), ('y', 'zh'), 0, 0, tiled=True)  23.7 us
    all_to_all x1, blocking collectives, local(): blocks = lax.all_to_all(blocks, ('x', 'zl'), 0, 0, tiled=True)  19.7 us
    pallas_call x10, Pallas kernels, run(): pl.pallas_call(kernel, out_shape=[jax.ShapeDtypeStruct(s, d) for s, d in...  16.3 us
    all_to_all x1, starting transfers between devices, local(): stats = lax.all_to_all(stats, ('x', 'zl', 'zh'), 0, 0, tiled=True)  11.5 us
    ppermute x1, starting transfers between devices, local(): top = lax.ppermute(last, rows, down)  4.28 us
    ppermute x1, starting transfers between devices, local(): side = lax.ppermute(side, columns, outward)  4.26 us
    ppermute x1, starting transfers between devices, local(): bottom = lax.ppermute(first, rows, up)  4.11 us
    all_to_all x1, waiting for transfers between devices, local(): stats = lax.all_to_all(stats, ('x', 'zl', 'zh'), 0, 0, tiled=True)  3.97 us
  transfers between devices with their start and end apart: 6, of which 2 were waited for; matrix products, arithmetic and copies ran while one was open for 0% of the time, Pallas kernels for 6%

profile of v11, /device:TPU:8, one launch (start us, length us, event | category | flops | bytes accessed | tf_op | source)
XLA Modules:
  0.0 95.1 jit_solution(11814559628082941969)
XLA Ops:
  0.6 1.4 %shard_map.148 = (bf16[2,16,320]{2,1,0:T(8,128)(2,1)}, bf16[2,16,320]{2,1,0:T(8,128)(2,1)}) custom-call(bf16[8,16,320]{2,1,0:T(8,128)(2,1)} %bitcast.14, bf16[8,16,320]{2,1,0:T(8,128)(2,1)} %bitcast.16), custom_call_target="tpu_custom_call" | custom-call | tf_op jit(solution)/shard_map/pallas_call | solution.py:32
  2.0 4.3 %collective-permute-start = (bf16[2,16,320]{2,1,0:T(8,128)(2,1)}, bf16[2,16,320]{2,1,0:T(8,128)(2,1)S(1)}, u32[]{:S(2)}, u32[]{:S(2)}) collective-permute-start(bf16[2,16,320]{2,1,0:T(8,128)(2,1)} %get-tuple-element.19), channel_id=1, source_target_pairs={{0,8},{8,16},{16,24},{24,32},{32,40},{40,48},{48,56},{56,0},{1,9},... | collective-permute-start | bytes 61448 | tf_op jit(solution)/shard_map/ppermute | solution.py:485
  6.3 4.1 %collective-permute-start.1 = (bf16[2,16,320]{2,1,0:T(8,128)(2,1)}, bf16[2,16,320]{2,1,0:T(8,128)(2,1)S(1)}, u32[]{:S(2)}, u32[]{:S(2)}) collective-permute-start(bf16[2,16,320]{2,1,0:T(8,128)(2,1)} %get-tuple-element.20), channel_id=1, source_target_pairs={{8,0},{16,8},{24,16},{32,24},{40,32},{48,40},{56,48},{0,56},{9,1},... | collective-permute-start | bytes 61448 | tf_op jit(solution)/shard_map/ppermute | solution.py:486
  10.5 2.4 %shard_map.147 = (f32[32,128]{1,0:T(8,128)}, bf16[2,16,320]{2,1,0:T(8,128)(2,1)}, bf16[2,16,16,320]{3,2,1,0:T(8,128)(2,1)}) custom-call(bf16[8,16,320]{2,1,0:T(8,128)(2,1)} %bitcast.15, bf16[8,16,320]{2,1,0:T(8,128)(2,1)} %bitcast.17, bf16[8,16,320]{2,1,0:T(8,128)(2,1)} %bitcast.18, bf16[8,16,320]{2,1,0:T(8,128)(2,1)} %bitcast.19), custom_call_target="tpu_custom_call" | custom-call | flops 10000000 | bytes 1000000 | tf_op jit(solution)/shard_map/pallas_call | solution.py:32
  12.8 11.5 %all-to-all-start = ((f32[32,1,128]{2,1,0:T(1,128)}), f32[32,1,128]{2,1,0:T(1,128)S(1)}, u32[]{:S(2)}, u32[]{:S(2)}) async-start(f32[32,1,128]{2,1,0:T(1,128)} %bitcast.20), calls=%async_computation | async-start | bytes 32768 | tf_op jit(solution)/shard_map/all_to_all | solution.py:496
  24.4 0.0 collective-permute-done.top
  24.4 0.0 collective-permute-done.1.bottom
  24.4 0.0 copy-start.4
  24.4 0.7 copy-done.4
  25.1 0.0 copy-start.3
  25.1 4.3 %collective-permute-start.2 = (bf16[2,16,320]{2,1,0:T(8,128)(2,1)S(1)}, bf16[2,16,320]{2,1,0:T(8,128)(2,1)S(1)}, u32[]{:S(2)}, u32[]{:S(2)}) collective-permute-start(bf16[2,16,320]{2,1,0:T(8,128)(2,1)S(1)} %shard_map.149), channel_id=1, source_target_pairs={{0,7},{1,2},{2,1},{3,4},{4,3},{5,6},{6,5},{7,0},{8,15},{9,10},{10,... | collective-permute-start | bytes 61448 | tf_op jit(solution)/shard_map/ppermute | solution.py:508
  30.1 4.0 %all-to-all-done = f32[32,1,128]{2,1,0:T(1,128)S(1)} async-done(((f32[32,1,128]{2,1,0:T(1,128)}), f32[32,1,128]{2,1,0:T(1,128)S(1)}, u32[]{:S(2)}, u32[]{:S(2)}) %all-to-all-start) | async-done | bytes 16416 | tf_op jit(solution)/shard_map/all_to_all | solution.py:496
  34.0 0.0 collective-permute-done.2.side
  34.0 0.0 copy-done.3
  34.0 0.0 copy-start.2
  34.1 0.0 copy-start
  34.1 0.0 copy-start.1
  34.1 0.0 copy-start.5
  34.1 0.0 copy-start.6
  34.1 0.0 copy-start.7
  34.1 0.0 copy-start.8
  34.2 2.2 %collective-permute-start.3 = (bf16[2,19,16,320]{3,2,1,0:T(8,128)(2,1)S(1)}, bf16[2,19,16,320]{3,2,1,0:T(8,128)(2,1)S(1)}, u32[]{:S(2)}, u32[]{:S(2)}) collective-permute-start(bf16[2,19,16,320]{3,2,1,0:T(8,128)(2,1)S(1)} %get-tuple-element.24.mine), channel_id=1, source_target_pairs={{0,1},{1,0},{2,3},{3,2},{4,5},{5,4},{6,7},{7,6},{8,9},{9,8},{10,11... | collective-permute-start | bytes 1167368 | tf_op jit(solution)/shard_map/ppermute | solution.py:515
  36.3 0.0 copy-done.2
  36.4 1.0 %shard_map.151.bias = f32[8,320]{1,0:T(8,128)S(1)} custom-call(s32[1]{0:T(128)S(6)} %copy.17.step, f32[320,320]{1,0:T(8,128)S(1)} %copy-done.2), custom_call_target="tpu_custom_call" | custom-call | flops 10000000000 | bytes 1000000 | tf_op jit(solution)/shard_map/pallas_call | solution.py:32
  37.3 0.8 collective-permute-done.3.theirs
  38.1 0.0 copy-done
  38.1 0.0 copy-done.1
  38.1 0.0 copy-done.5
  38.2 0.0 copy-done.6
  38.2 0.0 copy-done.7
  38.2 0.0 copy-done.8
  38.2 6.2 %shard_map.152 = (bf16[512,2880]{1,0:T(8,128)(2,1)S(1)}, bf16[512,320]{1,0:T(8,128)(2,1)S(1)}, f32[8,640]{1,0:T(8,128)S(1)}) custom-call(f32[8,128]{1,0:T(8,128)S(1)} %get-tuple-element.23.totals, f32[8,320]{1,0:T(8,128)S(1)} %shard_map.151.bias, bf16[2,19,16,320]{3,2,1,0:T(8,128)(2,1)S(1)} %get-tuple-element.24.mine, ...), custom_call_target="tpu_custom_call" | custom-call | flops 2000000000 | bytes 10000000 | tf_op jit(solution)/shard_map/pallas_call | solution.py:32
  44.4 2.0 %collective-permute-start.4 = (f32[8,640]{1,0:T(8,128)S(1)}, f32[8,640]{1,0:T(8,128)S(1)}, u32[]{:S(2)}, u32[]{:S(2)}) collective-permute-start(f32[8,640]{1,0:T(8,128)S(1)} %get-tuple-element.27.small), channel_id=1, source_target_pairs={{0,1},{1,0},{2,3},{3,2},{4,5},{5,4},{6,7},{7,6},{8,9},{9,8},{10,11... | collective-permute-start | bytes 61448 | tf_op jit(solution)/shard_map/ppermute | solution.py:538
  46.5 1.9 %shard_map.153.blocks = f32[32,48,320]{2,1,0:T(8,128)S(1)} custom-call(bf16[512,2880]{1,0:T(8,128)(2,1)S(1)} %get-tuple-element.25.cols, bf16[512,320]{1,0:T(8,128)(2,1)S(1)} %get-tuple-element.26.cot), custom_call_target="tpu_custom_call" | custom-call | flops 1000000000 | bytes 10000000 | tf_op jit(solution)/shard_map/pallas_call | solution.py:32
  48.4 0.0 collective-permute-done.4.other
  48.4 1.0 %shard_map.154 = s16[8,10,48,128]{3,2,1,0:T(8,128)(2,1)S(1)} custom-call(f32[32,48,320]{2,1,0:T(8,128)S(1)} %shard_map.153.blocks, f32[8,640]{1,0:T(8,128)S(1)} %get-tuple-element.27.small, f32[8,640]{1,0:T(8,128)S(1)} %collective-permute-done.4.other), custom_call_target="tpu_custom_call" | custom-call | tf_op jit(solution)/shard_map/pallas_call | solution.py:32
  49.3 19.7 %all_to_all.21.blocks = s16[8,10,48,128]{3,2,1,0:T(8,128)(2,1)S(1)} all-to-all(s16[8,10,48,128]{3,2,1,0:T(8,128)(2,1)S(1)} %shard_map.154), channel_id=1, replica_groups=mesh['y'=8,'x'=4,'zl'=2,'zh'=4,'core'=2] {'x','zl'}, dimensions={0} | all-to-all | bytes 1966080 | tf_op jit(solution)/shard_map/all_to_all | solution.py:550
  69.0 1.3 %shard_map.155 = s16[8,4,24,128]{3,2,1,0:T(8,128)(2,1)S(1)} custom-call(s16[8,10,48,128]{3,2,1,0:T(8,128)(2,1)S(1)} %all_to_all.21.blocks), custom_call_target="tpu_custom_call" | custom-call | tf_op jit(solution)/shard_map/pallas_call | solution.py:32
  70.3 23.7 %all_to_all.22 = s16[32,24,128]{2,1,0:T(8,128)(2,1)S(1)} all-to-all(s16[32,24,128]{2,1,0:T(8,128)(2,1)S(1)} %bitcast.11), channel_id=1, replica_groups=mesh['y'=8,'x'=4,'zl'=2,'zh'=4,'core'=2] {'y','zh'}, dimensions={0} | all-to-all | bytes 393216 | tf_op jit(solution)/shard_map/all_to_all | solution.py:552
  94.0 1.1 %shard_map.156 = (f32[1,1]{1,0:T(1,128)}, f32[40,45]{1,0:T(8,128)}, f32[320]{0:T(512)}, f32[320]{0:T(512)}) custom-call(s16[8,4,24,128]{3,2,1,0:T(8,128)(2,1)S(1)} %bitcast.12), custom_call_target="tpu_custom_call" | custom-call | tf_op jit(solution)/shard_map/pallas_call | solution.py:32
  (2 shorter events, 0.1 us)
Async XLA Ops:
  2.0 22.3 %collective-permute-start = (bf16[2,16,320]{2,1,0:T(8,128)(2,1)}, bf16[2,16,320]{2,1,0:T(8,128)(2,1)S(1)}, u32[]{:S(2)}, u32[]{:S(2)}) collective-permute-start(bf16[2,16,320]{2,1,0:T(8,128)(2,1)} %get-tuple-element.19), channel_id=1, source_target_pairs={{0,8},{8,16},{16,24},{24,32},{32,40},{40,48},{48,56},{56,0},{1,9},... | collective-permute-start | bytes 61448 | tf_op jit(solution)/shard_map/ppermute | solution.py:485
  6.3 18.0 %collective-permute-start.1 = (bf16[2,16,320]{2,1,0:T(8,128)(2,1)}, bf16[2,16,320]{2,1,0:T(8,128)(2,1)S(1)}, u32[]{:S(2)}, u32[]{:S(2)}) collective-permute-start(bf16[2,16,320]{2,1,0:T(8,128)(2,1)} %get-tuple-element.20), channel_id=1, source_target_pairs={{8,0},{16,8},{24,16},{32,24},{40,32},{48,40},{56,48},{0,56},{9,1},... | collective-permute-start | bytes 61448 | tf_op jit(solution)/shard_map/ppermute | solution.py:486
  12.8 21.2 %all-to-all-start = ((f32[32,1,128]{2,1,0:T(1,128)}), f32[32,1,128]{2,1,0:T(1,128)S(1)}, u32[]{:S(2)}, u32[]{:S(2)}) async-start(f32[32,1,128]{2,1,0:T(1,128)} %bitcast.20), calls=%async_computation | async-start | bytes 32768 | tf_op jit(solution)/shard_map/all_to_all | solution.py:496
  24.4 0.7 copy-start.4
  25.1 8.9 %copy-start.3 = (bf16[2,16,16,320]{3,2,1,0:T(8,128)(2,1)S(1)}, bf16[2,16,16,320]{3,2,1,0:T(8,128)(2,1)}, u32[]{:S(2)}) copy-start(bf16[2,16,16,320]{3,2,1,0:T(8,128)(2,1)} %get-tuple-element.22.here) | copy-start | bytes 983044
  25.1 8.9 %collective-permute-start.2 = (bf16[2,16,320]{2,1,0:T(8,128)(2,1)S(1)}, bf16[2,16,320]{2,1,0:T(8,128)(2,1)S(1)}, u32[]{:S(2)}, u32[]{:S(2)}) collective-permute-start(bf16[2,16,320]{2,1,0:T(8,128)(2,1)S(1)} %shard_map.149), channel_id=1, source_target_pairs={{0,7},{1,2},{2,1},{3,4},{4,3},{5,6},{6,5},{7,0},{8,15},{9,10},{10,... | collective-permute-start | bytes 61448 | tf_op jit(solution)/shard_map/ppermute | solution.py:508
  34.0 2.3 %copy-start.2 = (f32[320,320]{1,0:T(8,128)S(1)}, f32[320,320]{1,0:T(8,128)}, u32[]{:S(2)}) copy-start(f32[320,320]{1,0:T(8,128)} %time_weight.1) | copy-start | bytes 1228804
  34.1 4.1 %copy-start = (bf16[9,320,320]{2,1,0:T(8,128)(2,1)S(1)}, bf16[9,320,320]{2,1,0:T(8,128)(2,1)}, u32[]{:S(2)}) copy-start(bf16[9,320,320]{2,1,0:T(8,128)(2,1)} %weight_far.1) | copy-start | bytes 5529604
  34.1 4.1 %copy-start.1 = (bf16[9,320,320]{2,1,0:T(8,128)(2,1)S(1)}, bf16[9,320,320]{2,1,0:T(8,128)(2,1)}, u32[]{:S(2)}) copy-start(bf16[9,320,320]{2,1,0:T(8,128)(2,1)} %ref_far.1) | copy-start | bytes 5529604
  34.1 4.0 %copy-start.5 = (f32[320]{0:T(512)S(1)}, f32[320]{0:T(512)}, u32[]{:S(2)}) copy-start(f32[320]{0:T(512)} %gain_far.1) | copy-start | bytes 3844
  34.1 4.0 %copy-start.6 = (f32[320]{0:T(512)S(1)}, f32[320]{0:T(512)}, u32[]{:S(2)}) copy-start(f32[320]{0:T(512)} %shift_far.1) | copy-start | bytes 3844
  34.1 4.0 %copy-start.7 = (f32[320]{0:T(512)S(1)}, f32[320]{0:T(512)}, u32[]{:S(2)}) copy-start(f32[320]{0:T(512)} %ref_gain_far.1) | copy-start | bytes 3844
  34.1 4.0 %copy-start.8 = (f32[320]{0:T(512)S(1)}, f32[320]{0:T(512)}, u32[]{:S(2)}) copy-start(f32[320]{0:T(512)} %ref_shift_far.1) | copy-start | bytes 3844
  34.2 4.0 %collective-permute-start.3 = (bf16[2,19,16,320]{3,2,1,0:T(8,128)(2,1)S(1)}, bf16[2,19,16,320]{3,2,1,0:T(8,128)(2,1)S(1)}, u32[]{:S(2)}, u32[]{:S(2)}) collective-permute-start(bf16[2,19,16,320]{3,2,1,0:T(8,128)(2,1)S(1)} %get-tuple-element.24.mine), channel_id=1, source_target_pairs={{0,1},{1,0},{2,3},{3,2},{4,5},{5,4},{6,7},{7,6},{8,9},{9,8},{10,11... | collective-permute-start | bytes 1167368 | tf_op jit(solution)/shard_map/ppermute | solution.py:515
  44.4 3.9 %collective-permute-start.4 = (f32[8,640]{1,0:T(8,128)S(1)}, f32[8,640]{1,0:T(8,128)S(1)}, u32[]{:S(2)}, u32[]{:S(2)}) collective-permute-start(f32[8,640]{1,0:T(8,128)S(1)} %get-tuple-element.27.small), channel_id=1, source_target_pairs={{0,1},{1,0},{2,3},{3,2},{4,5},{5,4},{6,7},{7,6},{8,9},{9,8},{10,11... | collective-permute-start | bytes 61448 | tf_op jit(solution)/shard_map/ppermute | solution.py:538
